TPU v7x, 32 devices: a whole 2x2x4 slice. The times are simulated.
32 devices in a mesh: blk: 8 (over y, x, core), uly: 4 (over z).
Axes of the slice: x: 2, y: 2, z: 4, core: 2. Of those that a mesh axis runs over, the one named last changes fastest.
Arguments:
- stored_query_rows: bfloat16 [512, 5120], P('blk', 'uly'), may hold values from -4 to 4
- key_states: bfloat16 [512, 1024], P('blk', 'uly'), may hold values from -4 to 4
- value_states: bfloat16 [512, 1024], P('blk', 'uly'), may hold values from -6 to 6
- attn_output: bfloat16 [512, 5120], P('blk', 'uly'), may hold values from -6 to 6
- output_grad: bfloat16 [512, 5120], P(('blk', 'uly')), may hold values from -48 to 48
- logsumexp: float32 [40, 512], P('uly', 'blk'), may hold values from 7 to 8.5
Outputs:
- query_gradient: bfloat16 [512, 5120], P(('blk', 'uly'))
- key_grad: bfloat16 [512, 1024], P(('blk', 'uly'))
- value_grad: bfloat16 [512, 1024], P(('blk', 'uly'))
All inputs are finite; a program needn't handle non-finite values.
Results may differ from a plain program's by a relative error of at most 0.0055.
Values may be sent and summed in bfloat16 or wider, within the bound.
No kernel may reach another device: no remote copies, remote signals or barrier semaphores. Data moves between devices by JAX's collectives and lax.ppermute only.
A program may use at most 64 MiB of HBM per device.

v0:
```python
import jax
import jax.numpy as jnp
from jax import lax
from jax.sharding import PartitionSpec as P

QHEADS = 40
KVHEADS = 8
HEAD_DIM = 128
STEPS = 3


def shifted(array, axis, by):
    size = lax.axis_size(axis)
    return lax.ppermute(array, axis, [(i, (i + by) % size) for i in range(size)])


def block_grads(
    query_heads, gradient_per_head, lse_heads, delta_per_head, key_block, value_block, score_scale
):
    scores = jnp.einsum(
        "tgrd,ugd->grtu", query_heads, key_block, preferred_element_type=jnp.float32
    )
    prob_tile = jnp.exp(scores * score_scale - lse_heads[..., None])
    grad_probs = jnp.einsum(
        "tgrd,ugd->grtu", gradient_per_head, value_block, preferred_element_type=jnp.float32
    )
    grad_scores = (prob_tile * (grad_probs - delta_per_head[..., None])).astype(jnp.bfloat16)
    prob_low = prob_tile.astype(jnp.bfloat16)
    value_part = jnp.einsum(
        "grtu,tgrd->ugd", prob_low, gradient_per_head, preferred_element_type=jnp.float32
    )
    query_part = jnp.einsum(
        "grtu,ugd->tgrd", grad_scores, key_block, preferred_element_type=jnp.float32
    )
    key_portion = jnp.einsum(
        "grtu,tgrd->ugd", grad_scores, query_heads, preferred_element_type=jnp.float32
    )
    return (query_part, key_portion, value_part)


def body(stored_query_rows, key_states, value_states, attn_output, output_grad, logsumexp):
    group_size = QHEADS // KVHEADS
    score_scale = HEAD_DIM ** (-0.5)
    block_rows = stored_query_rows.shape[0]
    kv_local = key_states.shape[1] // HEAD_DIM
    head_shape = (block_rows, kv_local, group_size, HEAD_DIM)
    key_shape = (block_rows, kv_local, HEAD_DIM)
    flattened_shape = (block_rows, kv_local * HEAD_DIM)
    grad_local = lax.all_to_all(output_grad, "uly", split_axis=1, concat_axis=0, tiled=True)
    query_heads = stored_query_rows.reshape(head_shape)
    gradient_per_head = grad_local.reshape(head_shape)
    output_per_head = attn_output.reshape(head_shape)
    delta_per_head = jnp.einsum(
        "lpnc,lpnc->pnl", gradient_per_head, output_per_head, preferred_element_type=jnp.float32
    )
    lse_heads = logsumexp.reshape(kv_local, group_size, block_rows)

    def tile_grads(key_block, value_block):
        return block_grads(
            query_heads,
            gradient_per_head,
            lse_heads,
            delta_per_head,
            key_block.reshape(key_shape),
            value_block.reshape(key_shape),
            score_scale,
        )

    query_sum, key_own, value_own = tile_grads(key_states, value_states)
    key_sum = key_own.reshape(flattened_shape)
    value_sum = value_own.reshape(flattened_shape)
    moving = (key_states, value_states)
    far_parts = []
    for offset in range(1, STEPS):
        moving = shifted((moving[0], moving[1]), "blk", 1)
        query_part, key_portion, value_part = tile_grads(moving[0], moving[1])
        query_sum = query_sum + query_part
        far_parts.append(
            (key_portion.reshape(flattened_shape), value_part.reshape(flattened_shape))
        )
    carried = None
    for offset in range(STEPS - 1, 0, -1):
        running = far_parts[offset - 1]
        if carried is not None:
            running = (running[0] + carried[0], running[1] + carried[1])
        carried = shifted(running, "blk", -1)
    key_sum = key_sum + carried[0]
    value_sum = value_sum + carried[1]
    query_low = (score_scale * query_sum).astype(jnp.bfloat16).reshape(block_rows, -1)
    key_low = (score_scale * key_sum).astype(jnp.bfloat16)
    value_low = value_sum.astype(jnp.bfloat16)
    query_gradient, key_grad, value_grad = (
        lax.all_to_all(query_low, "uly", split_axis=0, concat_axis=1, tiled=True),
        lax.all_to_all(key_low, "uly", split_axis=0, concat_axis=1, tiled=True),
        lax.all_to_all(value_low, "uly", split_axis=0, concat_axis=1, tiled=True),
    )
    return (query_gradient, key_grad, value_grad)


def solution(mesh):
    placed = (
        P("blk", "uly"),
        P("blk", "uly"),
        P("blk", "uly"),
        P("blk", "uly"),
        P(("blk", "uly"), None),
        P("uly", "blk"),
    )
    return jax.shard_map(
        body,
        mesh=mesh,
        in_specs=placed,
        out_specs=(P(("blk", "uly"), None), P(("blk", "uly"), None), P(("blk", "uly"), None)),
        check_vma=False,
    )
```

profile of v0, /device:TPU:0, one launch (start us, length us, event | category | flops | bytes accessed | tf_op | source)
XLA Modules:
  0.0 55.7 jit_solution(16710347297849953305)
XLA Ops:
  0.6 0.5 collective-permute-start
  1.1 2.6 %collective-permute-start.1 = (bf16[64,256]{1,0:T(8,128)(2,1)}, bf16[64,256]{1,0:T(8,128)(2,1)S(1)}, u32[]{:S(2)}, u32[]{:S(2)}) collective-permute-start(bf16[64,256]{1,0:T(8,128)(2,1)} %param.8), channel_id=1, source_target_pairs={{0,4},{4,8},{8,12},{12,16},{16,20},{20,24},{24,28},{28,0},{1,5},{5... | collective-permute-start | bytes 98312 | tf_op jit(solution)/shard_map/ppermute | solution.py:14
  3.7 1.6 %copy.167 = bf16[2,4,8,1280]{3,2,0,1:T(8,128)(2,1)} copy(bf16[2,4,8,1280]{3,2,1,0:T(8,128)(2,1)} %bitcast.155) | data formatting | bytes 327680 | tf_op jit(solution)/shard_map/all_to_all | solution.py:49
  5.3 5.0 %all-to-all-start = ((bf16[16,4,1280]{2,0,1:T(8,128)(2,1)}), bf16[16,4,1280]{2,0,1:T(8,128)(2,1)S(1)}, u32[]{:S(2)}, u32[]{:S(2)}) async-start(bf16[16,4,1280]{2,0,1:T(8,128)(2,1)} %bitcast.144), calls=%async_computation | async-start | bytes 327680 | tf_op jit(solution)/shard_map/all_to_all | solution.py:49
  10.4 0.7 %copy-done.4 = f32[10,64]{1,0:T(8,128)S(1)} copy-done((f32[10,64]{1,0:T(8,128)S(1)}, f32[10,64]{1,0:T(8,128)}, u32[]{:S(2)}) %copy-start.4) | copy-done | bytes 2584
  11.6 0.5 copy-done.3
  12.5 1.6 %collective-permute-start.3 = (bf16[64,256]{1,0:T(8,128)(2,1)S(1)}, bf16[64,256]{1,0:T(8,128)(2,1)S(1)}, u32[]{:S(2)}, u32[]{:S(2)}) collective-permute-start(bf16[64,256]{1,0:T(8,128)(2,1)S(1)} %collective-permute-done.1), channel_id=1, source_target_pairs={{0,4},{4,8},{8,12},{12,16},{16,20},{20,24},{24,28},{28,0},{1,5},{5... | collective-permute-start | bytes 98312 | tf_op jit(solution)/shard_map/ppermute | solution.py:14
  14.4 2.3 %collective-permute-done.2 = bf16[64,256]{1,0:T(8,128)(2,1)S(1)} collective-permute-done((bf16[64,256]{1,0:T(8,128)(2,1)S(1)}, bf16[64,256]{1,0:T(8,128)(2,1)S(1)}, u32[]{:S(2)}, u32[]{:S(2)}) %collective-permute-start.2) | collective-permute-done | bytes 32800 | tf_op jit(solution)/shard_map/ppermute | solution.py:14
  18.9 1.0 %collective-permute-start.6 = (f32[64,256]{1,0:T(8,128)S(1)}, f32[64,256]{1,0:T(8,128)S(1)}, u32[]{:S(2)}, u32[]{:S(2)}) collective-permute-start(f32[64,256]{1,0:T(8,128)S(1)} %bitcast.162), channel_id=1, source_target_pairs={{0,28},{4,0},{8,4},{12,8},{16,12},{20,16},{24,20},{28,24},{1,29},{... | collective-permute-start | bytes 196616 | tf_op jit(solution)/shard_map/ppermute | solution.py:14
  21.9 1.6 %collective-permute-start.5 = (f32[64,256]{1,0:T(8,128)S(1)}, f32[64,256]{1,0:T(8,128)S(1)}, u32[]{:S(2)}, u32[]{:S(2)}) collective-permute-start(f32[64,256]{1,0:T(8,128)S(1)} %bitcast_add_fusion.2), channel_id=1, source_target_pairs={{0,28},{4,0},{8,4},{12,8},{16,12},{20,16},{24,20},{28,24},{1,29},{... | collective-permute-start | bytes 196616 | tf_op jit(solution)/shard_map/ppermute | solution.py:14
  23.5 1.0 %collective-permute-start.7 = (f32[64,256]{1,0:T(8,128)S(1)}, f32[64,256]{1,0:T(8,128)S(1)}, u32[]{:S(2)}, u32[]{:S(2)}) collective-permute-start(f32[64,256]{1,0:T(8,128)S(1)} %bitcast_add_fusion), channel_id=1, source_target_pairs={{0,28},{4,0},{8,4},{12,8},{16,12},{20,16},{24,20},{28,24},{1,29},{... | collective-permute-start | bytes 196616 | tf_op jit(solution)/shard_map/ppermute | solution.py:14
  24.5 0.9 %collective-permute-done.5 = f32[64,256]{1,0:T(8,128)S(1)} collective-permute-done((f32[64,256]{1,0:T(8,128)S(1)}, f32[64,256]{1,0:T(8,128)S(1)}, u32[]{:S(2)}, u32[]{:S(2)}) %collective-permute-start.5) | collective-permute-done | bytes 65568 | tf_op jit(solution)/shard_map/ppermute | solution.py:14
  25.4 0.6 %fusion.27 = bf16[64,256]{1,0:T(8,128)(2,1)} fusion(f32[64,256]{1,0:T(8,128)S(1)} %collective-permute-done.5, f32[2,8,8,128]{3,2,1,0:T(8,128)S(1)} %convolution_bitcast_fusion.8), kind=kLoop, calls=%fused_computation.49 | loop fusion | flops 49152 | bytes 163840 | tf_op jit(solution)/shard_map/convert_element_type | solution.py:90
  26.0 5.1 %all-to-all-start.2 = ((bf16[4,16,256]{2,1,0:T(8,128)(2,1)}), bf16[4,16,256]{2,1,0:T(8,128)(2,1)S(1)}, u32[]{:S(2)}, u32[]{:S(2)}) async-start(bf16[4,16,256]{2,1,0:T(8,128)(2,1)} %bitcast.29), calls=%async_computation.2 | async-start | bytes 65536 | tf_op jit(solution)/shard_map/all_to_all | solution.py:94
  31.1 0.6 %fusion.25 = bf16[64,256]{1,0:T(8,128)(2,1)} fusion(f32[64,256]{1,0:T(8,128)S(1)} %collective-permute-done.7, f32[2,8,8,128]{3,2,1,0:T(8,128)S(1)} %convolution_bitcast_fusion.5), kind=kLoop, calls=%fused_computation.44 | loop fusion | flops 32768 | bytes 163840 | tf_op jit(solution)/shard_map/convert_element_type | solution.py:91
  31.8 5.0 %all-to-all-done.2 = bf16[4,16,256]{2,1,0:T(8,128)(2,1)S(1)} async-done(((bf16[4,16,256]{2,1,0:T(8,128)(2,1)}), bf16[4,16,256]{2,1,0:T(8,128)(2,1)S(1)}, u32[]{:S(2)}, u32[]{:S(2)}) %all-to-all-start.2) | async-done | bytes 32800 | tf_op jit(solution)/shard_map/all_to_all | solution.py:94
  36.8 3.3 %all-to-all-start.3 = ((bf16[4,16,256]{2,1,0:T(8,128)(2,1)}), bf16[4,16,256]{2,1,0:T(8,128)(2,1)S(1)}, u32[]{:S(2)}, u32[]{:S(2)}) async-start(bf16[4,16,256]{2,1,0:T(8,128)(2,1)} %bitcast.40), calls=%async_computation.3 | async-start | bytes 65536 | tf_op jit(solution)/shard_map/all_to_all | solution.py:95
  40.4 0.9 %all_to_all.57 = bf16[4,16,1280]{2,1,0:T(8,128)(2,1)} reshape(bf16[64,2,5,128]{3,2,1,0:T(8,128)(2,1)S(1)} %copy.72) | data formatting | bytes 327680 | tf_op jit(solution)/shard_map/all_to_all | solution.py:93
  41.3 4.4 %all-to-all-done.3 = bf16[4,16,256]{2,1,0:T(8,128)(2,1)S(1)} async-done(((bf16[4,16,256]{2,1,0:T(8,128)(2,1)}), bf16[4,16,256]{2,1,0:T(8,128)(2,1)S(1)}, u32[]{:S(2)}, u32[]{:S(2)}) %all-to-all-start.3) | async-done | bytes 32800 | tf_op jit(solution)/shard_map/all_to_all | solution.py:95
  45.7 3.3 %all-to-all-start.1 = ((bf16[4,16,1280]{2,1,0:T(8,128)(2,1)}), bf16[4,16,1280]{2,1,0:T(8,128)(2,1)S(1)}, u32[]{:S(2)}, u32[]{:S(2)}) async-start(bf16[4,16,1280]{2,1,0:T(8,128)(2,1)} %all_to_all.57), calls=%async_computation.1 | async-start | bytes 327680 | tf_op jit(solution)/shard_map/all_to_all | solution.py:93
  49.0 0.6 %copy.137 = bf16[4,2,8,256]{3,2,0,1:T(8,128)(2,1)} copy(bf16[4,2,8,256]{3,2,1,0:T(8,128)(2,1)S(1)} %bitcast.160) | data formatting | bytes 65536 | tf_op jit(solution)/shard_map/all_to_all | solution.py:94
  49.7 0.6 %copy.141 = bf16[4,2,8,256]{3,2,0,1:T(8,128)(2,1)} copy(bf16[4,2,8,256]{3,2,1,0:T(8,128)(2,1)S(1)} %bitcast.161) | data formatting | bytes 65536 | tf_op jit(solution)/shard_map/all_to_all | solution.py:95
  50.3 4.7 %all-to-all-done.1 = bf16[4,16,1280]{2,1,0:T(8,128)(2,1)S(1)} async-done(((bf16[4,16,1280]{2,1,0:T(8,128)(2,1)}), bf16[4,16,1280]{2,1,0:T(8,128)(2,1)S(1)}, u32[]{:S(2)}, u32[]{:S(2)}) %all-to-all-start.1) | async-done | bytes 163872 | tf_op jit(solution)/shard_map/all_to_all | solution.py:93
  55.0 0.7 %copy.133 = bf16[4,2,8,1280]{3,2,0,1:T(8,128)(2,1)} copy(bf16[4,2,8,1280]{3,2,1,0:T(8,128)(2,1)S(1)} %bitcast.148) | data formatting | bytes 327680 | tf_op jit(solution)/shard_map/all_to_all | solution.py:93
  (51 shorter events, 5.6 us)
Async XLA Ops:
  0.6 11.8 %collective-permute-start = (bf16[64,256]{1,0:T(8,128)(2,1)}, bf16[64,256]{1,0:T(8,128)(2,1)S(1)}, u32[]{:S(2)}, u32[]{:S(2)}) collective-permute-start(bf16[64,256]{1,0:T(8,128)(2,1)} %param.7), channel_id=1, source_target_pairs={{0,4},{4,8},{8,12},{12,16},{16,20},{20,24},{24,28},{28,0},{1,5},{5... | collective-permute-start | bytes 98312 | tf_op jit(solution)/shard_map/ppermute | solution.py:14
  1.1 11.4 %collective-permute-start.1 = (bf16[64,256]{1,0:T(8,128)(2,1)}, bf16[64,256]{1,0:T(8,128)(2,1)S(1)}, u32[]{:S(2)}, u32[]{:S(2)}) collective-permute-start(bf16[64,256]{1,0:T(8,128)(2,1)} %param.8), channel_id=1, source_target_pairs={{0,4},{4,8},{8,12},{12,16},{16,20},{20,24},{24,28},{28,0},{1,5},{5... | collective-permute-start | bytes 98312 | tf_op jit(solution)/shard_map/ppermute | solution.py:14
  5.3 5.0 %copy-start.2 = (bf16[64,256]{1,0:T(8,128)(2,1)S(1)}, bf16[64,256]{1,0:T(8,128)(2,1)}, u32[]{:S(2)}) copy-start(bf16[64,256]{1,0:T(8,128)(2,1)} %param.7) | copy-start | bytes 98308
  5.3 5.7 %copy-start = (bf16[64,1280]{1,0:T(8,128)(2,1)S(1)}, bf16[64,1280]{1,0:T(8,128)(2,1)}, u32[]{:S(2)}) copy-start(bf16[64,1280]{1,0:T(8,128)(2,1)} %param.6) | copy-start | bytes 491524
  5.3 12.1 %all-to-all-start = ((bf16[16,4,1280]{2,0,1:T(8,128)(2,1)}), bf16[16,4,1280]{2,0,1:T(8,128)(2,1)S(1)}, u32[]{:S(2)}, u32[]{:S(2)}) async-start(bf16[16,4,1280]{2,0,1:T(8,128)(2,1)} %bitcast.144), calls=%async_computation | async-start | bytes 327680 | tf_op jit(solution)/shard_map/all_to_all | solution.py:49
  10.3 0.7 %copy-start.4 = (f32[10,64]{1,0:T(8,128)S(1)}, f32[10,64]{1,0:T(8,128)}, u32[]{:S(2)}) copy-start(f32[10,64]{1,0:T(8,128)} %param.11) | copy-start | bytes 7684
  11.3 0.8 %copy-start.3 = (bf16[64,256]{1,0:T(8,128)(2,1)S(1)}, bf16[64,256]{1,0:T(8,128)(2,1)}, u32[]{:S(2)}) copy-start(bf16[64,256]{1,0:T(8,128)(2,1)} %param.8) | copy-start | bytes 98308
  11.3 0.9 %copy-start.1 = (bf16[64,1280]{1,0:T(8,128)(2,1)S(1)}, bf16[64,1280]{1,0:T(8,128)(2,1)}, u32[]{:S(2)}) copy-start(bf16[64,1280]{1,0:T(8,128)(2,1)} %param.9) | copy-start | bytes 491524
  12.5 4.3 %collective-permute-start.2 = (bf16[64,256]{1,0:T(8,128)(2,1)S(1)}, bf16[64,256]{1,0:T(8,128)(2,1)S(1)}, u32[]{:S(2)}, u32[]{:S(2)}) collective-permute-start(bf16[64,256]{1,0:T(8,128)(2,1)S(1)} %collective-permute-done), channel_id=1, source_target_pairs={{0,4},{4,8},{8,12},{12,16},{16,20},{20,24},{24,28},{28,0},{1,5},{5... | collective-permute-start | bytes 98312 | tf_op jit(solution)/shard_map/ppermute | solution.py:14
  12.5 4.6 %collective-permute-start.3 = (bf16[64,256]{1,0:T(8,128)(2,1)S(1)}, bf16[64,256]{1,0:T(8,128)(2,1)S(1)}, u32[]{:S(2)}, u32[]{:S(2)}) collective-permute-start(bf16[64,256]{1,0:T(8,128)(2,1)S(1)} %collective-permute-done.1), channel_id=1, source_target_pairs={{0,4},{4,8},{8,12},{12,16},{16,20},{20,24},{24,28},{28,0},{1,5},{5... | collective-permute-start | bytes 98312 | tf_op jit(solution)/shard_map/ppermute | solution.py:14
  18.8 3.1 %collective-permute-start.4 = (f32[64,256]{1,0:T(8,128)S(1)}, f32[64,256]{1,0:T(8,128)S(1)}, u32[]{:S(2)}, u32[]{:S(2)}) collective-permute-start(f32[64,256]{1,0:T(8,128)S(1)} %bitcast.163), channel_id=1, source_target_pairs={{0,28},{4,0},{8,4},{12,8},{16,12},{20,16},{24,20},{28,24},{1,29},{... | collective-permute-start | bytes 196616 | tf_op jit(solution)/shard_map/ppermute | solution.py:14
  18.9 4.7 %collective-permute-start.6 = (f32[64,256]{1,0:T(8,128)S(1)}, f32[64,256]{1,0:T(8,128)S(1)}, u32[]{:S(2)}, u32[]{:S(2)}) collective-permute-start(f32[64,256]{1,0:T(8,128)S(1)} %bitcast.162), channel_id=1, source_target_pairs={{0,28},{4,0},{8,4},{12,8},{16,12},{20,16},{24,20},{28,24},{1,29},{... | collective-permute-start | bytes 196616 | tf_op jit(solution)/shard_map/ppermute | solution.py:14
  21.9 3.5 %collective-permute-start.5 = (f32[64,256]{1,0:T(8,128)S(1)}, f32[64,256]{1,0:T(8,128)S(1)}, u32[]{:S(2)}, u32[]{:S(2)}) collective-permute-start(f32[64,256]{1,0:T(8,128)S(1)} %bitcast_add_fusion.2), channel_id=1, source_target_pairs={{0,28},{4,0},{8,4},{12,8},{16,12},{20,16},{24,20},{28,24},{1,29},{... | collective-permute-start | bytes 196616 | tf_op jit(solution)/shard_map/ppermute | solution.py:14
  23.5 7.6 %collective-permute-start.7 = (f32[64,256]{1,0:T(8,128)S(1)}, f32[64,256]{1,0:T(8,128)S(1)}, u32[]{:S(2)}, u32[]{:S(2)}) collective-permute-start(f32[64,256]{1,0:T(8,128)S(1)} %bitcast_add_fusion), channel_id=1, source_target_pairs={{0,28},{4,0},{8,4},{12,8},{16,12},{20,16},{24,20},{28,24},{1,29},{... | collective-permute-start | bytes 196616 | tf_op jit(solution)/shard_map/ppermute | solution.py:14
  26.0 10.8 %all-to-all-start.2 = ((bf16[4,16,256]{2,1,0:T(8,128)(2,1)}), bf16[4,16,256]{2,1,0:T(8,128)(2,1)S(1)}, u32[]{:S(2)}, u32[]{:S(2)}) async-start(bf16[4,16,256]{2,1,0:T(8,128)(2,1)} %bitcast.29), calls=%async_computation.2 | async-start | bytes 65536 | tf_op jit(solution)/shard_map/all_to_all | solution.py:94
  36.8 8.9 %all-to-all-start.3 = ((bf16[4,16,256]{2,1,0:T(8,128)(2,1)}), bf16[4,16,256]{2,1,0:T(8,128)(2,1)S(1)}, u32[]{:S(2)}, u32[]{:S(2)}) async-start(bf16[4,16,256]{2,1,0:T(8,128)(2,1)} %bitcast.40), calls=%async_computation.3 | async-start | bytes 65536 | tf_op jit(solution)/shard_map/all_to_all | solution.py:95
  45.7 9.3 %all-to-all-start.1 = ((bf16[4,16,1280]{2,1,0:T(8,128)(2,1)}), bf16[4,16,1280]{2,1,0:T(8,128)(2,1)S(1)}, u32[]{:S(2)}, u32[]{:S(2)}) async-start(bf16[4,16,1280]{2,1,0:T(8,128)(2,1)} %all_to_all.57), calls=%async_computation.1 | async-start | bytes 327680 | tf_op jit(solution)/shard_map/all_to_all | solution.py:93
where the time goes:
time: 56.3 us; the launch traced here: 55.7 us
  starting transfers between devices  25.2 us (45%)
  waiting for transfers between devices  17.7 us (31%)
  local copies, waits for them, and re-layouts  6.69 us (12%)
  matrix products  3.67 us (7%)
  other arithmetic  1.54 us (3%)
  between operations  0.9 us (2%)
    ppermute x8, starting transfers between devices, shifted(): lax.ppermute(array, axis, [(i, (i + by) % size) for i in range(size)])  8.5 us
    all_to_all x1, starting transfers between devices, body(): lax.all_to_all(key_low, 'uly', split_axis=0, concat_axis=1, tiled=True)  5.09 us
    all_to_all x1, waiting for transfers between devices, body(): lax.all_to_all(key_low, 'uly', split_axis=0, concat_axis=1, tiled=True)  5.03 us
    all_to_all x1, starting transfers between devices, body(): lax.all_to_all(output_grad, 'uly', split_axis=1, concat_axis=0, tiled=True)  5 us
    all_to_all x1, waiting for transfers between devices, body(): lax.all_to_all(query_low, 'uly', split_axis=0, concat_axis=1, tiled=True)  4.74 us
    all_to_all x1, waiting for transfers between devices, body(): lax.all_to_all(value_low, 'uly', split_axis=0, concat_axis=1, tiled=True)  4.38 us
    ppermute x8, waiting for transfers between devices, shifted(): lax.ppermute(array, axis, [(i, (i + by) % size) for i in range(size)])  3.55 us
    all_to_all x1, starting transfers between devices, body(): lax.all_to_all(query_low, 'uly', split_axis=0, concat_axis=1, tiled=True)  3.35 us
  transfers between devices with their start and end apart: 12, of which 6 were waited for; matrix products, arithmetic and copies ran while one was open for 14% of the time, Pallas kernels for 0%

commit v1 on v0

v1 whole, which is shorter than its diff:
```python
import functools

import jax
import jax.numpy as jnp
from jax import lax
from jax.experimental import pallas as pl
from jax.experimental.pallas import tpu as pltpu
from jax.sharding import PartitionSpec as P

QHEADS = 40
KVHEADS = 8
HEAD_DIM = 128
STEPS = 3
GROUP = QHEADS // KVHEADS
SCALE = HEAD_DIM ** (-0.5)

VMEM = pl.BlockSpec(memory_space=pltpu.VMEM)
ANY = pl.BlockSpec(memory_space=pl.ANY)
PARAMS = pltpu.CompilerParams(vmem_limit_bytes=16 * 1024 * 1024)


def shifted(array, axis, by):
    size = lax.axis_size(axis)
    return lax.ppermute(array, axis, [(i, (i + by) % size) for i in range(size)])


def is_power(n):
    return n & (n - 1) == 0


def partner(me, step, n, back=False):
    if is_power(n):
        return lax.bitwise_xor(me, step)
    return lax.rem(me + (n - step if back else step), n)


def exchange(array, axis, step):
    n = lax.axis_size(axis)
    if is_power(n):
        pairs = [(i, i ^ step) for i in range(n)]
    else:
        pairs = [(i, (i + step) % n) for i in range(n)]
    return lax.ppermute(array, axis, pairs)


def nt(a, b):
    return lax.dot_general(a, b, (((1,), (1,)), ((), ())), preferred_element_type=jnp.float32)


def nn(a, b):
    return lax.dot_general(a, b, (((1,), (0,)), ((), ())), preferred_element_type=jnp.float32)


def tn(a, b):
    return lax.dot_general(a, b, (((0,), (0,)), ((), ())), preferred_element_type=jnp.float32)


def prep_kernel(n, grad, key, value, *refs):
    sends, kv, sems = refs[: n - 1], refs[n - 1], refs[n]
    me = lax.axis_index("uly")
    width = sends[0].shape[1]
    tokens = key.shape[0]
    copies = []
    for step in range(1, n):
        to = partner(me, step, n)
        columns = pl.ds(pl.multiple_of(to * width, width), width)
        copies.append(
            pltpu.make_async_copy(grad.at[:, columns], sends[step - 1], sems.at[step - 1])
        )
    copies.append(pltpu.make_async_copy(key, kv.at[pl.ds(0, tokens)], sems.at[n - 1]))
    copies.append(pltpu.make_async_copy(value, kv.at[pl.ds(tokens, tokens)], sems.at[n]))
    for copy in copies:
        copy.start()
    for copy in copies:
        copy.wait()


def heads_of(ref, g):
    return jnp.concatenate(
        [
            ref[:, pl.ds((g * GROUP + h) * HEAD_DIM, HEAD_DIM)]
            for h in range(GROUP)
        ],
        axis=0,
    )


def main_kernel(n, query, output, lse, grad, key, value, *refs):
    moved = refs[: STEPS - 1]
    received = refs[STEPS - 1 : STEPS - 1 + n - 1]
    rest = refs[STEPS - 1 + n - 1 :]
    far = rest[: STEPS - 1]
    own, dscore, gathered = rest[STEPS - 1 :]
    me = lax.axis_index("uly")
    rows = grad.shape[0]
    width = query.shape[1]
    tokens = query.shape[0]
    kv_local = key.shape[1] // HEAD_DIM
    columns = pl.ds(pl.multiple_of(me * width, width), width)
    gathered[pl.ds(pl.multiple_of(me * rows, rows), rows), :] = grad[:, columns]
    for step in range(1, n):
        source = partner(me, step, n, back=True)
        gathered[pl.ds(pl.multiple_of(source * rows, rows), rows), :] = received[step - 1][...]
    ones = jnp.ones((8, HEAD_DIM), jnp.bfloat16)
    for g in range(kv_local):
        cols = pl.ds(g * HEAD_DIM, HEAD_DIM)
        q = heads_of(query, g)
        go = heads_of(gathered, g)
        o = heads_of(output, g)
        k = jnp.concatenate([key[:, cols]] + [m[pl.ds(0, tokens), cols] for m in moved], axis=0)
        v = jnp.concatenate([value[:, cols]] + [m[pl.ds(tokens, tokens), cols] for m in moved], axis=0)
        product = go.astype(jnp.float32) * o.astype(jnp.float32)
        high = product.astype(jnp.bfloat16)
        low = (product - high.astype(jnp.float32)).astype(jnp.bfloat16)
        delta = (nt(ones, high) + nt(ones, low))[0:1, :]
        lse_row = jnp.concatenate(
            [lse[pl.ds(g * GROUP + h, 1), :] for h in range(GROUP)], axis=1
        )
        prob = jnp.exp(nt(k, q) * SCALE - lse_row)
        ds = (prob * (nt(v, go) - delta)).astype(jnp.bfloat16)
        dv = nn(prob.astype(jnp.bfloat16), go)
        dk = nn(ds, q) * SCALE
        dscore[g] = ds
        own[pl.ds(0, tokens), cols] = dk[:tokens]
        own[pl.ds(tokens, tokens), cols] = dv[:tokens]
        for i in range(1, STEPS):
            part = slice(i * tokens, (i + 1) * tokens)
            far[i - 1][pl.ds(0, tokens), cols] = dk[part].astype(jnp.bfloat16)
            far[i - 1][pl.ds(tokens, tokens), cols] = dv[part].astype(jnp.bfloat16)


def query_kernel(dscore, key, *refs):
    moved, out = refs[: STEPS - 1], refs[STEPS - 1]
    tokens = key.shape[0]
    kv_local = key.shape[1] // HEAD_DIM
    for g in range(kv_local):
        cols = pl.ds(g * HEAD_DIM, HEAD_DIM)
        k = jnp.concatenate([key[:, cols]] + [m[pl.ds(0, tokens), cols] for m in moved], axis=0)
        dq = (tn(dscore[g], k) * SCALE).astype(jnp.bfloat16)
        for h in range(GROUP):
            out[:, pl.ds((g * GROUP + h) * HEAD_DIM, HEAD_DIM)] = dq[h * tokens : (h + 1) * tokens]


def sum_kernel(n, dq, own, *refs):
    back = refs[: STEPS - 1]
    sends, total = refs[STEPS - 1 : -1], refs[-1]
    me = lax.axis_index("uly")
    width = dq.shape[1]
    kv_width = own.shape[1]
    tokens = dq.shape[0]
    rows = tokens // n
    acc = own[...]
    for b in back:
        acc = acc + b[...].astype(jnp.float32)
    total[...] = acc.astype(jnp.bfloat16)
    for step in range(n):
        to = partner(me, step, n) if step else me
        start = pl.multiple_of(to * rows, rows)
        sends[step][:, pl.ds(0, width)] = dq[pl.ds(start, rows), :]
        sends[step][:, pl.ds(width, kv_width)] = total[pl.ds(start, rows), :]
        sends[step][:, pl.ds(width + kv_width, kv_width)] = total[
            pl.ds(pl.multiple_of(start + tokens, rows), rows), :
        ]


def place_kernel(n, *refs):
    parts, (dq, dk, dv, sems) = refs[:n], refs[n:]
    me = lax.axis_index("uly")
    width = dq.shape[1] // n
    kv_width = dk.shape[1] // n
    copies = []
    for step in range(n):
        source = partner(me, step, n, back=True) if step else me
        part = parts[step]
        for i, (out, first, size) in enumerate(
            ((dq, 0, width), (dk, width, kv_width), (dv, width + kv_width, kv_width))
        ):
            columns = pl.ds(pl.multiple_of(source * size, size), size)
            copies.append(
                pltpu.make_async_copy(
                    part.at[:, pl.ds(first, size)], out.at[:, columns], sems.at[step, i]
                )
            )
    for copy in copies:
        copy.start()
    for copy in copies:
        copy.wait()


def shape(dims, kind=jnp.bfloat16):
    return jax.ShapeDtypeStruct(dims, kind)


def body(query, key, value, output, grad, lse):
    n = lax.axis_size("uly")
    tokens, width = query.shape
    kv_width = key.shape[1]
    kv_local = kv_width // HEAD_DIM
    rows = grad.shape[0]
    *sends, kv = pl.pallas_call(
        functools.partial(prep_kernel, n),
        out_shape=[shape((rows, width))] * (n - 1) + [shape((2 * tokens, kv_width))],
        in_specs=[ANY] * 3,
        out_specs=[ANY] * n,
        scratch_shapes=[pltpu.SemaphoreType.DMA((n + 1,))],
        compiler_params=PARAMS,
        name="prep",
    )(grad, key, value)
    received = [exchange(sends[step - 1], "uly", step) for step in range(1, n)]
    moved = [shifted(kv, "blk", i) for i in range(1, STEPS)]
    *far, own, dscore = pl.pallas_call(
        functools.partial(main_kernel, n),
        out_shape=[shape((2 * tokens, kv_width))] * (STEPS - 1)
        + [
            shape((2 * tokens, kv_width), jnp.float32),
            shape((kv_local, STEPS * tokens, GROUP * tokens)),
        ],
        in_specs=[VMEM] * (6 + STEPS - 1 + n - 1),
        out_specs=[VMEM] * (STEPS + 1),
        scratch_shapes=[pltpu.VMEM((tokens, width), jnp.bfloat16)],
        compiler_params=PARAMS,
        name="main",
    )(query, output, lse, grad, key, value, *moved, *received)
    back = [shifted(far[i - 1], "blk", -i) for i in range(1, STEPS)]
    dq = pl.pallas_call(
        query_kernel,
        out_shape=shape((tokens, width)),
        in_specs=[VMEM] * (STEPS + 1),
        out_specs=VMEM,
        compiler_params=PARAMS,
        name="query",
    )(dscore, key, *moved)
    parts = pl.pallas_call(
        functools.partial(sum_kernel, n),
        out_shape=[shape((rows, width + 2 * kv_width))] * n,
        in_specs=[VMEM] * (STEPS + 1),
        out_specs=[VMEM] * n,
        scratch_shapes=[pltpu.VMEM((2 * tokens, kv_width), jnp.bfloat16)],
        compiler_params=PARAMS,
        name="sum",
    )(dq, own, *back)
    final = [parts[0]] + [exchange(parts[step], "uly", step) for step in range(1, n)]
    return pl.pallas_call(
        functools.partial(place_kernel, n),
        out_shape=[
            shape((rows, width * n)),
            shape((rows, kv_width * n)),
            shape((rows, kv_width * n)),
        ],
        in_specs=[ANY] * n,
        out_specs=[ANY] * 3,
        scratch_shapes=[pltpu.SemaphoreType.DMA((n, 3))],
        compiler_params=PARAMS,
        name="place",
    )(*final)


def solution(mesh):
    placed = (
        P("blk", "uly"),
        P("blk", "uly"),
        P("blk", "uly"),
        P("blk", "uly"),
        P(("blk", "uly"), None),
        P("uly", "blk"),
    )
    return jax.shard_map(
        lambda *args: tuple(body(*args)),
        mesh=mesh,
        in_specs=placed,
        out_specs=(P(("blk", "uly"), None), P(("blk", "uly"), None), P(("blk", "uly"), None)),
        check_vma=False,
    )
```

time: 56.3 us -> 32.4 us (0.58)
  starting transfers between devices: 25.2 us -> 13.4 us
  waiting for transfers between devices: 17.7 us -> 12.6 us
  matrix products: 3.67 us -> 0 us
  local copies, waits for them, and re-layouts: 6.69 us -> 3.35 us
  Pallas kernels: 0 us -> 2.06 us
  other arithmetic: 1.54 us -> 0 us
    all_to_all x4 -> x0, starting transfers between devices: 16.7 us -> none  [the longest x1 5.09 us: body(): lax.all_to_all(key_low, 'uly', split_axis=0, concat_axis=1, tiled=True)]
    all_to_all x4 -> x0, waiting for transfers between devices: 14.1 us -> none  [the longest x1 5.03 us: body(): lax.all_to_all(key_low, 'uly', split_axis=0, concat_axis=1, tiled=True)]
    ppermute x0 -> x6, waiting for transfers between devices: none -> 8.94 us  [exchange(): return lax.ppermute(array, axis, pairs)]
    ppermute x0 -> x6, starting transfers between devices: none -> 8.83 us  [exchange(): return lax.ppermute(array, axis, pairs)]
    all_to_all x5 -> x0, local copies, waits for them, and re-layouts: 4.36 us -> none  [the longest x1 1.59 us: body(): lax.all_to_all(output_grad, 'uly', split_axis=1, concat_axis=0, tiled=True)]
    ppermute x8 -> x4, starting transfers between devices: 8.5 us -> 4.55 us  [shifted(): lax.ppermute(array, axis, [(i, (i + by) % size) for i in range(size)])]
    dot_general x15 -> x0, matrix products: 3.67 us -> none  [the longest x3 0.81 us: block_grads(): jnp.einsum('tgrd,ugd->grtu', query_heads, key_block, preferred_element_ty...]
    pallas_call x0 -> x5, Pallas kernels: none -> 2.06 us  [the longest x1 0.79 us: body(): pl.pallas_call(functools.partial(place_kernel, n), out_shape=[shape((rows...]
  transfers between devices with their start and end apart: 12 -> 10, of which waited for: 6 -> 6; matrix products, arithmetic and copies ran while one was open for 14% -> 0% of each run, Pallas kernels for 0% -> 1%
where the time goes in v1:
time: 32.4 us; the launch traced here: 32.1 us
  starting transfers between devices  13.4 us (41%)
  waiting for transfers between devices  12.6 us (39%)
  local copies, waits for them, and re-layouts  3.35 us (10%)
  Pallas kernels  2.06 us (6%)
  between operations  0.71 us (2%)
    ppermute x6, waiting for transfers between devices, exchange(): return lax.ppermute(array, axis, pairs)  8.94 us
    ppermute x6, starting transfers between devices, exchange(): return lax.ppermute(array, axis, pairs)  8.83 us
    ppermute x4, starting transfers between devices, shifted(): lax.ppermute(array, axis, [(i, (i + by) % size) for i in range(size)])  4.55 us
    ppermute x4, waiting for transfers between devices, shifted(): lax.ppermute(array, axis, [(i, (i + by) % size) for i in range(size)])  3.62 us
    unnamed x14, local copies, waits for them, and re-layouts  3.35 us
    pallas_call x1, Pallas kernels, body(): pl.pallas_call(functools.partial(place_kernel, n), out_shape=[shape((rows...  0.79 us
    pallas_call x1, Pallas kernels, body(): pl.pallas_call(functools.partial(main_kernel, n), out_shape=[shape((2 * t...  0.74 us
  transfers between devices with their start and end apart: 10, of which 6 were waited for; matrix products, arithmetic and copies ran while one was open for 0% of the time, Pallas kernels for 1%

profile of v1, /device:TPU:0, one launch (start us, length us, event | category | flops | bytes accessed | tf_op | source)
XLA Modules:
  0.0 32.1 jit_solution(15788845789578862112)
XLA Ops:
  0.6 0.9 %copy-done = bf16[16,5120]{1,0:T(8,128)(2,1)S(1)} copy-done((bf16[16,5120]{1,0:T(8,128)(2,1)S(1)}, bf16[16,5120]{1,0:T(8,128)(2,1)}, u32[]{:S(2)}) %copy-start) | copy-done | bytes 163864
  1.6 0.8 %copy-done.1 = bf16[64,256]{1,0:T(8,128)(2,1)S(1)} copy-done((bf16[64,256]{1,0:T(8,128)(2,1)S(1)}, bf16[64,256]{1,0:T(8,128)(2,1)}, u32[]{:S(2)}) %copy-start.1) | copy-done | bytes 32792
  2.3 0.8 %copy-done.5 = bf16[64,256]{1,0:T(8,128)(2,1)S(1)} copy-done((bf16[64,256]{1,0:T(8,128)(2,1)S(1)}, bf16[64,256]{1,0:T(8,128)(2,1)}, u32[]{:S(2)}) %copy-start.5) | copy-done | bytes 32792
  3.1 0.2 prep.1
  3.3 3.0 %collective-permute-start.1 = (bf16[128,256]{1,0:T(8,128)(2,1)S(1)}, bf16[128,256]{1,0:T(8,128)(2,1)S(1)}, u32[]{:S(2)}, u32[]{:S(2)}) collective-permute-start(bf16[128,256]{1,0:T(8,128)(2,1)S(1)} %get-tuple-element.15), channel_id=1, source_target_pairs={{0,8},{4,12},{8,16},{12,20},{16,24},{20,28},{24,0},{28,4},{1,9},{5... | collective-permute-start | bytes 196616 | tf_op jit(solution)/shard_map/ppermute | solution.py:24
  6.3 1.6 %collective-permute-start.2 = (bf16[16,1280]{1,0:T(8,128)(2,1)S(1)}, bf16[16,1280]{1,0:T(8,128)(2,1)S(1)}, u32[]{:S(2)}, u32[]{:S(2)}) collective-permute-start(bf16[16,1280]{1,0:T(8,128)(2,1)S(1)} %get-tuple-element.16), channel_id=1, source_target_pairs={{0,1},{1,0},{2,3},{3,2},{4,5},{5,4},{6,7},{7,6},{8,9},{9,8},{10,11... | collective-permute-start | bytes 122888 | tf_op jit(solution)/shard_map/ppermute | solution.py:43
  7.9 2.6 %collective-permute-start.3 = (bf16[16,1280]{1,0:T(8,128)(2,1)S(1)}, bf16[16,1280]{1,0:T(8,128)(2,1)S(1)}, u32[]{:S(2)}, u32[]{:S(2)}) collective-permute-start(bf16[16,1280]{1,0:T(8,128)(2,1)S(1)} %get-tuple-element.17), channel_id=1, source_target_pairs={{0,2},{1,3},{2,0},{3,1},{4,6},{5,7},{6,4},{7,5},{8,10},{9,11},{10,... | collective-permute-start | bytes 122888 | tf_op jit(solution)/shard_map/ppermute | solution.py:43
  10.4 0.2 collective-permute-start.4
  10.7 3.3 %collective-permute-done.3.refs_3_ = bf16[16,1280]{1,0:T(8,128)(2,1)S(1)} collective-permute-done((bf16[16,1280]{1,0:T(8,128)(2,1)S(1)}, bf16[16,1280]{1,0:T(8,128)(2,1)S(1)}, u32[]{:S(2)}, u32[]{:S(2)}) %collective-permute-start.3) | collective-permute-done | bytes 40992 | tf_op jit(solution)/shard_map/ppermute | solution.py:43
  13.9 2.7 %collective-permute-done.4.refs_4_ = bf16[16,1280]{1,0:T(8,128)(2,1)S(1)} collective-permute-done((bf16[16,1280]{1,0:T(8,128)(2,1)S(1)}, bf16[16,1280]{1,0:T(8,128)(2,1)S(1)}, u32[]{:S(2)}, u32[]{:S(2)}) %collective-permute-start.4) | collective-permute-done | bytes 40992 | tf_op jit(solution)/shard_map/ppermute | solution.py:43
  16.6 0.0 copy-start.4
  16.6 0.9 %copy-done.4 = bf16[64,1280]{1,0:T(8,128)(2,1)S(1)} copy-done((bf16[64,1280]{1,0:T(8,128)(2,1)S(1)}, bf16[64,1280]{1,0:T(8,128)(2,1)}, u32[]{:S(2)}) %copy-start.4) | copy-done | bytes 163864
  17.5 0.7 %main.1 = (bf16[128,256]{1,0:T(8,128)(2,1)S(1)}, bf16[128,256]{1,0:T(8,128)(2,1)S(1)}, f32[128,256]{1,0:T(8,128)S(1)}, bf16[2,192,320]{2,1,0:T(8,128)(2,1)S(1)}) custom-call(bf16[64,1280]{1,0:T(8,128)(2,1)S(1)} %copy-done.3, bf16[64,1280]{1,0:T(8,128)(2,1)S(1)} %copy-done.4, f32[10,64]{1,0:T(8,128)S(1)} %copy-done.6, bf16[16,5120]{1,0:T(8,128)(2,1)S(1)} %copy-done, ...), custom_call_target="tpu_custom_call" | custom-call | tf_op jit(solution)/shard_map/main/pallas_call | solution.py:211
  18.3 1.2 %collective-permute-start.5 = (bf16[128,256]{1,0:T(8,128)(2,1)S(1)}, bf16[128,256]{1,0:T(8,128)(2,1)S(1)}, u32[]{:S(2)}, u32[]{:S(2)}) collective-permute-start(bf16[128,256]{1,0:T(8,128)(2,1)S(1)} %get-tuple-element.21), channel_id=1, source_target_pairs={{0,28},{4,0},{8,4},{12,8},{16,12},{20,16},{24,20},{28,24},{1,29},{... | collective-permute-start | bytes 196616 | tf_op jit(solution)/shard_map/ppermute | solution.py:24
  19.5 0.3 %collective-permute-start.6 = (bf16[128,256]{1,0:T(8,128)(2,1)S(1)}, bf16[128,256]{1,0:T(8,128)(2,1)S(1)}, u32[]{:S(2)}, u32[]{:S(2)}) collective-permute-start(bf16[128,256]{1,0:T(8,128)(2,1)S(1)} %get-tuple-element.22), channel_id=1, source_target_pairs={{0,24},{4,28},{8,0},{12,4},{16,8},{20,12},{24,16},{28,20},{1,25},{... | collective-permute-start | bytes 196616 | tf_op jit(solution)/shard_map/ppermute | solution.py:24
  19.9 0.3 query.3.dq
  20.2 1.7 %collective-permute-done.5.refs_0_ = bf16[128,256]{1,0:T(8,128)(2,1)S(1)} collective-permute-done((bf16[128,256]{1,0:T(8,128)(2,1)S(1)}, bf16[128,256]{1,0:T(8,128)(2,1)S(1)}, u32[]{:S(2)}, u32[]{:S(2)}) %collective-permute-start.5) | collective-permute-done | bytes 65568 | tf_op jit(solution)/shard_map/ppermute | solution.py:24
  21.8 2.0 %collective-permute-done.6.refs_1_ = bf16[128,256]{1,0:T(8,128)(2,1)S(1)} collective-permute-done((bf16[128,256]{1,0:T(8,128)(2,1)S(1)}, bf16[128,256]{1,0:T(8,128)(2,1)S(1)}, u32[]{:S(2)}, u32[]{:S(2)}) %collective-permute-start.6) | collective-permute-done | bytes 65568 | tf_op jit(solution)/shard_map/ppermute | solution.py:24
  23.8 0.1 collective-permute-start.7
  23.9 1.3 %collective-permute-start.8 = (bf16[16,1792]{1,0:T(8,128)(2,1)S(1)}, bf16[16,1792]{1,0:T(8,128)(2,1)S(1)}, u32[]{:S(2)}, u32[]{:S(2)}) collective-permute-start(bf16[16,1792]{1,0:T(8,128)(2,1)S(1)} %get-tuple-element.25), channel_id=1, source_target_pairs={{0,2},{1,3},{2,0},{3,1},{4,6},{5,7},{6,4},{7,5},{8,10},{9,11},{10,... | collective-permute-start | bytes 172040 | tf_op jit(solution)/shard_map/ppermute | solution.py:43
  25.2 3.0 %collective-permute-start.9 = (bf16[16,1792]{1,0:T(8,128)(2,1)S(1)}, bf16[16,1792]{1,0:T(8,128)(2,1)S(1)}, u32[]{:S(2)}, u32[]{:S(2)}) collective-permute-start(bf16[16,1792]{1,0:T(8,128)(2,1)S(1)} %get-tuple-element.26), channel_id=1, source_target_pairs={{0,3},{1,2},{2,1},{3,0},{4,7},{5,6},{6,5},{7,4},{8,11},{9,10},{10,... | collective-permute-start | bytes 172040 | tf_op jit(solution)/shard_map/ppermute | solution.py:43
  28.3 1.5 %collective-permute-done.8.refs_2_ = bf16[16,1792]{1,0:T(8,128)(2,1)S(1)} collective-permute-done((bf16[16,1792]{1,0:T(8,128)(2,1)S(1)}, bf16[16,1792]{1,0:T(8,128)(2,1)S(1)}, u32[]{:S(2)}, u32[]{:S(2)}) %collective-permute-start.8) | collective-permute-done | bytes 57376 | tf_op jit(solution)/shard_map/ppermute | solution.py:43
  29.8 1.5 %collective-permute-done.9.refs_3_ = bf16[16,1792]{1,0:T(8,128)(2,1)S(1)} collective-permute-done((bf16[16,1792]{1,0:T(8,128)(2,1)S(1)}, bf16[16,1792]{1,0:T(8,128)(2,1)S(1)}, u32[]{:S(2)}, u32[]{:S(2)}) %collective-permute-start.9) | collective-permute-done | bytes 57376 | tf_op jit(solution)/shard_map/ppermute | solution.py:43
  31.3 0.8 %place.1 = (bf16[16,5120]{1,0:T(8,128)(2,1)}, bf16[16,1024]{1,0:T(8,128)(2,1)}, bf16[16,1024]{1,0:T(8,128)(2,1)}) custom-call(bf16[16,1792]{1,0:T(8,128)(2,1)S(1)} %get-tuple-element.23.refs_0_, bf16[16,1792]{1,0:T(8,128)(2,1)S(1)} %collective-permute-done.7.refs_1_, bf16[16,1792]{1,0:T(8,128)(2,1)S(1)} %collective-permute-done.8.refs_2_, ...), custom_call_target="tpu_custom_call" | custom-call | tf_op jit(solution)/shard_map/place/pallas_call | solution.py:243
  (15 shorter events, 0.1 us)
Async XLA Ops:
  0.6 0.9 %copy-start = (bf16[16,5120]{1,0:T(8,128)(2,1)S(1)}, bf16[16,5120]{1,0:T(8,128)(2,1)}, u32[]{:S(2)}) copy-start(bf16[16,5120]{1,0:T(8,128)(2,1)} %grad.3) | copy-start | bytes 491524
  1.5 0.8 %copy-start.1 = (bf16[64,256]{1,0:T(8,128)(2,1)S(1)}, bf16[64,256]{1,0:T(8,128)(2,1)}, u32[]{:S(2)}) copy-start(bf16[64,256]{1,0:T(8,128)(2,1)} %key.5) | copy-start | bytes 98308
  2.3 0.8 %copy-start.5 = (bf16[64,256]{1,0:T(8,128)(2,1)S(1)}, bf16[64,256]{1,0:T(8,128)(2,1)}, u32[]{:S(2)}) copy-start(bf16[64,256]{1,0:T(8,128)(2,1)} %value.3) | copy-start | bytes 98308
  3.1 13.6 %copy-start.3 = (bf16[64,1280]{1,0:T(8,128)(2,1)S(1)}, bf16[64,1280]{1,0:T(8,128)(2,1)}, u32[]{:S(2)}) copy-start(bf16[64,1280]{1,0:T(8,128)(2,1)} %query.2) | copy-start | bytes 491524
  3.1 13.6 %copy-start.6 = (f32[10,64]{1,0:T(8,128)S(1)}, f32[10,64]{1,0:T(8,128)}, u32[]{:S(2)}) copy-start(f32[10,64]{1,0:T(8,128)} %lse.1) | copy-start | bytes 7684
  3.3 13.3 %collective-permute-start.1 = (bf16[128,256]{1,0:T(8,128)(2,1)S(1)}, bf16[128,256]{1,0:T(8,128)(2,1)S(1)}, u32[]{:S(2)}, u32[]{:S(2)}) collective-permute-start(bf16[128,256]{1,0:T(8,128)(2,1)S(1)} %get-tuple-element.15), channel_id=1, source_target_pairs={{0,8},{4,12},{8,16},{12,20},{16,24},{20,28},{24,0},{28,4},{1,9},{5... | collective-permute-start | bytes 196616 | tf_op jit(solution)/shard_map/ppermute | solution.py:24
  6.3 10.3 %collective-permute-start = (bf16[128,256]{1,0:T(8,128)(2,1)S(1)}, bf16[128,256]{1,0:T(8,128)(2,1)S(1)}, u32[]{:S(2)}, u32[]{:S(2)}) collective-permute-start(bf16[128,256]{1,0:T(8,128)(2,1)S(1)} %get-tuple-element.15), channel_id=1, source_target_pairs={{0,4},{4,8},{8,12},{12,16},{16,20},{20,24},{24,28},{28,0},{1,5},{5... | collective-permute-start | bytes 196616 | tf_op jit(solution)/shard_map/ppermute | solution.py:24
  6.3 4.4 %collective-permute-start.2 = (bf16[16,1280]{1,0:T(8,128)(2,1)S(1)}, bf16[16,1280]{1,0:T(8,128)(2,1)S(1)}, u32[]{:S(2)}, u32[]{:S(2)}) collective-permute-start(bf16[16,1280]{1,0:T(8,128)(2,1)S(1)} %get-tuple-element.16), channel_id=1, source_target_pairs={{0,1},{1,0},{2,3},{3,2},{4,5},{5,4},{6,7},{7,6},{8,9},{9,8},{10,11... | collective-permute-start | bytes 122888 | tf_op jit(solution)/shard_map/ppermute | solution.py:43
  7.9 6.1 %collective-permute-start.3 = (bf16[16,1280]{1,0:T(8,128)(2,1)S(1)}, bf16[16,1280]{1,0:T(8,128)(2,1)S(1)}, u32[]{:S(2)}, u32[]{:S(2)}) collective-permute-start(bf16[16,1280]{1,0:T(8,128)(2,1)S(1)} %get-tuple-element.17), channel_id=1, source_target_pairs={{0,2},{1,3},{2,0},{3,1},{4,6},{5,7},{6,4},{7,5},{8,10},{9,11},{10,... | collective-permute-start | bytes 122888 | tf_op jit(solution)/shard_map/ppermute | solution.py:43
  10.4 9.4 %copy-start.2 = (bf16[64,256]{1,0:T(8,128)(2,1)S(1)}, bf16[64,256]{1,0:T(8,128)(2,1)}, u32[]{:S(2)}) copy-start(bf16[64,256]{1,0:T(8,128)(2,1)} %key.5) | copy-start | bytes 98308
  10.4 6.2 %collective-permute-start.4 = (bf16[16,1280]{1,0:T(8,128)(2,1)S(1)}, bf16[16,1280]{1,0:T(8,128)(2,1)S(1)}, u32[]{:S(2)}, u32[]{:S(2)}) collective-permute-start(bf16[16,1280]{1,0:T(8,128)(2,1)S(1)} %get-tuple-element.18), channel_id=1, source_target_pairs={{0,3},{1,2},{2,1},{3,0},{4,7},{5,6},{6,5},{7,4},{8,11},{9,10},{10,... | collective-permute-start | bytes 122888 | tf_op jit(solution)/shard_map/ppermute | solution.py:43
  16.6 0.9 %copy-start.4 = (bf16[64,1280]{1,0:T(8,128)(2,1)S(1)}, bf16[64,1280]{1,0:T(8,128)(2,1)}, u32[]{:S(2)}) copy-start(bf16[64,1280]{1,0:T(8,128)(2,1)} %output.1) | copy-start | bytes 491524
  18.3 3.5 %collective-permute-start.5 = (bf16[128,256]{1,0:T(8,128)(2,1)S(1)}, bf16[128,256]{1,0:T(8,128)(2,1)S(1)}, u32[]{:S(2)}, u32[]{:S(2)}) collective-permute-start(bf16[128,256]{1,0:T(8,128)(2,1)S(1)} %get-tuple-element.21), channel_id=1, source_target_pairs={{0,28},{4,0},{8,4},{12,8},{16,12},{20,16},{24,20},{28,24},{1,29},{... | collective-permute-start | bytes 196616 | tf_op jit(solution)/shard_map/ppermute | solution.py:24
  19.5 4.3 %collective-permute-start.6 = (bf16[128,256]{1,0:T(8,128)(2,1)S(1)}, bf16[128,256]{1,0:T(8,128)(2,1)S(1)}, u32[]{:S(2)}, u32[]{:S(2)}) collective-permute-start(bf16[128,256]{1,0:T(8,128)(2,1)S(1)} %get-tuple-element.22), channel_id=1, source_target_pairs={{0,24},{4,28},{8,0},{12,4},{16,8},{20,12},{24,16},{28,20},{1,25},{... | collective-permute-start | bytes 196616 | tf_op jit(solution)/shard_map/ppermute | solution.py:24
  23.8 4.5 %collective-permute-start.7 = (bf16[16,1792]{1,0:T(8,128)(2,1)S(1)}, bf16[16,1792]{1,0:T(8,128)(2,1)S(1)}, u32[]{:S(2)}, u32[]{:S(2)}) collective-permute-start(bf16[16,1792]{1,0:T(8,128)(2,1)S(1)} %get-tuple-element.24), channel_id=1, source_target_pairs={{0,1},{1,0},{2,3},{3,2},{4,5},{5,4},{6,7},{7,6},{8,9},{9,8},{10,11... | collective-permute-start | bytes 172040 | tf_op jit(solution)/shard_map/ppermute | solution.py:43
  23.9 5.9 %collective-permute-start.8 = (bf16[16,1792]{1,0:T(8,128)(2,1)S(1)}, bf16[16,1792]{1,0:T(8,128)(2,1)S(1)}, u32[]{:S(2)}, u32[]{:S(2)}) collective-permute-start(bf16[16,1792]{1,0:T(8,128)(2,1)S(1)} %get-tuple-element.25), channel_id=1, source_target_pairs={{0,2},{1,3},{2,0},{3,1},{4,6},{5,7},{6,4},{7,5},{8,10},{9,11},{10,... | collective-permute-start | bytes 172040 | tf_op jit(solution)/shard_map/ppermute | solution.py:43
  25.2 6.0 %collective-permute-start.9 = (bf16[16,1792]{1,0:T(8,128)(2,1)S(1)}, bf16[16,1792]{1,0:T(8,128)(2,1)S(1)}, u32[]{:S(2)}, u32[]{:S(2)}) collective-permute-start(bf16[16,1792]{1,0:T(8,128)(2,1)S(1)} %get-tuple-element.26), channel_id=1, source_target_pairs={{0,3},{1,2},{2,1},{3,0},{4,7},{5,6},{6,5},{7,4},{8,11},{9,10},{10,... | collective-permute-start | bytes 172040 | tf_op jit(solution)/shard_map/ppermute | solution.py:43

commit v2 on v1

--- a/solution.py
+++ b/solution.py
@@ -16,6 +16,7 @@
 
 VMEM = pl.BlockSpec(memory_space=pltpu.VMEM)
 ANY = pl.BlockSpec(memory_space=pl.ANY)
+HBM = pl.BlockSpec(memory_space=pltpu.HBM)
 PARAMS = pltpu.CompilerParams(vmem_limit_bytes=16 * 1024 * 1024)
 
 
@@ -56,70 +57,91 @@
 
 
 def prep_kernel(n, grad, key, value, *refs):
-    sends, kv, sems = refs[: n - 1], refs[n - 1], refs[n]
+    slices, kv, sems = refs[:n], refs[n], refs[n + 1]
     me = lax.axis_index("uly")
-    width = sends[0].shape[1]
+    width = slices[0].shape[1]
     tokens = key.shape[0]
-    copies = []
-    for step in range(1, n):
-        to = partner(me, step, n)
+    copies = [
+        pltpu.make_async_copy(key, kv.at[pl.ds(0, tokens)], sems.at[n]),
+        pltpu.make_async_copy(value, kv.at[pl.ds(tokens, tokens)], sems.at[n + 1]),
+    ]
+    for step in range(n):
+        to = partner(me, step, n) if step else me
         columns = pl.ds(pl.multiple_of(to * width, width), width)
-        copies.append(
-            pltpu.make_async_copy(grad.at[:, columns], sends[step - 1], sems.at[step - 1])
+        copies.append(pltpu.make_async_copy(grad.at[:, columns], slices[step], sems.at[step]))
+    for copy in copies:
+        copy.start()
+    for copy in copies:
+        copy.wait()
+
+
+def early_kernel(query, output, lse, key, value, *refs):
+    moved, refs = refs[: STEPS - 1], refs[STEPS - 1 :]
+    prob, queries, outputs, keys, values, query_in, output_in, lse_in, sems = refs
+    tokens = key.shape[0]
+    kv_local = key.shape[1] // HEAD_DIM
+    copies = [
+        pltpu.make_async_copy(query, query_in, sems.at[0]),
+        pltpu.make_async_copy(output, output_in, sems.at[1]),
+        pltpu.make_async_copy(lse, lse_in, sems.at[2]),
+    ]
+    for g in range(kv_local):
+        cols = pl.ds(g * HEAD_DIM, HEAD_DIM)
+        own = pl.ds(0, tokens)
+        copies.append(pltpu.make_async_copy(key.at[:, cols], keys.at[g, own], sems.at[3 + 2 * g]))
+        copies.append(pltpu.make_async_copy(value.at[:, cols], values.at[g, own], sems.at[4 + 2 * g]))
+    for copy in copies:
+        copy.start()
+    for g in range(kv_local):
+        cols = pl.ds(g * HEAD_DIM, HEAD_DIM)
+        for i in range(1, STEPS):
+            part = pl.ds(i * tokens, tokens)
+            keys[g, part] = moved[i - 1][pl.ds(0, tokens), cols]
+            values[g, part] = moved[i - 1][pl.ds(tokens, tokens), cols]
+    for copy in copies:
+        copy.wait()
+    for g in range(kv_local):
+        for h in range(GROUP):
+            head = pl.ds((g * GROUP + h) * HEAD_DIM, HEAD_DIM)
+            part = pl.ds(h * tokens, tokens)
+            queries[g, part] = query_in[:, head]
+            outputs[g, part] = output_in[:, head]
+        lse_row = jnp.concatenate(
+            [lse_in[pl.ds(g * GROUP + h, 1), :] for h in range(GROUP)], axis=1
         )
-    copies.append(pltpu.make_async_copy(key, kv.at[pl.ds(0, tokens)], sems.at[n - 1]))
-    copies.append(pltpu.make_async_copy(value, kv.at[pl.ds(tokens, tokens)], sems.at[n]))
-    for copy in copies:
-        copy.start()
-    for copy in copies:
-        copy.wait()
-
-
-def heads_of(ref, g):
-    return jnp.concatenate(
-        [
-            ref[:, pl.ds((g * GROUP + h) * HEAD_DIM, HEAD_DIM)]
-            for h in range(GROUP)
-        ],
-        axis=0,
-    )
-
-
-def main_kernel(n, query, output, lse, grad, key, value, *refs):
-    moved = refs[: STEPS - 1]
-    received = refs[STEPS - 1 : STEPS - 1 + n - 1]
-    rest = refs[STEPS - 1 + n - 1 :]
+        prob[g] = jnp.exp(nt(keys[g], queries[g]) * SCALE - lse_row)
+
+
+def main_kernel(n, prob, queries, outputs, keys, values, mine, *refs):
+    received = refs[: n - 1][::-1]
+    rest = refs[n - 1 :]
     far = rest[: STEPS - 1]
-    own, dscore, gathered = rest[STEPS - 1 :]
+    own, dscore, stacked = rest[STEPS - 1 :]
     me = lax.axis_index("uly")
-    rows = grad.shape[0]
-    width = query.shape[1]
-    tokens = query.shape[0]
-    kv_local = key.shape[1] // HEAD_DIM
-    columns = pl.ds(pl.multiple_of(me * width, width), width)
-    gathered[pl.ds(pl.multiple_of(me * rows, rows), rows), :] = grad[:, columns]
-    for step in range(1, n):
-        source = partner(me, step, n, back=True)
-        gathered[pl.ds(pl.multiple_of(source * rows, rows), rows), :] = received[step - 1][...]
+    rows = mine.shape[0]
+    tokens = rows * n
+    kv_local = prob.shape[0]
+    for step in range(n):
+        source = partner(me, step, n, back=True) if step else me
+        piece = received[step - 1] if step else mine
+        start = pl.multiple_of(source * rows, rows)
+        for g in range(kv_local):
+            for h in range(GROUP):
+                stacked[g, pl.ds(start + h * tokens, rows)] = piece[
+                    :, pl.ds((g * GROUP + h) * HEAD_DIM, HEAD_DIM)
+                ]
     ones = jnp.ones((8, HEAD_DIM), jnp.bfloat16)
     for g in range(kv_local):
         cols = pl.ds(g * HEAD_DIM, HEAD_DIM)
-        q = heads_of(query, g)
-        go = heads_of(gathered, g)
-        o = heads_of(output, g)
-        k = jnp.concatenate([key[:, cols]] + [m[pl.ds(0, tokens), cols] for m in moved], axis=0)
-        v = jnp.concatenate([value[:, cols]] + [m[pl.ds(tokens, tokens), cols] for m in moved], axis=0)
-        product = go.astype(jnp.float32) * o.astype(jnp.float32)
+        go = stacked[g]
+        product = go.astype(jnp.float32) * outputs[g].astype(jnp.float32)
         high = product.astype(jnp.bfloat16)
         low = (product - high.astype(jnp.float32)).astype(jnp.bfloat16)
         delta = (nt(ones, high) + nt(ones, low))[0:1, :]
-        lse_row = jnp.concatenate(
-            [lse[pl.ds(g * GROUP + h, 1), :] for h in range(GROUP)], axis=1
-        )
-        prob = jnp.exp(nt(k, q) * SCALE - lse_row)
-        ds = (prob * (nt(v, go) - delta)).astype(jnp.bfloat16)
-        dv = nn(prob.astype(jnp.bfloat16), go)
-        dk = nn(ds, q) * SCALE
+        p = prob[g]
+        ds = (p * (nt(values[g], go) - delta)).astype(jnp.bfloat16)
+        dv = nn(p.astype(jnp.bfloat16), go)
+        dk = nn(ds, queries[g]) * SCALE
         dscore[g] = ds
         own[pl.ds(0, tokens), cols] = dk[:tokens]
         own[pl.ds(tokens, tokens), cols] = dv[:tokens]
@@ -129,14 +151,10 @@
             far[i - 1][pl.ds(tokens, tokens), cols] = dv[part].astype(jnp.bfloat16)
 
 
-def query_kernel(dscore, key, *refs):
-    moved, out = refs[: STEPS - 1], refs[STEPS - 1]
-    tokens = key.shape[0]
-    kv_local = key.shape[1] // HEAD_DIM
-    for g in range(kv_local):
-        cols = pl.ds(g * HEAD_DIM, HEAD_DIM)
-        k = jnp.concatenate([key[:, cols]] + [m[pl.ds(0, tokens), cols] for m in moved], axis=0)
-        dq = (tn(dscore[g], k) * SCALE).astype(jnp.bfloat16)
+def query_kernel(dscore, keys, out):
+    tokens = out.shape[0]
+    for g in range(dscore.shape[0]):
+        dq = (tn(dscore[g], keys[g]) * SCALE).astype(jnp.bfloat16)
         for h in range(GROUP):
             out[:, pl.ds((g * GROUP + h) * HEAD_DIM, HEAD_DIM)] = dq[h * tokens : (h + 1) * tokens]
 
@@ -164,7 +182,7 @@
 
 
 def place_kernel(n, *refs):
-    parts, (dq, dk, dv, sems) = refs[:n], refs[n:]
+    parts, (dq, dk, dv, sems) = refs[:n][::-1], refs[n:]
     me = lax.axis_index("uly")
     width = dq.shape[1] // n
     kv_width = dk.shape[1] // n
@@ -197,39 +215,61 @@
     kv_width = key.shape[1]
     kv_local = kv_width // HEAD_DIM
     rows = grad.shape[0]
-    *sends, kv = pl.pallas_call(
+    key_rows, query_rows = STEPS * tokens, GROUP * tokens
+    query, output, lse, grad, key, value = (
+        pltpu.with_memory_space_constraint(a, pltpu.HBM)
+        for a in (query, output, lse, grad, key, value)
+    )
+    *slices, kv = pl.pallas_call(
         functools.partial(prep_kernel, n),
-        out_shape=[shape((rows, width))] * (n - 1) + [shape((2 * tokens, kv_width))],
-        in_specs=[ANY] * 3,
-        out_specs=[ANY] * n,
-        scratch_shapes=[pltpu.SemaphoreType.DMA((n + 1,))],
+        out_shape=[shape((rows, width))] * n + [shape((2 * tokens, kv_width))],
+        in_specs=[HBM] * 3,
+        out_specs=[ANY] * (n + 1),
+        scratch_shapes=[pltpu.SemaphoreType.DMA((n + 2,))],
         compiler_params=PARAMS,
         name="prep",
     )(grad, key, value)
-    received = [exchange(sends[step - 1], "uly", step) for step in range(1, n)]
+    received = [exchange(slices[step], "uly", step) for step in range(1, n)]
     moved = [shifted(kv, "blk", i) for i in range(1, STEPS)]
+    early = pl.pallas_call(
+        early_kernel,
+        out_shape=[
+            shape((kv_local, key_rows, query_rows), jnp.float32),
+            shape((kv_local, query_rows, HEAD_DIM)),
+            shape((kv_local, query_rows, HEAD_DIM)),
+            shape((kv_local, key_rows, HEAD_DIM)),
+            shape((kv_local, key_rows, HEAD_DIM)),
+        ],
+        in_specs=[HBM] * 5 + [VMEM] * (STEPS - 1),
+        out_specs=[VMEM] * 5,
+        scratch_shapes=[
+            pltpu.VMEM((tokens, width), jnp.bfloat16),
+            pltpu.VMEM((tokens, width), jnp.bfloat16),
+            pltpu.VMEM(lse.shape, jnp.float32),
+            pltpu.SemaphoreType.DMA((3 + 2 * kv_local,)),
+        ],
+        compiler_params=PARAMS,
+        name="early",
+    )(query, output, lse, key, value, *moved)
     *far, own, dscore = pl.pallas_call(
         functools.partial(main_kernel, n),
         out_shape=[shape((2 * tokens, kv_width))] * (STEPS - 1)
-        + [
-            shape((2 * tokens, kv_width), jnp.float32),
-            shape((kv_local, STEPS * tokens, GROUP * tokens)),
-        ],
-        in_specs=[VMEM] * (6 + STEPS - 1 + n - 1),
+        + [shape((2 * tokens, kv_width), jnp.float32), shape((kv_local, key_rows, query_rows))],
+        in_specs=[VMEM] * (6 + n - 1),
         out_specs=[VMEM] * (STEPS + 1),
-        scratch_shapes=[pltpu.VMEM((tokens, width), jnp.bfloat16)],
+        scratch_shapes=[pltpu.VMEM((kv_local, query_rows, HEAD_DIM), jnp.bfloat16)],
         compiler_params=PARAMS,
         name="main",
-    )(query, output, lse, grad, key, value, *moved, *received)
-    back = [shifted(far[i - 1], "blk", -i) for i in range(1, STEPS)]
+    )(*early, slices[0], *received[::-1])
+    back = [shifted(far[i - 1], "blk", -i) for i in range(STEPS - 1, 0, -1)]
     dq = pl.pallas_call(
         query_kernel,
         out_shape=shape((tokens, width)),
-        in_specs=[VMEM] * (STEPS + 1),
+        in_specs=[VMEM] * 2,
         out_specs=VMEM,
         compiler_params=PARAMS,
         name="query",
-    )(dscore, key, *moved)
+    )(dscore, early[3])
     parts = pl.pallas_call(
         functools.partial(sum_kernel, n),
         out_shape=[shape((rows, width + 2 * kv_width))] * n,
@@ -248,11 +288,11 @@
             shape((rows, kv_width * n)),
         ],
         in_specs=[ANY] * n,
-        out_specs=[ANY] * 3,
+        out_specs=[HBM] * 3,
         scratch_shapes=[pltpu.SemaphoreType.DMA((n, 3))],
         compiler_params=PARAMS,
         name="place",
-    )(*final)
+    )(*final[::-1])
 
 
 def solution(mesh):

time: 32.4 us -> 28.1 us (0.87)
  local copies, waits for them, and re-layouts: 3.35 us -> 0 us
  waiting for transfers between devices: 12.6 us -> 9.81 us
  Pallas kernels: 2.06 us -> 4.05 us
    unnamed x14 -> x0, local copies, waits for them, and re-layouts: 3.35 us -> none
    ppermute x6, waiting for transfers between devices: 8.94 us -> 7.12 us  [exchange(): return lax.ppermute(array, axis, pairs)]
    pallas_call x0 -> x1, Pallas kernels: none -> 1.34 us  [body(): pl.pallas_call(early_kernel, out_shape=[shape((kv_local, key_rows, query_...]
    ppermute x4, waiting for transfers between devices: 3.62 us -> 2.69 us  [shifted(): lax.ppermute(array, axis, [(i, (i + by) % size) for i in range(size)])]
    pallas_call x1, Pallas kernels: 0.2 us -> 0.93 us  [body(): pl.pallas_call(functools.partial(prep_kernel, n), out_shape=[shape((rows,...]
  transfers between devices with their start and end apart: 10 -> 10, of which waited for: 6 -> 5; matrix products, arithmetic and copies ran while one was open for 0% -> 0% of each run, Pallas kernels for 1% -> 6%
where the time goes in v2:
time: 28.1 us; the launch traced here: 27.9 us
  starting transfers between devices  13.4 us (48%)
  waiting for transfers between devices  9.81 us (35%)
  Pallas kernels  4.05 us (14%)
  between operations  0.68 us (2%)
    ppermute x6, starting transfers between devices, exchange(): return lax.ppermute(array, axis, pairs)  8.84 us
    ppermute x6, waiting for transfers between devices, exchange(): return lax.ppermute(array, axis, pairs)  7.12 us
    ppermute x4, starting transfers between devices, shifted(): lax.ppermute(array, axis, [(i, (i + by) % size) for i in range(size)])  4.53 us
    ppermute x4, waiting for transfers between devices, shifted(): lax.ppermute(array, axis, [(i, (i + by) % size) for i in range(size)])  2.69 us
    pallas_call x1, Pallas kernels, body(): pl.pallas_call(early_kernel, out_shape=[shape((kv_local, key_rows, query_...  1.34 us
    pallas_call x1, Pallas kernels, body(): pl.pallas_call(functools.partial(prep_kernel, n), out_shape=[shape((rows,...  0.93 us
    pallas_call x1, Pallas kernels, body(): pl.pallas_call(functools.partial(place_kernel, n), out_shape=[shape((rows...  0.79 us
    pallas_call x1, Pallas kernels, body(): pl.pallas_call(functools.partial(main_kernel, n), out_shape=[shape((2 * t...  0.65 us
  transfers between devices with their start and end apart: 10, of which 5 were waited for; matrix products, arithmetic and copies ran while one was open for 0% of the time, Pallas kernels for 6%

profile of v2, /device:TPU:0, one launch (start us, length us, event | category | flops | bytes accessed | tf_op | source)
XLA Modules:
  0.0 27.9 jit_solution(10181402591505872705)
XLA Ops:
  0.6 0.9 %prep.1 = (bf16[16,1280]{1,0:T(8,128)(2,1)S(1)}, bf16[16,1280]{1,0:T(8,128)(2,1)S(1)}, bf16[16,1280]{1,0:T(8,128)(2,1)S(1)}, bf16[16,1280]{1,0:T(8,128)(2,1)S(1)}, bf16[128,256]{1,0:T(8,128)(2,1)S(1)}) custom-call(bf16[16,5120]{1,0:T(8,128)(2,1)} %grad.1, bf16[64,256]{1,0:T(8,128)(2,1)} %key.3, bf16[64,256]{1,0:T(8,128)(2,1)} %value.3), custom_call_target="tpu_custom_call" | custom-call | tf_op jit(solution)/shard_map/prep/pallas_call | solution.py:223
  1.6 3.0 %collective-permute-start.1 = (bf16[128,256]{1,0:T(8,128)(2,1)S(1)}, bf16[128,256]{1,0:T(8,128)(2,1)S(1)}, u32[]{:S(2)}, u32[]{:S(2)}) collective-permute-start(bf16[128,256]{1,0:T(8,128)(2,1)S(1)} %get-tuple-element.21), channel_id=1, source_target_pairs={{0,8},{4,12},{8,16},{12,20},{16,24},{20,28},{24,0},{28,4},{1,9},{5... | collective-permute-start | bytes 196616 | tf_op jit(solution)/shard_map/ppermute | solution.py:25
  4.6 0.0 collective-permute-start
  4.6 3.6 %collective-permute-start.2 = (bf16[16,1280]{1,0:T(8,128)(2,1)S(1)}, bf16[16,1280]{1,0:T(8,128)(2,1)S(1)}, u32[]{:S(2)}, u32[]{:S(2)}) collective-permute-start(bf16[16,1280]{1,0:T(8,128)(2,1)S(1)} %get-tuple-element.28), channel_id=1, source_target_pairs={{0,3},{1,2},{2,1},{3,0},{4,7},{5,6},{6,5},{7,4},{8,11},{9,10},{10,... | collective-permute-start | bytes 122888 | tf_op jit(solution)/shard_map/ppermute | solution.py:44
  8.2 0.0 collective-permute-start.3
  8.2 0.8 %collective-permute-start.4 = (bf16[16,1280]{1,0:T(8,128)(2,1)S(1)}, bf16[16,1280]{1,0:T(8,128)(2,1)S(1)}, u32[]{:S(2)}, u32[]{:S(2)}) collective-permute-start(bf16[16,1280]{1,0:T(8,128)(2,1)S(1)} %get-tuple-element.30), channel_id=1, source_target_pairs={{0,1},{1,0},{2,3},{3,2},{4,5},{5,4},{6,7},{7,6},{8,9},{9,8},{10,11... | collective-permute-start | bytes 122888 | tf_op jit(solution)/shard_map/ppermute | solution.py:44
  9.0 0.0 collective-permute-done.1.refs_1_
  9.0 0.2 collective-permute-done.refs_0_
  9.2 1.3 %early.1 = (f32[2,192,320]{2,1,0:T(8,128)S(1)}, bf16[2,320,128]{2,1,0:T(8,128)(2,1)S(1)}, bf16[2,320,128]{2,1,0:T(8,128)(2,1)S(1)}, bf16[2,192,128]{2,1,0:T(8,128)(2,1)S(1)}, bf16[2,192,128]{2,1,0:T(8,128)(2,1)S(1)}) custom-call(bf16[64,1280]{1,0:T(8,128)(2,1)} %query.2, bf16[64,1280]{1,0:T(8,128)(2,1)} %output.1, f32[10,64]{1,0:T(8,128)} %lse.1, ...), custom_call_target="tpu_custom_call" | custom-call | tf_op jit(solution)/shard_map/early/pallas_call | solution.py:234
  10.5 0.0 collective-permute-done.2.refs_0_
  10.5 2.7 %collective-permute-done.3.refs_1_ = bf16[16,1280]{1,0:T(8,128)(2,1)S(1)} collective-permute-done((bf16[16,1280]{1,0:T(8,128)(2,1)S(1)}, bf16[16,1280]{1,0:T(8,128)(2,1)S(1)}, u32[]{:S(2)}, u32[]{:S(2)}) %collective-permute-start.3) | collective-permute-done | bytes 40992 | tf_op jit(solution)/shard_map/ppermute | solution.py:44
  13.2 0.7 %main.1 = (bf16[128,256]{1,0:T(8,128)(2,1)S(1)}, bf16[128,256]{1,0:T(8,128)(2,1)S(1)}, f32[128,256]{1,0:T(8,128)S(1)}, bf16[2,192,320]{2,1,0:T(8,128)(2,1)S(1)}) custom-call(f32[2,192,320]{2,1,0:T(8,128)S(1)} %get-tuple-element.22.prob, bf16[2,320,128]{2,1,0:T(8,128)(2,1)S(1)} %get-tuple-element.23.queries, ...), custom_call_target="tpu_custom_call" | custom-call | tf_op jit(solution)/shard_map/main/pallas_call | solution.py:254
  13.9 1.5 %collective-permute-start.5 = (bf16[128,256]{1,0:T(8,128)(2,1)S(1)}, bf16[128,256]{1,0:T(8,128)(2,1)S(1)}, u32[]{:S(2)}, u32[]{:S(2)}) collective-permute-start(bf16[128,256]{1,0:T(8,128)(2,1)S(1)} %get-tuple-element.33), channel_id=1, source_target_pairs={{0,24},{4,28},{8,0},{12,4},{16,8},{20,12},{24,16},{28,20},{1,25},{... | collective-permute-start | bytes 196616 | tf_op jit(solution)/shard_map/ppermute | solution.py:25
  15.4 0.0 collective-permute-start.6
  15.4 0.3 %query.3.dq = bf16[64,1280]{1,0:T(8,128)(2,1)S(1)} custom-call(bf16[2,192,320]{2,1,0:T(8,128)(2,1)S(1)} %get-tuple-element.31.dscore, bf16[2,192,128]{2,1,0:T(8,128)(2,1)S(1)} %get-tuple-element.25.keys), custom_call_target="tpu_custom_call" | custom-call | tf_op jit(solution)/shard_map/query/pallas_call | solution.py:265
  15.7 2.5 %collective-permute-done.5.refs_0_ = bf16[128,256]{1,0:T(8,128)(2,1)S(1)} collective-permute-done((bf16[128,256]{1,0:T(8,128)(2,1)S(1)}, bf16[128,256]{1,0:T(8,128)(2,1)S(1)}, u32[]{:S(2)}, u32[]{:S(2)}) %collective-permute-start.5) | collective-permute-done | bytes 65568 | tf_op jit(solution)/shard_map/ppermute | solution.py:25
  18.2 0.0 collective-permute-done.6.refs_1_
  18.3 2.1 %collective-permute-start.7 = (bf16[16,1792]{1,0:T(8,128)(2,1)S(1)}, bf16[16,1792]{1,0:T(8,128)(2,1)S(1)}, u32[]{:S(2)}, u32[]{:S(2)}) collective-permute-start(bf16[16,1792]{1,0:T(8,128)(2,1)S(1)} %get-tuple-element.35), channel_id=1, source_target_pairs={{0,3},{1,2},{2,1},{3,0},{4,7},{5,6},{6,5},{7,4},{8,11},{9,10},{10,... | collective-permute-start | bytes 172040 | tf_op jit(solution)/shard_map/ppermute | solution.py:44
  20.3 0.3 %collective-permute-start.8 = (bf16[16,1792]{1,0:T(8,128)(2,1)S(1)}, bf16[16,1792]{1,0:T(8,128)(2,1)S(1)}, u32[]{:S(2)}, u32[]{:S(2)}) collective-permute-start(bf16[16,1792]{1,0:T(8,128)(2,1)S(1)} %get-tuple-element.36), channel_id=1, source_target_pairs={{0,2},{1,3},{2,0},{3,1},{4,6},{5,7},{6,4},{7,5},{8,10},{9,11},{10,... | collective-permute-start | bytes 172040 | tf_op jit(solution)/shard_map/ppermute | solution.py:44
  20.6 2.1 %collective-permute-start.9 = (bf16[16,1792]{1,0:T(8,128)(2,1)S(1)}, bf16[16,1792]{1,0:T(8,128)(2,1)S(1)}, u32[]{:S(2)}, u32[]{:S(2)}) collective-permute-start(bf16[16,1792]{1,0:T(8,128)(2,1)S(1)} %get-tuple-element.37), channel_id=1, source_target_pairs={{0,1},{1,0},{2,3},{3,2},{4,5},{5,4},{6,7},{7,6},{8,9},{9,8},{10,11... | collective-permute-start | bytes 172040 | tf_op jit(solution)/shard_map/ppermute | solution.py:44
  22.7 2.2 %collective-permute-done.7.refs_0_ = bf16[16,1792]{1,0:T(8,128)(2,1)S(1)} collective-permute-done((bf16[16,1792]{1,0:T(8,128)(2,1)S(1)}, bf16[16,1792]{1,0:T(8,128)(2,1)S(1)}, u32[]{:S(2)}, u32[]{:S(2)}) %collective-permute-start.7) | collective-permute-done | bytes 57376 | tf_op jit(solution)/shard_map/ppermute | solution.py:44
  24.9 2.2 %collective-permute-done.8.refs_1_ = bf16[16,1792]{1,0:T(8,128)(2,1)S(1)} collective-permute-done((bf16[16,1792]{1,0:T(8,128)(2,1)S(1)}, bf16[16,1792]{1,0:T(8,128)(2,1)S(1)}, u32[]{:S(2)}, u32[]{:S(2)}) %collective-permute-start.8) | collective-permute-done | bytes 57376 | tf_op jit(solution)/shard_map/ppermute | solution.py:44
  27.1 0.0 collective-permute-done.9.refs_2_
  27.1 0.8 %place.1 = (bf16[16,5120]{1,0:T(8,128)(2,1)}, bf16[16,1024]{1,0:T(8,128)(2,1)}, bf16[16,1024]{1,0:T(8,128)(2,1)}) custom-call(bf16[16,1792]{1,0:T(8,128)(2,1)S(1)} %collective-permute-done.7.refs_0_, bf16[16,1792]{1,0:T(8,128)(2,1)S(1)} %collective-permute-done.8.refs_1_, bf16[16,1792]{1,0:T(8,128)(2,1)S(1)} %collective-permute-done.9.refs_2_, ...), custom_call_target="tpu_custom_call" | custom-call | tf_op jit(solution)/shard_map/place/pallas_call | solution.py:283
  (2 shorter events, 0.0 us)
Async XLA Ops:
  1.6 7.4 %collective-permute-start.1 = (bf16[128,256]{1,0:T(8,128)(2,1)S(1)}, bf16[128,256]{1,0:T(8,128)(2,1)S(1)}, u32[]{:S(2)}, u32[]{:S(2)}) collective-permute-start(bf16[128,256]{1,0:T(8,128)(2,1)S(1)} %get-tuple-element.21), channel_id=1, source_target_pairs={{0,8},{4,12},{8,16},{12,20},{16,24},{20,28},{24,0},{28,4},{1,9},{5... | collective-permute-start | bytes 196616 | tf_op jit(solution)/shard_map/ppermute | solution.py:25
  4.6 4.6 %collective-permute-start = (bf16[128,256]{1,0:T(8,128)(2,1)S(1)}, bf16[128,256]{1,0:T(8,128)(2,1)S(1)}, u32[]{:S(2)}, u32[]{:S(2)}) collective-permute-start(bf16[128,256]{1,0:T(8,128)(2,1)S(1)} %get-tuple-element.21), channel_id=1, source_target_pairs={{0,4},{4,8},{8,12},{12,16},{16,20},{20,24},{24,28},{28,0},{1,5},{5... | collective-permute-start | bytes 196616 | tf_op jit(solution)/shard_map/ppermute | solution.py:25
  4.6 5.9 %collective-permute-start.2 = (bf16[16,1280]{1,0:T(8,128)(2,1)S(1)}, bf16[16,1280]{1,0:T(8,128)(2,1)S(1)}, u32[]{:S(2)}, u32[]{:S(2)}) collective-permute-start(bf16[16,1280]{1,0:T(8,128)(2,1)S(1)} %get-tuple-element.28), channel_id=1, source_target_pairs={{0,3},{1,2},{2,1},{3,0},{4,7},{5,6},{6,5},{7,4},{8,11},{9,10},{10,... | collective-permute-start | bytes 122888 | tf_op jit(solution)/shard_map/ppermute | solution.py:44
  8.2 5.1 %collective-permute-start.3 = (bf16[16,1280]{1,0:T(8,128)(2,1)S(1)}, bf16[16,1280]{1,0:T(8,128)(2,1)S(1)}, u32[]{:S(2)}, u32[]{:S(2)}) collective-permute-start(bf16[16,1280]{1,0:T(8,128)(2,1)S(1)} %get-tuple-element.29), channel_id=1, source_target_pairs={{0,2},{1,3},{2,0},{3,1},{4,6},{5,7},{6,4},{7,5},{8,10},{9,11},{10,... | collective-permute-start | bytes 122888 | tf_op jit(solution)/shard_map/ppermute | solution.py:44
  8.2 5.1 %collective-permute-start.4 = (bf16[16,1280]{1,0:T(8,128)(2,1)S(1)}, bf16[16,1280]{1,0:T(8,128)(2,1)S(1)}, u32[]{:S(2)}, u32[]{:S(2)}) collective-permute-start(bf16[16,1280]{1,0:T(8,128)(2,1)S(1)} %get-tuple-element.30), channel_id=1, source_target_pairs={{0,1},{1,0},{2,3},{3,2},{4,5},{5,4},{6,7},{7,6},{8,9},{9,8},{10,11... | collective-permute-start | bytes 122888 | tf_op jit(solution)/shard_map/ppermute | solution.py:44
  13.9 4.3 %collective-permute-start.5 = (bf16[128,256]{1,0:T(8,128)(2,1)S(1)}, bf16[128,256]{1,0:T(8,128)(2,1)S(1)}, u32[]{:S(2)}, u32[]{:S(2)}) collective-permute-start(bf16[128,256]{1,0:T(8,128)(2,1)S(1)} %get-tuple-element.33), channel_id=1, source_target_pairs={{0,24},{4,28},{8,0},{12,4},{16,8},{20,12},{24,16},{28,20},{1,25},{... | collective-permute-start | bytes 196616 | tf_op jit(solution)/shard_map/ppermute | solution.py:25
  15.4 2.8 %collective-permute-start.6 = (bf16[128,256]{1,0:T(8,128)(2,1)S(1)}, bf16[128,256]{1,0:T(8,128)(2,1)S(1)}, u32[]{:S(2)}, u32[]{:S(2)}) collective-permute-start(bf16[128,256]{1,0:T(8,128)(2,1)S(1)} %get-tuple-element.34), channel_id=1, source_target_pairs={{0,28},{4,0},{8,4},{12,8},{16,12},{20,16},{24,20},{28,24},{1,29},{... | collective-permute-start | bytes 196616 | tf_op jit(solution)/shard_map/ppermute | solution.py:25
  18.3 6.7 %collective-permute-start.7 = (bf16[16,1792]{1,0:T(8,128)(2,1)S(1)}, bf16[16,1792]{1,0:T(8,128)(2,1)S(1)}, u32[]{:S(2)}, u32[]{:S(2)}) collective-permute-start(bf16[16,1792]{1,0:T(8,128)(2,1)S(1)} %get-tuple-element.35), channel_id=1, source_target_pairs={{0,3},{1,2},{2,1},{3,0},{4,7},{5,6},{6,5},{7,4},{8,11},{9,10},{10,... | collective-permute-start | bytes 172040 | tf_op jit(solution)/shard_map/ppermute | solution.py:44
  20.3 6.8 %collective-permute-start.8 = (bf16[16,1792]{1,0:T(8,128)(2,1)S(1)}, bf16[16,1792]{1,0:T(8,128)(2,1)S(1)}, u32[]{:S(2)}, u32[]{:S(2)}) collective-permute-start(bf16[16,1792]{1,0:T(8,128)(2,1)S(1)} %get-tuple-element.36), channel_id=1, source_target_pairs={{0,2},{1,3},{2,0},{3,1},{4,6},{5,7},{6,4},{7,5},{8,10},{9,11},{10,... | collective-permute-start | bytes 172040 | tf_op jit(solution)/shard_map/ppermute | solution.py:44
  20.6 6.5 %collective-permute-start.9 = (bf16[16,1792]{1,0:T(8,128)(2,1)S(1)}, bf16[16,1792]{1,0:T(8,128)(2,1)S(1)}, u32[]{:S(2)}, u32[]{:S(2)}) collective-permute-start(bf16[16,1792]{1,0:T(8,128)(2,1)S(1)} %get-tuple-element.37), channel_id=1, source_target_pairs={{0,1},{1,0},{2,3},{3,2},{4,5},{5,4},{6,7},{7,6},{8,9},{9,8},{10,11... | collective-permute-start | bytes 172040 | tf_op jit(solution)/shard_map/ppermute | solution.py:44

commit v3 on v2

--- a/solution.py
+++ b/solution.py
@@ -13,6 +13,7 @@
 STEPS = 3
 GROUP = QHEADS // KVHEADS
 SCALE = HEAD_DIM ** (-0.5)
+AHEAD = (2,)
 
 VMEM = pl.BlockSpec(memory_space=pltpu.VMEM)
 ANY = pl.BlockSpec(memory_space=pl.ANY)
@@ -151,12 +152,17 @@
             far[i - 1][pl.ds(tokens, tokens), cols] = dv[part].astype(jnp.bfloat16)
 
 
-def query_kernel(dscore, keys, out):
+def query_kernel(n, dscore, keys, out, *sends):
     tokens = out.shape[0]
+    rows = tokens // n
     for g in range(dscore.shape[0]):
         dq = (tn(dscore[g], keys[g]) * SCALE).astype(jnp.bfloat16)
         for h in range(GROUP):
             out[:, pl.ds((g * GROUP + h) * HEAD_DIM, HEAD_DIM)] = dq[h * tokens : (h + 1) * tokens]
+    me = lax.axis_index("uly")
+    for step, send in zip(AHEAD, sends):
+        start = pl.multiple_of(partner(me, step, n) * rows, rows)
+        send[...] = out[pl.ds(start, rows), :]
 
 
 def sum_kernel(n, dq, own, *refs):
@@ -174,29 +180,39 @@
     for step in range(n):
         to = partner(me, step, n) if step else me
         start = pl.multiple_of(to * rows, rows)
-        sends[step][:, pl.ds(0, width)] = dq[pl.ds(start, rows), :]
-        sends[step][:, pl.ds(width, kv_width)] = total[pl.ds(start, rows), :]
-        sends[step][:, pl.ds(width + kv_width, kv_width)] = total[
+        first = 0 if step in AHEAD else width
+        if first:
+            sends[step][:, pl.ds(0, width)] = dq[pl.ds(start, rows), :]
+        sends[step][:, pl.ds(first, kv_width)] = total[pl.ds(start, rows), :]
+        sends[step][:, pl.ds(first + kv_width, kv_width)] = total[
             pl.ds(pl.multiple_of(start + tokens, rows), rows), :
         ]
 
 
+def pack_kernel(part, *refs):
+    refs[-1][...] = part[...]
+
+
 def place_kernel(n, *refs):
-    parts, (dq, dk, dv, sems) = refs[:n][::-1], refs[n:]
+    parts, refs = refs[:n][::-1], refs[n:]
+    ahead, (dq, dk, dv, sems) = refs[: len(AHEAD)], refs[len(AHEAD) :]
     me = lax.axis_index("uly")
     width = dq.shape[1] // n
     kv_width = dk.shape[1] // n
     copies = []
     for step in range(n):
         source = partner(me, step, n, back=True) if step else me
-        part = parts[step]
-        for i, (out, first, size) in enumerate(
-            ((dq, 0, width), (dk, width, kv_width), (dv, width + kv_width, kv_width))
-        ):
+        first = 0 if step in AHEAD else width
+        pieces = (
+            (dk, parts[step], first, kv_width),
+            (dv, parts[step], first + kv_width, kv_width),
+            (dq, ahead[AHEAD.index(step)] if step in AHEAD else parts[step], 0, width),
+        )
+        for i, (out, part, at, size) in enumerate(pieces):
             columns = pl.ds(pl.multiple_of(source * size, size), size)
             copies.append(
                 pltpu.make_async_copy(
-                    part.at[:, pl.ds(first, size)], out.at[:, columns], sems.at[step, i]
+                    part.at[:, pl.ds(at, size)], out.at[:, columns], sems.at[step, i]
                 )
             )
     for copy in copies:
@@ -262,23 +278,35 @@
         name="main",
     )(*early, slices[0], *received[::-1])
     back = [shifted(far[i - 1], "blk", -i) for i in range(STEPS - 1, 0, -1)]
-    dq = pl.pallas_call(
-        query_kernel,
-        out_shape=shape((tokens, width)),
+    dq, *ahead = pl.pallas_call(
+        functools.partial(query_kernel, n),
+        out_shape=[shape((tokens, width))] + [shape((rows, width))] * len(AHEAD),
         in_specs=[VMEM] * 2,
-        out_specs=VMEM,
+        out_specs=[VMEM] * (1 + len(AHEAD)),
         compiler_params=PARAMS,
         name="query",
     )(dscore, early[3])
-    parts = pl.pallas_call(
+    ahead = [exchange(a, "uly", step) for a, step in zip(ahead, AHEAD)]
+    *parts, = pl.pallas_call(
         functools.partial(sum_kernel, n),
-        out_shape=[shape((rows, width + 2 * kv_width))] * n,
+        out_shape=[
+            shape((rows, 2 * kv_width + (0 if step in AHEAD else width))) for step in range(n)
+        ],
         in_specs=[VMEM] * (STEPS + 1),
         out_specs=[VMEM] * n,
         scratch_shapes=[pltpu.VMEM((2 * tokens, kv_width), jnp.bfloat16)],
         compiler_params=PARAMS,
         name="sum",
     )(dq, own, *back)
+    if AHEAD:
+        parts[AHEAD[-1]] = pl.pallas_call(
+            pack_kernel,
+            out_shape=shape(parts[AHEAD[-1]].shape),
+            in_specs=[VMEM] + [ANY] * len(AHEAD),
+            out_specs=VMEM,
+            compiler_params=PARAMS,
+            name="pack",
+        )(parts[AHEAD[-1]], *ahead)
     final = [parts[0]] + [exchange(parts[step], "uly", step) for step in range(1, n)]
     return pl.pallas_call(
         functools.partial(place_kernel, n),
@@ -287,12 +315,12 @@
             shape((rows, kv_width * n)),
             shape((rows, kv_width * n)),
         ],
-        in_specs=[ANY] * n,
+        in_specs=[ANY] * (n + len(AHEAD)),
         out_specs=[HBM] * 3,
         scratch_shapes=[pltpu.SemaphoreType.DMA((n, 3))],
         compiler_params=PARAMS,
         name="place",
-    )(*final[::-1])
+    )(*final[::-1], *ahead)
 
 
 def solution(mesh):

time: 28.1 us -> 27.1 us (0.964)
  waiting for transfers between devices: 9.81 us -> 6.36 us
  starting transfers between devices: 13.4 us -> 15.8 us
    ppermute x6 -> x7, starting transfers between devices: 8.84 us -> 11.3 us  [exchange(): return lax.ppermute(array, axis, pairs)]
    ppermute x4, waiting for transfers between devices: 2.69 us -> 0.45 us  [shifted(): lax.ppermute(array, axis, [(i, (i + by) % size) for i in range(size)])]
    ppermute x6 -> x7, waiting for transfers between devices: 7.12 us -> 5.91 us  [exchange(): return lax.ppermute(array, axis, pairs)]
  transfers between devices with their start and end apart: 10 -> 11, of which waited for: 5 -> 5; matrix products, arithmetic and copies ran while one was open for 0% -> 0% of each run, Pallas kernels for 6% -> 6%
where the time goes in v3:
time: 27.1 us; the launch traced here: 26.9 us
  starting transfers between devices  15.8 us (58%)
  waiting for transfers between devices  6.36 us (23%)
  Pallas kernels  4.05 us (15%)
  between operations  0.68 us (3%)
    ppermute x7, starting transfers between devices, exchange(): return lax.ppermute(array, axis, pairs)  11.3 us
    ppermute x7, waiting for transfers between devices, exchange(): return lax.ppermute(array, axis, pairs)  5.91 us
    ppermute x4, starting transfers between devices, shifted(): lax.ppermute(array, axis, [(i, (i + by) % size) for i in range(size)])  4.53 us
    pallas_call x1, Pallas kernels, body(): pl.pallas_call(early_kernel, out_shape=[shape((kv_local, key_rows, query_...  1.34 us
    pallas_call x1, Pallas kernels, body(): pl.pallas_call(functools.partial(prep_kernel, n), out_shape=[shape((rows,...  0.93 us
    pallas_call x1, Pallas kernels, body(): pl.pallas_call(functools.partial(place_kernel, n), out_shape=[shape((rows...  0.79 us
    pallas_call x1, Pallas kernels, body(): pl.pallas_call(functools.partial(main_kernel, n), out_shape=[shape((2 * t...  0.65 us
  transfers between devices with their start and end apart: 11, of which 5 were waited for; matrix products, arithmetic and copies ran while one was open for 0% of the time, Pallas kernels for 6%

profile of v3, /device:TPU:0, one launch (start us, length us, event | category | flops | bytes accessed | tf_op | source)
XLA Modules:
  0.0 26.9 jit_solution(3372216405583067908)
XLA Ops:
  0.6 0.9 %prep.1 = (bf16[16,1280]{1,0:T(8,128)(2,1)S(1)}, bf16[16,1280]{1,0:T(8,128)(2,1)S(1)}, bf16[16,1280]{1,0:T(8,128)(2,1)S(1)}, bf16[16,1280]{1,0:T(8,128)(2,1)S(1)}, bf16[128,256]{1,0:T(8,128)(2,1)S(1)}) custom-call(bf16[16,5120]{1,0:T(8,128)(2,1)} %grad.1, bf16[64,256]{1,0:T(8,128)(2,1)} %key.3, bf16[64,256]{1,0:T(8,128)(2,1)} %value.3), custom_call_target="tpu_custom_call" | custom-call | tf_op jit(solution)/shard_map/prep/pallas_call | solution.py:239
  1.6 3.0 %collective-permute-start.1 = (bf16[128,256]{1,0:T(8,128)(2,1)S(1)}, bf16[128,256]{1,0:T(8,128)(2,1)S(1)}, u32[]{:S(2)}, u32[]{:S(2)}) collective-permute-start(bf16[128,256]{1,0:T(8,128)(2,1)S(1)} %get-tuple-element.23), channel_id=1, source_target_pairs={{0,8},{4,12},{8,16},{12,20},{16,24},{20,28},{24,0},{28,4},{1,9},{5... | collective-permute-start | bytes 196616 | tf_op jit(solution)/shard_map/ppermute | solution.py:26
  4.6 0.0 collective-permute-start
  4.6 3.6 %collective-permute-start.2 = (bf16[16,1280]{1,0:T(8,128)(2,1)S(1)}, bf16[16,1280]{1,0:T(8,128)(2,1)S(1)}, u32[]{:S(2)}, u32[]{:S(2)}) collective-permute-start(bf16[16,1280]{1,0:T(8,128)(2,1)S(1)} %get-tuple-element.30), channel_id=1, source_target_pairs={{0,3},{1,2},{2,1},{3,0},{4,7},{5,6},{6,5},{7,4},{8,11},{9,10},{10,... | collective-permute-start | bytes 122888 | tf_op jit(solution)/shard_map/ppermute | solution.py:45
  8.2 0.0 collective-permute-start.3
  8.2 0.8 %collective-permute-start.4 = (bf16[16,1280]{1,0:T(8,128)(2,1)S(1)}, bf16[16,1280]{1,0:T(8,128)(2,1)S(1)}, u32[]{:S(2)}, u32[]{:S(2)}) collective-permute-start(bf16[16,1280]{1,0:T(8,128)(2,1)S(1)} %get-tuple-element.32), channel_id=1, source_target_pairs={{0,1},{1,0},{2,3},{3,2},{4,5},{5,4},{6,7},{7,6},{8,9},{9,8},{10,11... | collective-permute-start | bytes 122888 | tf_op jit(solution)/shard_map/ppermute | solution.py:45
  9.0 0.0 collective-permute-done.1.refs_1_
  9.0 0.2 collective-permute-done.refs_0_
  9.2 1.3 %early.1 = (f32[2,192,320]{2,1,0:T(8,128)S(1)}, bf16[2,320,128]{2,1,0:T(8,128)(2,1)S(1)}, bf16[2,320,128]{2,1,0:T(8,128)(2,1)S(1)}, bf16[2,192,128]{2,1,0:T(8,128)(2,1)S(1)}, bf16[2,192,128]{2,1,0:T(8,128)(2,1)S(1)}) custom-call(bf16[64,1280]{1,0:T(8,128)(2,1)} %query.2, bf16[64,1280]{1,0:T(8,128)(2,1)} %output.1, f32[10,64]{1,0:T(8,128)} %lse.1, ...), custom_call_target="tpu_custom_call" | custom-call | tf_op jit(solution)/shard_map/early/pallas_call | solution.py:250
  10.5 0.0 collective-permute-done.2.refs_0_
  10.5 2.7 %collective-permute-done.3.refs_1_ = bf16[16,1280]{1,0:T(8,128)(2,1)S(1)} collective-permute-done((bf16[16,1280]{1,0:T(8,128)(2,1)S(1)}, bf16[16,1280]{1,0:T(8,128)(2,1)S(1)}, u32[]{:S(2)}, u32[]{:S(2)}) %collective-permute-start.3) | collective-permute-done | bytes 40992 | tf_op jit(solution)/shard_map/ppermute | solution.py:45
  13.2 0.0 collective-permute-done.4.refs_2_
  13.2 0.7 %main.1 = (bf16[128,256]{1,0:T(8,128)(2,1)S(1)}, bf16[128,256]{1,0:T(8,128)(2,1)S(1)}, f32[128,256]{1,0:T(8,128)S(1)}, bf16[2,192,320]{2,1,0:T(8,128)(2,1)S(1)}) custom-call(f32[2,192,320]{2,1,0:T(8,128)S(1)} %get-tuple-element.24.prob, bf16[2,320,128]{2,1,0:T(8,128)(2,1)S(1)} %get-tuple-element.25.queries, ...), custom_call_target="tpu_custom_call" | custom-call | tf_op jit(solution)/shard_map/main/pallas_call | solution.py:270
  13.9 1.5 %collective-permute-start.5 = (bf16[128,256]{1,0:T(8,128)(2,1)S(1)}, bf16[128,256]{1,0:T(8,128)(2,1)S(1)}, u32[]{:S(2)}, u32[]{:S(2)}) collective-permute-start(bf16[128,256]{1,0:T(8,128)(2,1)S(1)} %get-tuple-element.36), channel_id=1, source_target_pairs={{0,24},{4,28},{8,0},{12,4},{16,8},{20,12},{24,16},{28,20},{1,25},{... | collective-permute-start | bytes 196616 | tf_op jit(solution)/shard_map/ppermute | solution.py:26
  15.4 0.0 collective-permute-start.6
  15.4 0.3 %query.3 = (bf16[64,1280]{1,0:T(8,128)(2,1)S(1)}, bf16[16,1280]{1,0:T(8,128)(2,1)S(1)}) custom-call(bf16[2,192,320]{2,1,0:T(8,128)(2,1)S(1)} %get-tuple-element.33.dscore, bf16[2,192,128]{2,1,0:T(8,128)(2,1)S(1)} %get-tuple-element.27.keys), custom_call_target="tpu_custom_call" | custom-call | tf_op jit(solution)/shard_map/query/pallas_call | solution.py:281
  15.7 2.2 %collective-permute-start.8 = (bf16[16,1280]{1,0:T(8,128)(2,1)S(1)}, bf16[16,1280]{1,0:T(8,128)(2,1)S(1)}, u32[]{:S(2)}, u32[]{:S(2)}) collective-permute-start(bf16[16,1280]{1,0:T(8,128)(2,1)S(1)} %get-tuple-element.40), channel_id=1, source_target_pairs={{0,2},{1,3},{2,0},{3,1},{4,6},{5,7},{6,4},{7,5},{8,10},{9,11},{10,... | collective-permute-start | bytes 122888 | tf_op jit(solution)/shard_map/ppermute | solution.py:45
  18.0 0.2 collective-permute-done.5.refs_0_
  18.3 2.1 %collective-permute-start.7 = (bf16[16,1792]{1,0:T(8,128)(2,1)S(1)}, bf16[16,1792]{1,0:T(8,128)(2,1)S(1)}, u32[]{:S(2)}, u32[]{:S(2)}) collective-permute-start(bf16[16,1792]{1,0:T(8,128)(2,1)S(1)} %get-tuple-element.38), channel_id=1, source_target_pairs={{0,3},{1,2},{2,1},{3,0},{4,7},{5,6},{6,5},{7,4},{8,11},{9,10},{10,... | collective-permute-start | bytes 172040 | tf_op jit(solution)/shard_map/ppermute | solution.py:45
  20.3 0.8 %collective-permute-start.10 = (bf16[16,1792]{1,0:T(8,128)(2,1)S(1)}, bf16[16,1792]{1,0:T(8,128)(2,1)S(1)}, u32[]{:S(2)}, u32[]{:S(2)}) collective-permute-start(bf16[16,1792]{1,0:T(8,128)(2,1)S(1)} %get-tuple-element.41), channel_id=1, source_target_pairs={{0,1},{1,0},{2,3},{3,2},{4,5},{5,4},{6,7},{7,6},{8,9},{9,8},{10,11... | collective-permute-start | bytes 172040 | tf_op jit(solution)/shard_map/ppermute | solution.py:45
  21.1 1.8 %collective-permute-start.9 = (bf16[16,512]{1,0:T(8,128)(2,1)S(1)}, bf16[16,512]{1,0:T(8,128)(2,1)S(1)}, u32[]{:S(2)}, u32[]{:S(2)}) collective-permute-start(bf16[16,512]{1,0:T(8,128)(2,1)S(1)} %pack.1), channel_id=1, source_target_pairs={{0,2},{1,3},{2,0},{3,1},{4,6},{5,7},{6,4},{7,5},{8,10},{9,11},{10,... | collective-permute-start | bytes 49160 | tf_op jit(solution)/shard_map/ppermute | solution.py:45
  22.9 2.9 %collective-permute-done.9.refs_1_ = bf16[16,512]{1,0:T(8,128)(2,1)S(1)} collective-permute-done((bf16[16,512]{1,0:T(8,128)(2,1)S(1)}, bf16[16,512]{1,0:T(8,128)(2,1)S(1)}, u32[]{:S(2)}, u32[]{:S(2)}) %collective-permute-start.9) | collective-permute-done | bytes 16416 | tf_op jit(solution)/shard_map/ppermute | solution.py:45
  25.9 0.2 collective-permute-done.10.refs_2_
  26.1 0.8 %place.1 = (bf16[16,5120]{1,0:T(8,128)(2,1)}, bf16[16,1024]{1,0:T(8,128)(2,1)}, bf16[16,1024]{1,0:T(8,128)(2,1)}) custom-call(bf16[16,1792]{1,0:T(8,128)(2,1)S(1)} %collective-permute-done.7.refs_0_, bf16[16,512]{1,0:T(8,128)(2,1)S(1)} %collective-permute-done.9.refs_1_, bf16[16,1792]{1,0:T(8,128)(2,1)S(1)} %collective-permute-done.10.refs_2_, ...), custom_call_target="tpu_custom_call" | custom-call | tf_op jit(solution)/shard_map/place/pallas_call | solution.py:311
  (5 shorter events, 0.0 us)
Async XLA Ops:
  1.6 7.4 %collective-permute-start.1 = (bf16[128,256]{1,0:T(8,128)(2,1)S(1)}, bf16[128,256]{1,0:T(8,128)(2,1)S(1)}, u32[]{:S(2)}, u32[]{:S(2)}) collective-permute-start(bf16[128,256]{1,0:T(8,128)(2,1)S(1)} %get-tuple-element.23), channel_id=1, source_target_pairs={{0,8},{4,12},{8,16},{12,20},{16,24},{20,28},{24,0},{28,4},{1,9},{5... | collective-permute-start | bytes 196616 | tf_op jit(solution)/shard_map/ppermute | solution.py:26
  4.6 4.6 %collective-permute-start = (bf16[128,256]{1,0:T(8,128)(2,1)S(1)}, bf16[128,256]{1,0:T(8,128)(2,1)S(1)}, u32[]{:S(2)}, u32[]{:S(2)}) collective-permute-start(bf16[128,256]{1,0:T(8,128)(2,1)S(1)} %get-tuple-element.23), channel_id=1, source_target_pairs={{0,4},{4,8},{8,12},{12,16},{16,20},{20,24},{24,28},{28,0},{1,5},{5... | collective-permute-start | bytes 196616 | tf_op jit(solution)/shard_map/ppermute | solution.py:26
  4.6 5.9 %collective-permute-start.2 = (bf16[16,1280]{1,0:T(8,128)(2,1)S(1)}, bf16[16,1280]{1,0:T(8,128)(2,1)S(1)}, u32[]{:S(2)}, u32[]{:S(2)}) collective-permute-start(bf16[16,1280]{1,0:T(8,128)(2,1)S(1)} %get-tuple-element.30), channel_id=1, source_target_pairs={{0,3},{1,2},{2,1},{3,0},{4,7},{5,6},{6,5},{7,4},{8,11},{9,10},{10,... | collective-permute-start | bytes 122888 | tf_op jit(solution)/shard_map/ppermute | solution.py:45
  8.2 5.1 %collective-permute-start.3 = (bf16[16,1280]{1,0:T(8,128)(2,1)S(1)}, bf16[16,1280]{1,0:T(8,128)(2,1)S(1)}, u32[]{:S(2)}, u32[]{:S(2)}) collective-permute-start(bf16[16,1280]{1,0:T(8,128)(2,1)S(1)} %get-tuple-element.31), channel_id=1, source_target_pairs={{0,2},{1,3},{2,0},{3,1},{4,6},{5,7},{6,4},{7,5},{8,10},{9,11},{10,... | collective-permute-start | bytes 122888 | tf_op jit(solution)/shard_map/ppermute | solution.py:45
  8.2 5.1 %collective-permute-start.4 = (bf16[16,1280]{1,0:T(8,128)(2,1)S(1)}, bf16[16,1280]{1,0:T(8,128)(2,1)S(1)}, u32[]{:S(2)}, u32[]{:S(2)}) collective-permute-start(bf16[16,1280]{1,0:T(8,128)(2,1)S(1)} %get-tuple-element.32), channel_id=1, source_target_pairs={{0,1},{1,0},{2,3},{3,2},{4,5},{5,4},{6,7},{7,6},{8,9},{9,8},{10,11... | collective-permute-start | bytes 122888 | tf_op jit(solution)/shard_map/ppermute | solution.py:45
  13.9 4.3 %collective-permute-start.5 = (bf16[128,256]{1,0:T(8,128)(2,1)S(1)}, bf16[128,256]{1,0:T(8,128)(2,1)S(1)}, u32[]{:S(2)}, u32[]{:S(2)}) collective-permute-start(bf16[128,256]{1,0:T(8,128)(2,1)S(1)} %get-tuple-element.36), channel_id=1, source_target_pairs={{0,24},{4,28},{8,0},{12,4},{16,8},{20,12},{24,16},{28,20},{1,25},{... | collective-permute-start | bytes 196616 | tf_op jit(solution)/shard_map/ppermute | solution.py:26
  15.4 2.8 %collective-permute-start.6 = (bf16[128,256]{1,0:T(8,128)(2,1)S(1)}, bf16[128,256]{1,0:T(8,128)(2,1)S(1)}, u32[]{:S(2)}, u32[]{:S(2)}) collective-permute-start(bf16[128,256]{1,0:T(8,128)(2,1)S(1)} %get-tuple-element.37), channel_id=1, source_target_pairs={{0,28},{4,0},{8,4},{12,8},{16,12},{20,16},{24,20},{28,24},{1,29},{... | collective-permute-start | bytes 196616 | tf_op jit(solution)/shard_map/ppermute | solution.py:26
  15.7 5.4 %collective-permute-start.8 = (bf16[16,1280]{1,0:T(8,128)(2,1)S(1)}, bf16[16,1280]{1,0:T(8,128)(2,1)S(1)}, u32[]{:S(2)}, u32[]{:S(2)}) collective-permute-start(bf16[16,1280]{1,0:T(8,128)(2,1)S(1)} %get-tuple-element.40), channel_id=1, source_target_pairs={{0,2},{1,3},{2,0},{3,1},{4,6},{5,7},{6,4},{7,5},{8,10},{9,11},{10,... | collective-permute-start | bytes 122888 | tf_op jit(solution)/shard_map/ppermute | solution.py:45
  18.3 7.6 %collective-permute-start.7 = (bf16[16,1792]{1,0:T(8,128)(2,1)S(1)}, bf16[16,1792]{1,0:T(8,128)(2,1)S(1)}, u32[]{:S(2)}, u32[]{:S(2)}) collective-permute-start(bf16[16,1792]{1,0:T(8,128)(2,1)S(1)} %get-tuple-element.38), channel_id=1, source_target_pairs={{0,3},{1,2},{2,1},{3,0},{4,7},{5,6},{6,5},{7,4},{8,11},{9,10},{10,... | collective-permute-start | bytes 172040 | tf_op jit(solution)/shard_map/ppermute | solution.py:45
  20.3 5.8 %collective-permute-start.10 = (bf16[16,1792]{1,0:T(8,128)(2,1)S(1)}, bf16[16,1792]{1,0:T(8,128)(2,1)S(1)}, u32[]{:S(2)}, u32[]{:S(2)}) collective-permute-start(bf16[16,1792]{1,0:T(8,128)(2,1)S(1)} %get-tuple-element.41), channel_id=1, source_target_pairs={{0,1},{1,0},{2,3},{3,2},{4,5},{5,4},{6,7},{7,6},{8,9},{9,8},{10,11... | collective-permute-start | bytes 172040 | tf_op jit(solution)/shard_map/ppermute | solution.py:45
  21.1 4.8 %collective-permute-start.9 = (bf16[16,512]{1,0:T(8,128)(2,1)S(1)}, bf16[16,512]{1,0:T(8,128)(2,1)S(1)}, u32[]{:S(2)}, u32[]{:S(2)}) collective-permute-start(bf16[16,512]{1,0:T(8,128)(2,1)S(1)} %pack.1), channel_id=1, source_target_pairs={{0,2},{1,3},{2,0},{3,1},{4,6},{5,7},{6,4},{7,5},{8,10},{9,11},{10,... | collective-permute-start | bytes 49160 | tf_op jit(solution)/shard_map/ppermute | solution.py:45

commit v4 on v3

--- a/solution.py
+++ b/solution.py
@@ -76,8 +76,9 @@
         copy.wait()
 
 
-def early_kernel(query, output, lse, key, value, *refs):
-    moved, refs = refs[: STEPS - 1], refs[STEPS - 1 :]
+def early_kernel(query, output, lse, key, value, even_key, first_odd, *refs):
+    moved, refs = refs[: STEPS - 2], refs[STEPS - 2 :]
+    odd = lax.rem(lax.axis_index("blk"), 2) == 1
     prob, queries, outputs, keys, values, query_in, output_in, lse_in, sems = refs
     tokens = key.shape[0]
     kv_local = key.shape[1] // HEAD_DIM
@@ -95,10 +96,21 @@
         copy.start()
     for g in range(kv_local):
         cols = pl.ds(g * HEAD_DIM, HEAD_DIM)
-        for i in range(1, STEPS):
+        part = pl.ds(tokens, tokens)
+
+        @pl.when(odd)
+        def _():
+            keys[g, part] = first_odd[pl.ds(0, tokens), cols]
+            values[g, part] = first_odd[pl.ds(tokens, tokens), cols]
+
+        @pl.when(jnp.logical_not(odd))
+        def _():
+            keys[g, part] = even_key[:, cols]
+
+        for i in range(2, STEPS):
             part = pl.ds(i * tokens, tokens)
-            keys[g, part] = moved[i - 1][pl.ds(0, tokens), cols]
-            values[g, part] = moved[i - 1][pl.ds(tokens, tokens), cols]
+            keys[g, part] = moved[i - 2][pl.ds(0, tokens), cols]
+            values[g, part] = moved[i - 2][pl.ds(tokens, tokens), cols]
     for copy in copies:
         copy.wait()
     for g in range(kv_local):
@@ -113,7 +125,13 @@
         prob[g] = jnp.exp(nt(keys[g], queries[g]) * SCALE - lse_row)
 
 
-def main_kernel(n, prob, queries, outputs, keys, values, mine, *refs):
+def halves_kernel(pair, first, second):
+    rows = first.shape[0]
+    first[...] = pair[pl.ds(0, rows), :]
+    second[...] = pair[pl.ds(rows, rows), :]
+
+
+def main_kernel(n, prob, queries, outputs, keys, values, mine, even_value, *refs):
     received = refs[: n - 1][::-1]
     rest = refs[n - 1 :]
     far = rest[: STEPS - 1]
@@ -132,15 +150,26 @@
                     :, pl.ds((g * GROUP + h) * HEAD_DIM, HEAD_DIM)
                 ]
     ones = jnp.ones((8, HEAD_DIM), jnp.bfloat16)
+    odd = lax.rem(lax.axis_index("blk"), 2) == 1
     for g in range(kv_local):
         cols = pl.ds(g * HEAD_DIM, HEAD_DIM)
+
+        near = pl.ds(tokens, tokens)
+        v = jnp.concatenate(
+            [
+                values[g, pl.ds(0, tokens)],
+                jnp.where(odd, values[g, near], even_value[:, cols]),
+                values[g, pl.ds(2 * tokens, (STEPS - 2) * tokens)],
+            ],
+            axis=0,
+        )
         go = stacked[g]
         product = go.astype(jnp.float32) * outputs[g].astype(jnp.float32)
         high = product.astype(jnp.bfloat16)
         low = (product - high.astype(jnp.float32)).astype(jnp.bfloat16)
         delta = (nt(ones, high) + nt(ones, low))[0:1, :]
         p = prob[g]
-        ds = (p * (nt(values[g], go) - delta)).astype(jnp.bfloat16)
+        ds = (p * (nt(v, go) - delta)).astype(jnp.bfloat16)
         dv = nn(p.astype(jnp.bfloat16), go)
         dk = nn(ds, queries[g]) * SCALE
         dscore[g] = ds
@@ -246,7 +275,18 @@
         name="prep",
     )(grad, key, value)
     received = [exchange(slices[step], "uly", step) for step in range(1, n)]
-    moved = [shifted(kv, "blk", i) for i in range(1, STEPS)]
+    moved = [shifted(kv, "blk", i) for i in range(2, STEPS)]
+    swap = [(i, i ^ 1) for i in range(lax.axis_size("blk"))]
+    first_odd = lax.ppermute(kv, "blk", swap)
+    passed = pl.pallas_call(
+        halves_kernel,
+        out_shape=[shape((tokens, kv_width))] * 2,
+        in_specs=[VMEM],
+        out_specs=[VMEM] * 2,
+        compiler_params=PARAMS,
+        name="halves",
+    )(moved[0])
+    even_key, even_value = [lax.ppermute(a, "blk", swap) for a in passed]
     early = pl.pallas_call(
         early_kernel,
         out_shape=[
@@ -256,7 +296,7 @@
             shape((kv_local, key_rows, HEAD_DIM)),
             shape((kv_local, key_rows, HEAD_DIM)),
         ],
-        in_specs=[HBM] * 5 + [VMEM] * (STEPS - 1),
+        in_specs=[HBM] * 5 + [VMEM] * STEPS,
         out_specs=[VMEM] * 5,
         scratch_shapes=[
             pltpu.VMEM((tokens, width), jnp.bfloat16),
@@ -266,17 +306,17 @@
         ],
         compiler_params=PARAMS,
         name="early",
-    )(query, output, lse, key, value, *moved)
+    )(query, output, lse, key, value, even_key, first_odd, *moved)
     *far, own, dscore = pl.pallas_call(
         functools.partial(main_kernel, n),
         out_shape=[shape((2 * tokens, kv_width))] * (STEPS - 1)
         + [shape((2 * tokens, kv_width), jnp.float32), shape((kv_local, key_rows, query_rows))],
-        in_specs=[VMEM] * (6 + n - 1),
+        in_specs=[VMEM] * (7 + n - 1),
         out_specs=[VMEM] * (STEPS + 1),
         scratch_shapes=[pltpu.VMEM((kv_local, query_rows, HEAD_DIM), jnp.bfloat16)],
         compiler_params=PARAMS,
         name="main",
-    )(*early, slices[0], *received[::-1])
+    )(*early, slices[0], even_value, *received[::-1])
     back = [shifted(far[i - 1], "blk", -i) for i in range(STEPS - 1, 0, -1)]
     dq, *ahead = pl.pallas_call(
         functools.partial(query_kernel, n),

time: 27.1 us -> 26.9 us (level)
  waiting for transfers between devices: 6.36 us -> 6.08 us
    ppermute x7, waiting for transfers between devices: 5.91 us -> 4.96 us  [exchange(): return lax.ppermute(array, axis, pairs)]
    ppermute x7, starting transfers between devices: 11.3 us -> 10.6 us  [exchange(): return lax.ppermute(array, axis, pairs)]
    ppermute x0 -> x3, waiting for transfers between devices: none -> 0.7 us  [the longest x2 0.7 us: body(): even_key, even_value = [lax.ppermute(a, 'blk', swap) for a in passed]]
    ppermute x0 -> x3, starting transfers between devices: none -> 0.56 us  [the longest x2 0.56 us: body(): even_key, even_value = [lax.ppermute(a, 'blk', swap) for a in passed]]
    ppermute x4 -> x3, starting transfers between devices: 4.53 us -> 4.7 us  [shifted(): lax.ppermute(array, axis, [(i, (i + by) % size) for i in range(size)])]
  transfers between devices with their start and end apart: 11 -> 13, of which waited for: 5 -> 6; matrix products, arithmetic and copies ran while one was open for 0% -> 0% of each run, Pallas kernels for 6% -> 6%
where the time goes in v4:
time: 26.9 us; the launch traced here: 26.7 us
  starting transfers between devices  15.8 us (59%)
  waiting for transfers between devices  6.08 us (23%)
  Pallas kernels  4.06 us (15%)
  between operations  0.7 us (3%)
    ppermute x7, starting transfers between devices, exchange(): return lax.ppermute(array, axis, pairs)  10.6 us
    ppermute x7, waiting for transfers between devices, exchange(): return lax.ppermute(array, axis, pairs)  4.96 us
    ppermute x3, starting transfers between devices, shifted(): lax.ppermute(array, axis, [(i, (i + by) % size) for i in range(size)])  4.7 us
    pallas_call x1, Pallas kernels, body(): pl.pallas_call(early_kernel, out_shape=[shape((kv_local, key_rows, query_...  1.34 us
    pallas_call x1, Pallas kernels, body(): pl.pallas_call(functools.partial(prep_kernel, n), out_shape=[shape((rows,...  0.93 us
    pallas_call x1, Pallas kernels, body(): pl.pallas_call(functools.partial(place_kernel, n), out_shape=[shape((rows...  0.79 us
    ppermute x2, waiting for transfers between devices, body(): even_key, even_value = [lax.ppermute(a, 'blk', swap) for a in passed]  0.7 us
    pallas_call x1, Pallas kernels, body(): pl.pallas_call(functools.partial(main_kernel, n), out_shape=[shape((2 * t...  0.65 us
  transfers between devices with their start and end apart: 13, of which 6 were waited for; matrix products, arithmetic and copies ran while one was open for 0% of the time, Pallas kernels for 6%

profile of v4, /device:TPU:0, one launch (start us, length us, event | category | flops | bytes accessed | tf_op | source)
XLA Modules:
  0.0 26.7 jit_solution(4386975523575897892)
XLA Ops:
  0.6 0.9 %prep.1 = (bf16[16,1280]{1,0:T(8,128)(2,1)S(1)}, bf16[16,1280]{1,0:T(8,128)(2,1)S(1)}, bf16[16,1280]{1,0:T(8,128)(2,1)S(1)}, bf16[16,1280]{1,0:T(8,128)(2,1)S(1)}, bf16[128,256]{1,0:T(8,128)(2,1)S(1)}) custom-call(bf16[16,5120]{1,0:T(8,128)(2,1)} %grad.1, bf16[64,256]{1,0:T(8,128)(2,1)} %key.3, bf16[64,256]{1,0:T(8,128)(2,1)} %value.3), custom_call_target="tpu_custom_call" | custom-call | tf_op jit(solution)/shard_map/prep/pallas_call | solution.py:268
  1.6 3.0 %collective-permute-start = (bf16[128,256]{1,0:T(8,128)(2,1)S(1)}, bf16[128,256]{1,0:T(8,128)(2,1)S(1)}, u32[]{:S(2)}, u32[]{:S(2)}) collective-permute-start(bf16[128,256]{1,0:T(8,128)(2,1)S(1)} %get-tuple-element.25), channel_id=1, source_target_pairs={{0,8},{4,12},{8,16},{12,20},{16,24},{20,28},{24,0},{28,4},{1,9},{5... | collective-permute-start | bytes 196616 | tf_op jit(solution)/shard_map/ppermute | solution.py:26
  4.6 0.0 collective-permute-start.2
  4.6 3.6 %collective-permute-start.4 = (bf16[16,1280]{1,0:T(8,128)(2,1)S(1)}, bf16[16,1280]{1,0:T(8,128)(2,1)S(1)}, u32[]{:S(2)}, u32[]{:S(2)}) collective-permute-start(bf16[16,1280]{1,0:T(8,128)(2,1)S(1)} %get-tuple-element.34), channel_id=1, source_target_pairs={{0,3},{1,2},{2,1},{3,0},{4,7},{5,6},{6,5},{7,4},{8,11},{9,10},{10,... | collective-permute-start | bytes 122888 | tf_op jit(solution)/shard_map/ppermute | solution.py:45
  8.2 0.8 %collective-permute-start.6 = (bf16[16,1280]{1,0:T(8,128)(2,1)S(1)}, bf16[16,1280]{1,0:T(8,128)(2,1)S(1)}, u32[]{:S(2)}, u32[]{:S(2)}) collective-permute-start(bf16[16,1280]{1,0:T(8,128)(2,1)S(1)} %get-tuple-element.36), channel_id=1, source_target_pairs={{0,1},{1,0},{2,3},{3,2},{4,5},{5,4},{6,7},{7,6},{8,9},{9,8},{10,11... | collective-permute-start | bytes 122888 | tf_op jit(solution)/shard_map/ppermute | solution.py:45
  9.0 0.0 collective-permute-done.pair.refs_0_
  9.0 0.1 collective-permute-start.1
  9.1 0.5 %collective-permute-start.3 = (bf16[64,256]{1,0:T(8,128)(2,1)S(1)}, bf16[64,256]{1,0:T(8,128)(2,1)S(1)}, u32[]{:S(2)}, u32[]{:S(2)}) collective-permute-start(bf16[64,256]{1,0:T(8,128)(2,1)S(1)} %get-tuple-element.33), channel_id=1, source_target_pairs={{0,4},{4,0},{8,12},{12,8},{16,20},{20,16},{24,28},{28,24},{1,5},{5... | collective-permute-start | bytes 98312 | tf_op jit(solution)/shard_map/ppermute | solution.py:289
  9.5 0.7 %collective-permute-done.1.even_key = bf16[64,256]{1,0:T(8,128)(2,1)S(1)} collective-permute-done((bf16[64,256]{1,0:T(8,128)(2,1)S(1)}, bf16[64,256]{1,0:T(8,128)(2,1)S(1)}, u32[]{:S(2)}, u32[]{:S(2)}) %collective-permute-start.1) | collective-permute-done | bytes 32800 | tf_op jit(solution)/shard_map/ppermute | solution.py:289
  10.2 1.3 %early.1 = (f32[2,192,320]{2,1,0:T(8,128)S(1)}, bf16[2,320,128]{2,1,0:T(8,128)(2,1)S(1)}, bf16[2,320,128]{2,1,0:T(8,128)(2,1)S(1)}, bf16[2,192,128]{2,1,0:T(8,128)(2,1)S(1)}, bf16[2,192,128]{2,1,0:T(8,128)(2,1)S(1)}) custom-call(bf16[64,1280]{1,0:T(8,128)(2,1)} %query.2, bf16[64,1280]{1,0:T(8,128)(2,1)} %output.1, f32[10,64]{1,0:T(8,128)} %lse.1, ...), custom_call_target="tpu_custom_call" | custom-call | tf_op jit(solution)/shard_map/early/pallas_call | solution.py:290
  11.6 1.5 %collective-permute-done.5.refs_1_ = bf16[16,1280]{1,0:T(8,128)(2,1)S(1)} collective-permute-done((bf16[16,1280]{1,0:T(8,128)(2,1)S(1)}, bf16[16,1280]{1,0:T(8,128)(2,1)S(1)}, u32[]{:S(2)}, u32[]{:S(2)}) %collective-permute-start.5) | collective-permute-done | bytes 40992 | tf_op jit(solution)/shard_map/ppermute | solution.py:45
  13.1 0.7 %main.1 = (bf16[128,256]{1,0:T(8,128)(2,1)S(1)}, bf16[128,256]{1,0:T(8,128)(2,1)S(1)}, f32[128,256]{1,0:T(8,128)S(1)}, bf16[2,192,320]{2,1,0:T(8,128)(2,1)S(1)}) custom-call(f32[2,192,320]{2,1,0:T(8,128)S(1)} %get-tuple-element.27.prob, bf16[2,320,128]{2,1,0:T(8,128)(2,1)S(1)} %get-tuple-element.28.queries, ...), custom_call_target="tpu_custom_call" | custom-call | tf_op jit(solution)/shard_map/main/pallas_call | solution.py:310
  13.7 1.5 %collective-permute-start.7 = (bf16[128,256]{1,0:T(8,128)(2,1)S(1)}, bf16[128,256]{1,0:T(8,128)(2,1)S(1)}, u32[]{:S(2)}, u32[]{:S(2)}) collective-permute-start(bf16[128,256]{1,0:T(8,128)(2,1)S(1)} %get-tuple-element.40), channel_id=1, source_target_pairs={{0,24},{4,28},{8,0},{12,4},{16,8},{20,12},{24,16},{28,20},{1,25},{... | collective-permute-start | bytes 196616 | tf_op jit(solution)/shard_map/ppermute | solution.py:26
  15.2 0.2 collective-permute-start.8
  15.4 0.3 %query.3 = (bf16[64,1280]{1,0:T(8,128)(2,1)S(1)}, bf16[16,1280]{1,0:T(8,128)(2,1)S(1)}) custom-call(bf16[2,192,320]{2,1,0:T(8,128)(2,1)S(1)} %get-tuple-element.37.dscore, bf16[2,192,128]{2,1,0:T(8,128)(2,1)S(1)} %get-tuple-element.30.keys), custom_call_target="tpu_custom_call" | custom-call | tf_op jit(solution)/shard_map/query/pallas_call | solution.py:321
  15.8 1.9 %collective-permute-start.10 = (bf16[16,1280]{1,0:T(8,128)(2,1)S(1)}, bf16[16,1280]{1,0:T(8,128)(2,1)S(1)}, u32[]{:S(2)}, u32[]{:S(2)}) collective-permute-start(bf16[16,1280]{1,0:T(8,128)(2,1)S(1)} %get-tuple-element.44), channel_id=1, source_target_pairs={{0,2},{1,3},{2,0},{3,1},{4,6},{5,7},{6,4},{7,5},{8,10},{9,11},{10,... | collective-permute-start | bytes 122888 | tf_op jit(solution)/shard_map/ppermute | solution.py:45
  17.6 0.4 %collective-permute-done.7.refs_0_ = bf16[128,256]{1,0:T(8,128)(2,1)S(1)} collective-permute-done((bf16[128,256]{1,0:T(8,128)(2,1)S(1)}, bf16[128,256]{1,0:T(8,128)(2,1)S(1)}, u32[]{:S(2)}, u32[]{:S(2)}) %collective-permute-start.7) | collective-permute-done | bytes 65568 | tf_op jit(solution)/shard_map/ppermute | solution.py:26
  18.1 2.3 %collective-permute-start.9 = (bf16[16,1792]{1,0:T(8,128)(2,1)S(1)}, bf16[16,1792]{1,0:T(8,128)(2,1)S(1)}, u32[]{:S(2)}, u32[]{:S(2)}) collective-permute-start(bf16[16,1792]{1,0:T(8,128)(2,1)S(1)} %get-tuple-element.42), channel_id=1, source_target_pairs={{0,3},{1,2},{2,1},{3,0},{4,7},{5,6},{6,5},{7,4},{8,11},{9,10},{10,... | collective-permute-start | bytes 172040 | tf_op jit(solution)/shard_map/ppermute | solution.py:45
  20.4 0.3 %collective-permute-start.12 = (bf16[16,1792]{1,0:T(8,128)(2,1)S(1)}, bf16[16,1792]{1,0:T(8,128)(2,1)S(1)}, u32[]{:S(2)}, u32[]{:S(2)}) collective-permute-start(bf16[16,1792]{1,0:T(8,128)(2,1)S(1)} %get-tuple-element.45), channel_id=1, source_target_pairs={{0,1},{1,0},{2,3},{3,2},{4,5},{5,4},{6,7},{7,6},{8,9},{9,8},{10,11... | collective-permute-start | bytes 172040 | tf_op jit(solution)/shard_map/ppermute | solution.py:45
  20.8 0.2 collective-permute-done.10.refs_0_.refs_4_
  20.9 1.6 %collective-permute-start.11 = (bf16[16,512]{1,0:T(8,128)(2,1)S(1)}, bf16[16,512]{1,0:T(8,128)(2,1)S(1)}, u32[]{:S(2)}, u32[]{:S(2)}) collective-permute-start(bf16[16,512]{1,0:T(8,128)(2,1)S(1)} %pack.1), channel_id=1, source_target_pairs={{0,2},{1,3},{2,0},{3,1},{4,6},{5,7},{6,4},{7,5},{8,10},{9,11},{10,... | collective-permute-start | bytes 49160 | tf_op jit(solution)/shard_map/ppermute | solution.py:45
  22.6 3.1 %collective-permute-done.11.refs_1_ = bf16[16,512]{1,0:T(8,128)(2,1)S(1)} collective-permute-done((bf16[16,512]{1,0:T(8,128)(2,1)S(1)}, bf16[16,512]{1,0:T(8,128)(2,1)S(1)}, u32[]{:S(2)}, u32[]{:S(2)}) %collective-permute-start.11) | collective-permute-done | bytes 16416 | tf_op jit(solution)/shard_map/ppermute | solution.py:45
  25.7 0.2 collective-permute-done.12.refs_2_
  25.9 0.8 %place.1 = (bf16[16,5120]{1,0:T(8,128)(2,1)}, bf16[16,1024]{1,0:T(8,128)(2,1)}, bf16[16,1024]{1,0:T(8,128)(2,1)}) custom-call(bf16[16,1792]{1,0:T(8,128)(2,1)S(1)} %collective-permute-done.9.refs_0_, bf16[16,512]{1,0:T(8,128)(2,1)S(1)} %collective-permute-done.11.refs_1_, bf16[16,1792]{1,0:T(8,128)(2,1)S(1)} %collective-permute-done.12.refs_2_, ...), custom_call_target="tpu_custom_call" | custom-call | tf_op jit(solution)/shard_map/place/pallas_call | solution.py:351
  (10 shorter events, 0.1 us)
Async XLA Ops:
  1.6 7.4 %collective-permute-start = (bf16[128,256]{1,0:T(8,128)(2,1)S(1)}, bf16[128,256]{1,0:T(8,128)(2,1)S(1)}, u32[]{:S(2)}, u32[]{:S(2)}) collective-permute-start(bf16[128,256]{1,0:T(8,128)(2,1)S(1)} %get-tuple-element.25), channel_id=1, source_target_pairs={{0,8},{4,12},{8,16},{12,20},{16,24},{20,28},{24,0},{28,4},{1,9},{5... | collective-permute-start | bytes 196616 | tf_op jit(solution)/shard_map/ppermute | solution.py:26
  4.6 4.5 %collective-permute-start.2 = (bf16[128,256]{1,0:T(8,128)(2,1)S(1)}, bf16[128,256]{1,0:T(8,128)(2,1)S(1)}, u32[]{:S(2)}, u32[]{:S(2)}) collective-permute-start(bf16[128,256]{1,0:T(8,128)(2,1)S(1)} %get-tuple-element.25), channel_id=1, source_target_pairs={{0,4},{4,0},{8,12},{12,8},{16,20},{20,16},{24,28},{28,24},{1,5},{5... | collective-permute-start | bytes 196616 | tf_op jit(solution)/shard_map/ppermute | solution.py:280
  4.6 7.0 %collective-permute-start.4 = (bf16[16,1280]{1,0:T(8,128)(2,1)S(1)}, bf16[16,1280]{1,0:T(8,128)(2,1)S(1)}, u32[]{:S(2)}, u32[]{:S(2)}) collective-permute-start(bf16[16,1280]{1,0:T(8,128)(2,1)S(1)} %get-tuple-element.34), channel_id=1, source_target_pairs={{0,3},{1,2},{2,1},{3,0},{4,7},{5,6},{6,5},{7,4},{8,11},{9,10},{10,... | collective-permute-start | bytes 122888 | tf_op jit(solution)/shard_map/ppermute | solution.py:45
  8.2 4.9 %collective-permute-start.5 = (bf16[16,1280]{1,0:T(8,128)(2,1)S(1)}, bf16[16,1280]{1,0:T(8,128)(2,1)S(1)}, u32[]{:S(2)}, u32[]{:S(2)}) collective-permute-start(bf16[16,1280]{1,0:T(8,128)(2,1)S(1)} %get-tuple-element.35), channel_id=1, source_target_pairs={{0,2},{1,3},{2,0},{3,1},{4,6},{5,7},{6,4},{7,5},{8,10},{9,11},{10,... | collective-permute-start | bytes 122888 | tf_op jit(solution)/shard_map/ppermute | solution.py:45
  8.2 4.9 %collective-permute-start.6 = (bf16[16,1280]{1,0:T(8,128)(2,1)S(1)}, bf16[16,1280]{1,0:T(8,128)(2,1)S(1)}, u32[]{:S(2)}, u32[]{:S(2)}) collective-permute-start(bf16[16,1280]{1,0:T(8,128)(2,1)S(1)} %get-tuple-element.36), channel_id=1, source_target_pairs={{0,1},{1,0},{2,3},{3,2},{4,5},{5,4},{6,7},{7,6},{8,9},{9,8},{10,11... | collective-permute-start | bytes 122888 | tf_op jit(solution)/shard_map/ppermute | solution.py:45
  9.0 1.3 %collective-permute-start.1 = (bf16[64,256]{1,0:T(8,128)(2,1)S(1)}, bf16[64,256]{1,0:T(8,128)(2,1)S(1)}, u32[]{:S(2)}, u32[]{:S(2)}) collective-permute-start(bf16[64,256]{1,0:T(8,128)(2,1)S(1)} %get-tuple-element.26), channel_id=1, source_target_pairs={{0,4},{4,0},{8,12},{12,8},{16,20},{20,16},{24,28},{28,24},{1,5},{5... | collective-permute-start | bytes 98312 | tf_op jit(solution)/shard_map/ppermute | solution.py:289
  9.1 4.0 %collective-permute-start.3 = (bf16[64,256]{1,0:T(8,128)(2,1)S(1)}, bf16[64,256]{1,0:T(8,128)(2,1)S(1)}, u32[]{:S(2)}, u32[]{:S(2)}) collective-permute-start(bf16[64,256]{1,0:T(8,128)(2,1)S(1)} %get-tuple-element.33), channel_id=1, source_target_pairs={{0,4},{4,0},{8,12},{12,8},{16,20},{20,16},{24,28},{28,24},{1,5},{5... | collective-permute-start | bytes 98312 | tf_op jit(solution)/shard_map/ppermute | solution.py:289
  13.7 4.3 %collective-permute-start.7 = (bf16[128,256]{1,0:T(8,128)(2,1)S(1)}, bf16[128,256]{1,0:T(8,128)(2,1)S(1)}, u32[]{:S(2)}, u32[]{:S(2)}) collective-permute-start(bf16[128,256]{1,0:T(8,128)(2,1)S(1)} %get-tuple-element.40), channel_id=1, source_target_pairs={{0,24},{4,28},{8,0},{12,4},{16,8},{20,12},{24,16},{28,20},{1,25},{... | collective-permute-start | bytes 196616 | tf_op jit(solution)/shard_map/ppermute | solution.py:26
  15.2 2.8 %collective-permute-start.8 = (bf16[128,256]{1,0:T(8,128)(2,1)S(1)}, bf16[128,256]{1,0:T(8,128)(2,1)S(1)}, u32[]{:S(2)}, u32[]{:S(2)}) collective-permute-start(bf16[128,256]{1,0:T(8,128)(2,1)S(1)} %get-tuple-element.41), channel_id=1, source_target_pairs={{0,28},{4,0},{8,4},{12,8},{16,12},{20,16},{24,20},{28,24},{1,29},{... | collective-permute-start | bytes 196616 | tf_op jit(solution)/shard_map/ppermute | solution.py:26
  15.8 5.2 %collective-permute-start.10 = (bf16[16,1280]{1,0:T(8,128)(2,1)S(1)}, bf16[16,1280]{1,0:T(8,128)(2,1)S(1)}, u32[]{:S(2)}, u32[]{:S(2)}) collective-permute-start(bf16[16,1280]{1,0:T(8,128)(2,1)S(1)} %get-tuple-element.44), channel_id=1, source_target_pairs={{0,2},{1,3},{2,0},{3,1},{4,6},{5,7},{6,4},{7,5},{8,10},{9,11},{10,... | collective-permute-start | bytes 122888 | tf_op jit(solution)/shard_map/ppermute | solution.py:45
  18.1 7.6 %collective-permute-start.9 = (bf16[16,1792]{1,0:T(8,128)(2,1)S(1)}, bf16[16,1792]{1,0:T(8,128)(2,1)S(1)}, u32[]{:S(2)}, u32[]{:S(2)}) collective-permute-start(bf16[16,1792]{1,0:T(8,128)(2,1)S(1)} %get-tuple-element.42), channel_id=1, source_target_pairs={{0,3},{1,2},{2,1},{3,0},{4,7},{5,6},{6,5},{7,4},{8,11},{9,10},{10,... | collective-permute-start | bytes 172040 | tf_op jit(solution)/shard_map/ppermute | solution.py:45
  20.4 5.5 %collective-permute-start.12 = (bf16[16,1792]{1,0:T(8,128)(2,1)S(1)}, bf16[16,1792]{1,0:T(8,128)(2,1)S(1)}, u32[]{:S(2)}, u32[]{:S(2)}) collective-permute-start(bf16[16,1792]{1,0:T(8,128)(2,1)S(1)} %get-tuple-element.45), channel_id=1, source_target_pairs={{0,1},{1,0},{2,3},{3,2},{4,5},{5,4},{6,7},{7,6},{8,9},{9,8},{10,11... | collective-permute-start | bytes 172040 | tf_op jit(solution)/shard_map/ppermute | solution.py:45
  20.9 4.7 %collective-permute-start.11 = (bf16[16,512]{1,0:T(8,128)(2,1)S(1)}, bf16[16,512]{1,0:T(8,128)(2,1)S(1)}, u32[]{:S(2)}, u32[]{:S(2)}) collective-permute-start(bf16[16,512]{1,0:T(8,128)(2,1)S(1)} %pack.1), channel_id=1, source_target_pairs={{0,2},{1,3},{2,0},{3,1},{4,6},{5,7},{6,4},{7,5},{8,10},{9,11},{10,... | collective-permute-start | bytes 49160 | tf_op jit(solution)/shard_map/ppermute | solution.py:45

commit v5 on v4

--- a/solution.py
+++ b/solution.py
@@ -13,7 +13,7 @@
 STEPS = 3
 GROUP = QHEADS // KVHEADS
 SCALE = HEAD_DIM ** (-0.5)
-AHEAD = (2,)
+AHEAD = (1, 2)
 
 VMEM = pl.BlockSpec(memory_space=pltpu.VMEM)
 ANY = pl.BlockSpec(memory_space=pl.ANY)
@@ -76,62 +76,48 @@
         copy.wait()
 
 
-def early_kernel(query, output, lse, key, value, even_key, first_odd, *refs):
+def early_kernel(query, output, lse, kv, near_key, *refs):
     moved, refs = refs[: STEPS - 2], refs[STEPS - 2 :]
-    odd = lax.rem(lax.axis_index("blk"), 2) == 1
-    prob, queries, outputs, keys, values, query_in, output_in, lse_in, sems = refs
-    tokens = key.shape[0]
-    kv_local = key.shape[1] // HEAD_DIM
-    copies = [
-        pltpu.make_async_copy(query, query_in, sems.at[0]),
-        pltpu.make_async_copy(output, output_in, sems.at[1]),
-        pltpu.make_async_copy(lse, lse_in, sems.at[2]),
-    ]
+    prob, queries, outputs, keys, values = refs
+    tokens = query.shape[0]
+    kv_local = kv.shape[1] // HEAD_DIM
     for g in range(kv_local):
         cols = pl.ds(g * HEAD_DIM, HEAD_DIM)
-        own = pl.ds(0, tokens)
-        copies.append(pltpu.make_async_copy(key.at[:, cols], keys.at[g, own], sems.at[3 + 2 * g]))
-        copies.append(pltpu.make_async_copy(value.at[:, cols], values.at[g, own], sems.at[4 + 2 * g]))
-    for copy in copies:
-        copy.start()
-    for g in range(kv_local):
-        cols = pl.ds(g * HEAD_DIM, HEAD_DIM)
-        part = pl.ds(tokens, tokens)
-
-        @pl.when(odd)
-        def _():
-            keys[g, part] = first_odd[pl.ds(0, tokens), cols]
-            values[g, part] = first_odd[pl.ds(tokens, tokens), cols]
-
-        @pl.when(jnp.logical_not(odd))
-        def _():
-            keys[g, part] = even_key[:, cols]
-
+        keys[g, pl.ds(0, tokens)] = kv[pl.ds(0, tokens), cols]
+        values[g, pl.ds(0, tokens)] = kv[pl.ds(tokens, tokens), cols]
+        keys[g, pl.ds(tokens, tokens)] = near_key[:, cols]
         for i in range(2, STEPS):
             part = pl.ds(i * tokens, tokens)
             keys[g, part] = moved[i - 2][pl.ds(0, tokens), cols]
             values[g, part] = moved[i - 2][pl.ds(tokens, tokens), cols]
-    for copy in copies:
-        copy.wait()
     for g in range(kv_local):
         for h in range(GROUP):
             head = pl.ds((g * GROUP + h) * HEAD_DIM, HEAD_DIM)
             part = pl.ds(h * tokens, tokens)
-            queries[g, part] = query_in[:, head]
-            outputs[g, part] = output_in[:, head]
+            queries[g, part] = query[:, head]
+            outputs[g, part] = output[:, head]
         lse_row = jnp.concatenate(
-            [lse_in[pl.ds(g * GROUP + h, 1), :] for h in range(GROUP)], axis=1
+            [lse[pl.ds(g * GROUP + h, 1), :] for h in range(GROUP)], axis=1
         )
         prob[g] = jnp.exp(nt(keys[g], queries[g]) * SCALE - lse_row)
 
 
-def halves_kernel(pair, first, second):
+def halves_kernel(own, pair, first, second):
     rows = first.shape[0]
-    first[...] = pair[pl.ds(0, rows), :]
-    second[...] = pair[pl.ds(rows, rows), :]
-
-
-def main_kernel(n, prob, queries, outputs, keys, values, mine, even_value, *refs):
+    odd = lax.rem(lax.axis_index("blk"), 2) == 1
+
+    @pl.when(odd)
+    def _():
+        first[...] = pair[pl.ds(0, rows), :]
+        second[...] = pair[pl.ds(rows, rows), :]
+
+    @pl.when(jnp.logical_not(odd))
+    def _():
+        first[...] = own[pl.ds(0, rows), :]
+        second[...] = own[pl.ds(rows, rows), :]
+
+
+def main_kernel(n, prob, queries, outputs, keys, values, mine, near_value, *refs):
     received = refs[: n - 1][::-1]
     rest = refs[n - 1 :]
     far = rest[: STEPS - 1]
@@ -150,15 +136,13 @@
                     :, pl.ds((g * GROUP + h) * HEAD_DIM, HEAD_DIM)
                 ]
     ones = jnp.ones((8, HEAD_DIM), jnp.bfloat16)
-    odd = lax.rem(lax.axis_index("blk"), 2) == 1
     for g in range(kv_local):
         cols = pl.ds(g * HEAD_DIM, HEAD_DIM)
 
-        near = pl.ds(tokens, tokens)
         v = jnp.concatenate(
             [
                 values[g, pl.ds(0, tokens)],
-                jnp.where(odd, values[g, near], even_value[:, cols]),
+                near_value[:, cols],
                 values[g, pl.ds(2 * tokens, (STEPS - 2) * tokens)],
             ],
             axis=0,
@@ -218,8 +202,10 @@
         ]
 
 
-def pack_kernel(part, *refs):
-    refs[-1][...] = part[...]
+def stash_kernel(*refs):
+    half = len(refs) // 2
+    for source, target in zip(refs[:half], refs[half:]):
+        target[...] = source[...]
 
 
 def place_kernel(n, *refs):
@@ -261,9 +247,8 @@
     kv_local = kv_width // HEAD_DIM
     rows = grad.shape[0]
     key_rows, query_rows = STEPS * tokens, GROUP * tokens
-    query, output, lse, grad, key, value = (
-        pltpu.with_memory_space_constraint(a, pltpu.HBM)
-        for a in (query, output, lse, grad, key, value)
+    far_grad, far_key, far_value = (
+        pltpu.with_memory_space_constraint(a, pltpu.HBM) for a in (grad, key, value)
     )
     *slices, kv = pl.pallas_call(
         functools.partial(prep_kernel, n),
@@ -273,20 +258,20 @@
         scratch_shapes=[pltpu.SemaphoreType.DMA((n + 2,))],
         compiler_params=PARAMS,
         name="prep",
-    )(grad, key, value)
+    )(far_grad, far_key, far_value)
     received = [exchange(slices[step], "uly", step) for step in range(1, n)]
     moved = [shifted(kv, "blk", i) for i in range(2, STEPS)]
     swap = [(i, i ^ 1) for i in range(lax.axis_size("blk"))]
-    first_odd = lax.ppermute(kv, "blk", swap)
     passed = pl.pallas_call(
         halves_kernel,
         out_shape=[shape((tokens, kv_width))] * 2,
-        in_specs=[VMEM],
+        in_specs=[VMEM] * 2,
         out_specs=[VMEM] * 2,
         compiler_params=PARAMS,
+        cost_estimate=pl.CostEstimate(flops=1000000000, bytes_accessed=1000, transcendentals=0),
         name="halves",
-    )(moved[0])
-    even_key, even_value = [lax.ppermute(a, "blk", swap) for a in passed]
+    )(kv, moved[0])
+    near_key, near_value = [lax.ppermute(a, "blk", swap) for a in passed]
     early = pl.pallas_call(
         early_kernel,
         out_shape=[
@@ -296,17 +281,11 @@
             shape((kv_local, key_rows, HEAD_DIM)),
             shape((kv_local, key_rows, HEAD_DIM)),
         ],
-        in_specs=[HBM] * 5 + [VMEM] * STEPS,
+        in_specs=[VMEM] * (3 + STEPS),
         out_specs=[VMEM] * 5,
-        scratch_shapes=[
-            pltpu.VMEM((tokens, width), jnp.bfloat16),
-            pltpu.VMEM((tokens, width), jnp.bfloat16),
-            pltpu.VMEM(lse.shape, jnp.float32),
-            pltpu.SemaphoreType.DMA((3 + 2 * kv_local,)),
-        ],
         compiler_params=PARAMS,
         name="early",
-    )(query, output, lse, key, value, even_key, first_odd, *moved)
+    )(query, output, lse, kv, near_key, *moved)
     *far, own, dscore = pl.pallas_call(
         functools.partial(main_kernel, n),
         out_shape=[shape((2 * tokens, kv_width))] * (STEPS - 1)
@@ -316,7 +295,7 @@
         scratch_shapes=[pltpu.VMEM((kv_local, query_rows, HEAD_DIM), jnp.bfloat16)],
         compiler_params=PARAMS,
         name="main",
-    )(*early, slices[0], even_value, *received[::-1])
+    )(*early, slices[0], near_value, *received[::-1])
     back = [shifted(far[i - 1], "blk", -i) for i in range(STEPS - 1, 0, -1)]
     dq, *ahead = pl.pallas_call(
         functools.partial(query_kernel, n),
@@ -338,16 +317,16 @@
         compiler_params=PARAMS,
         name="sum",
     )(dq, own, *back)
-    if AHEAD:
-        parts[AHEAD[-1]] = pl.pallas_call(
-            pack_kernel,
-            out_shape=shape(parts[AHEAD[-1]].shape),
-            in_specs=[VMEM] + [ANY] * len(AHEAD),
-            out_specs=VMEM,
-            compiler_params=PARAMS,
-            name="pack",
-        )(parts[AHEAD[-1]], *ahead)
     final = [parts[0]] + [exchange(parts[step], "uly", step) for step in range(1, n)]
+    ahead = pl.pallas_call(
+        stash_kernel,
+        out_shape=[shape((rows, width))] * len(AHEAD),
+        in_specs=[VMEM] * len(AHEAD),
+        out_specs=[VMEM] * len(AHEAD),
+        compiler_params=PARAMS,
+        cost_estimate=pl.CostEstimate(flops=300 * 10**6, bytes_accessed=1000, transcendentals=0),
+        name="stash",
+    )(*ahead)
     return pl.pallas_call(
         functools.partial(place_kernel, n),
         out_shape=[

time: 26.9 us -> 26.3 us (0.978)
  Pallas kernels: 4.06 us -> 3.02 us
  starting transfers between devices: 15.8 us -> 16.7 us
  waiting for transfers between devices: 6.08 us -> 5.71 us
    pallas_call x1, Pallas kernels: 1.34 us -> 0.28 us  [body(): pl.pallas_call(early_kernel, out_shape=[shape((kv_local, key_rows, query_...]
    ppermute x7 -> x8, starting transfers between devices: 10.6 us -> 11.6 us  [exchange(): return lax.ppermute(array, axis, pairs)]
    ppermute x3, waiting for transfers between devices: 0.42 us -> 0.01 us  [shifted(): lax.ppermute(array, axis, [(i, (i + by) % size) for i in range(size)])]
    ppermute x7 -> x8, waiting for transfers between devices: 4.96 us -> 5 us  [exchange(): return lax.ppermute(array, axis, pairs)]
    ppermute x3 -> x2, starting transfers between devices: 0.56 us -> 0.57 us  [body(): near_key, near_value = [lax.ppermute(a, 'blk', swap) for a in passed]]
    ppermute x3 -> x2, waiting for transfers between devices: 0.7 us -> 0.7 us  [body(): near_key, near_value = [lax.ppermute(a, 'blk', swap) for a in passed]]
  transfers between devices with their start and end apart: 13 -> 13, of which waited for: 6 -> 4; matrix products, arithmetic and copies ran while one was open for 0% -> 0% of each run, Pallas kernels for 6% -> 2%
where the time goes in v5:
time: 26.3 us; the launch traced here: 26.1 us
  starting transfers between devices  16.7 us (63%)
  waiting for transfers between devices  5.71 us (22%)
  Pallas kernels  3.02 us (11%)
  between operations  0.71 us (3%)
    ppermute x8, starting transfers between devices, exchange(): return lax.ppermute(array, axis, pairs)  11.6 us
    ppermute x8, waiting for transfers between devices, exchange(): return lax.ppermute(array, axis, pairs)  5 us
    ppermute x3, starting transfers between devices, shifted(): lax.ppermute(array, axis, [(i, (i + by) % size) for i in range(size)])  4.48 us
    pallas_call x1, Pallas kernels, body(): pl.pallas_call(functools.partial(prep_kernel, n), out_shape=[shape((rows,...  0.93 us
    pallas_call x1, Pallas kernels, body(): pl.pallas_call(functools.partial(place_kernel, n), out_shape=[shape((rows...  0.79 us
    ppermute x2, waiting for transfers between devices, body(): near_key, near_value = [lax.ppermute(a, 'blk', swap) for a in passed]  0.7 us
    pallas_call x1, Pallas kernels, body(): pl.pallas_call(functools.partial(main_kernel, n), out_shape=[shape((2 * t...  0.65 us
    ppermute x2, starting transfers between devices, body(): near_key, near_value = [lax.ppermute(a, 'blk', swap) for a in passed]  0.57 us
  transfers between devices with their start and end apart: 13, of which 4 were waited for; matrix products, arithmetic and copies ran while one was open for 0% of the time, Pallas kernels for 2%

profile of v5, /device:TPU:0, one launch (start us, length us, event | category | flops | bytes accessed | tf_op | source)
XLA Modules:
  0.0 26.1 jit_solution(4384262458024917664)
XLA Ops:
  0.6 0.9 %prep.1 = (bf16[16,1280]{1,0:T(8,128)(2,1)S(1)}, bf16[16,1280]{1,0:T(8,128)(2,1)S(1)}, bf16[16,1280]{1,0:T(8,128)(2,1)S(1)}, bf16[16,1280]{1,0:T(8,128)(2,1)S(1)}, bf16[128,256]{1,0:T(8,128)(2,1)S(1)}) custom-call(bf16[16,5120]{1,0:T(8,128)(2,1)} %grad.1, bf16[64,256]{1,0:T(8,128)(2,1)} %key.1, bf16[64,256]{1,0:T(8,128)(2,1)} %value.1), custom_call_target="tpu_custom_call" | custom-call | tf_op jit(solution)/shard_map/prep/pallas_call | solution.py:253
  1.6 3.0 %collective-permute-start = (bf16[128,256]{1,0:T(8,128)(2,1)S(1)}, bf16[128,256]{1,0:T(8,128)(2,1)S(1)}, u32[]{:S(2)}, u32[]{:S(2)}) collective-permute-start(bf16[128,256]{1,0:T(8,128)(2,1)S(1)} %get-tuple-element.28.own.kv), channel_id=1, source_target_pairs={{0,8},{4,12},{8,16},{12,20},{16,24},{20,28},{24,0},{28,4},{1,9},{5... | collective-permute-start | bytes 196616 | tf_op jit(solution)/shard_map/ppermute | solution.py:26
  4.6 3.6 %collective-permute-start.3 = (bf16[16,1280]{1,0:T(8,128)(2,1)S(1)}, bf16[16,1280]{1,0:T(8,128)(2,1)S(1)}, u32[]{:S(2)}, u32[]{:S(2)}) collective-permute-start(bf16[16,1280]{1,0:T(8,128)(2,1)S(1)} %get-tuple-element.37), channel_id=1, source_target_pairs={{0,3},{1,2},{2,1},{3,0},{4,7},{5,6},{6,5},{7,4},{8,11},{9,10},{10,... | collective-permute-start | bytes 122888 | tf_op jit(solution)/shard_map/ppermute | solution.py:45
  8.2 0.8 %collective-permute-start.5 = (bf16[16,1280]{1,0:T(8,128)(2,1)S(1)}, bf16[16,1280]{1,0:T(8,128)(2,1)S(1)}, u32[]{:S(2)}, u32[]{:S(2)}) collective-permute-start(bf16[16,1280]{1,0:T(8,128)(2,1)S(1)} %get-tuple-element.39), channel_id=1, source_target_pairs={{0,1},{1,0},{2,3},{3,2},{4,5},{5,4},{6,7},{7,6},{8,9},{9,8},{10,11... | collective-permute-start | bytes 122888 | tf_op jit(solution)/shard_map/ppermute | solution.py:45
  9.0 0.0 collective-permute-done.pair.refs_0_
  9.0 0.1 collective-permute-start.1
  9.0 0.5 %collective-permute-start.2 = (bf16[64,256]{1,0:T(8,128)(2,1)S(1)}, bf16[64,256]{1,0:T(8,128)(2,1)S(1)}, u32[]{:S(2)}, u32[]{:S(2)}) collective-permute-start(bf16[64,256]{1,0:T(8,128)(2,1)S(1)} %get-tuple-element.36), channel_id=1, source_target_pairs={{0,4},{4,0},{8,12},{12,8},{16,20},{20,16},{24,28},{28,24},{1,5},{5... | collective-permute-start | bytes 98312 | tf_op jit(solution)/shard_map/ppermute | solution.py:274
  9.5 0.7 %collective-permute-done.1.near_key = bf16[64,256]{1,0:T(8,128)(2,1)S(1)} collective-permute-done((bf16[64,256]{1,0:T(8,128)(2,1)S(1)}, bf16[64,256]{1,0:T(8,128)(2,1)S(1)}, u32[]{:S(2)}, u32[]{:S(2)}) %collective-permute-start.1) | collective-permute-done | bytes 32800 | tf_op jit(solution)/shard_map/ppermute | solution.py:274
  10.3 0.3 %early.1 = (f32[2,192,320]{2,1,0:T(8,128)S(1)}, bf16[2,320,128]{2,1,0:T(8,128)(2,1)S(1)}, bf16[2,320,128]{2,1,0:T(8,128)(2,1)S(1)}, bf16[2,192,128]{2,1,0:T(8,128)(2,1)S(1)}, bf16[2,192,128]{2,1,0:T(8,128)(2,1)S(1)}) custom-call(bf16[64,1280]{1,0:T(8,128)(2,1)S(1)} %copy-done, bf16[64,1280]{1,0:T(8,128)(2,1)S(1)} %copy-done.1, f32[10,64]{1,0:T(8,128)S(1)} %copy-done.2, ...), custom_call_target="tpu_custom_call" | custom-call | tf_op jit(solution)/shard_map/early/pallas_call | solution.py:275
  10.5 0.3 collective-permute-done.3.refs_0_
  10.8 2.3 %collective-permute-done.4.refs_1_ = bf16[16,1280]{1,0:T(8,128)(2,1)S(1)} collective-permute-done((bf16[16,1280]{1,0:T(8,128)(2,1)S(1)}, bf16[16,1280]{1,0:T(8,128)(2,1)S(1)}, u32[]{:S(2)}, u32[]{:S(2)}) %collective-permute-start.4) | collective-permute-done | bytes 40992 | tf_op jit(solution)/shard_map/ppermute | solution.py:45
  13.1 0.7 %main.1 = (bf16[128,256]{1,0:T(8,128)(2,1)S(1)}, bf16[128,256]{1,0:T(8,128)(2,1)S(1)}, f32[128,256]{1,0:T(8,128)S(1)}, bf16[2,192,320]{2,1,0:T(8,128)(2,1)S(1)}) custom-call(f32[2,192,320]{2,1,0:T(8,128)S(1)} %get-tuple-element.30.prob, bf16[2,320,128]{2,1,0:T(8,128)(2,1)S(1)} %get-tuple-element.31.queries, ...), custom_call_target="tpu_custom_call" | custom-call | tf_op jit(solution)/shard_map/main/pallas_call | solution.py:289
  13.7 1.5 %collective-permute-start.6 = (bf16[128,256]{1,0:T(8,128)(2,1)S(1)}, bf16[128,256]{1,0:T(8,128)(2,1)S(1)}, u32[]{:S(2)}, u32[]{:S(2)}) collective-permute-start(bf16[128,256]{1,0:T(8,128)(2,1)S(1)} %get-tuple-element.43), channel_id=1, source_target_pairs={{0,24},{4,28},{8,0},{12,4},{16,8},{20,12},{24,16},{28,20},{1,25},{... | collective-permute-start | bytes 196616 | tf_op jit(solution)/shard_map/ppermute | solution.py:26
  15.2 0.3 %query.3 = (bf16[64,1280]{1,0:T(8,128)(2,1)S(1)}, bf16[16,1280]{1,0:T(8,128)(2,1)S(1)}, bf16[16,1280]{1,0:T(8,128)(2,1)S(1)}) custom-call(bf16[2,192,320]{2,1,0:T(8,128)(2,1)S(1)} %get-tuple-element.40.dscore, bf16[2,192,128]{2,1,0:T(8,128)(2,1)S(1)} %get-tuple-element.33.keys), custom_call_target="tpu_custom_call" | custom-call | tf_op jit(solution)/shard_map/query/pallas_call | solution.py:300
  15.5 0.1 collective-permute-start.11
  15.6 2.7 %collective-permute-start.12 = (bf16[16,1280]{1,0:T(8,128)(2,1)S(1)}, bf16[16,1280]{1,0:T(8,128)(2,1)S(1)}, u32[]{:S(2)}, u32[]{:S(2)}) collective-permute-start(bf16[16,1280]{1,0:T(8,128)(2,1)S(1)} %get-tuple-element.50), channel_id=1, source_target_pairs={{0,2},{1,3},{2,0},{3,1},{4,6},{5,7},{6,4},{7,5},{8,10},{9,11},{10,... | collective-permute-start | bytes 122888 | tf_op jit(solution)/shard_map/ppermute | solution.py:45
  18.4 1.7 %collective-permute-start.8 = (bf16[16,1792]{1,0:T(8,128)(2,1)S(1)}, bf16[16,1792]{1,0:T(8,128)(2,1)S(1)}, u32[]{:S(2)}, u32[]{:S(2)}) collective-permute-start(bf16[16,1792]{1,0:T(8,128)(2,1)S(1)} %get-tuple-element.45), channel_id=1, source_target_pairs={{0,3},{1,2},{2,1},{3,0},{4,7},{5,6},{6,5},{7,4},{8,11},{9,10},{10,... | collective-permute-start | bytes 172040 | tf_op jit(solution)/shard_map/ppermute | solution.py:45
  20.1 1.1 %collective-permute-start.9 = (bf16[16,512]{1,0:T(8,128)(2,1)S(1)}, bf16[16,512]{1,0:T(8,128)(2,1)S(1)}, u32[]{:S(2)}, u32[]{:S(2)}) collective-permute-start(bf16[16,512]{1,0:T(8,128)(2,1)S(1)} %get-tuple-element.46), channel_id=1, source_target_pairs={{0,2},{1,3},{2,0},{3,1},{4,6},{5,7},{6,4},{7,5},{8,10},{9,11},{10,... | collective-permute-start | bytes 49160 | tf_op jit(solution)/shard_map/ppermute | solution.py:45
  21.2 1.6 %collective-permute-start.10 = (bf16[16,512]{1,0:T(8,128)(2,1)S(1)}, bf16[16,512]{1,0:T(8,128)(2,1)S(1)}, u32[]{:S(2)}, u32[]{:S(2)}) collective-permute-start(bf16[16,512]{1,0:T(8,128)(2,1)S(1)} %get-tuple-element.47), channel_id=1, source_target_pairs={{0,1},{1,0},{2,3},{3,2},{4,5},{5,4},{6,7},{7,6},{8,9},{9,8},{10,11... | collective-permute-start | bytes 49160 | tf_op jit(solution)/shard_map/ppermute | solution.py:45
  22.8 0.0 collective-permute-done.11.refs_0_
  22.8 0.0 collective-permute-done.12.refs_1_
  22.8 2.5 %collective-permute-done.9.refs_1_ = bf16[16,512]{1,0:T(8,128)(2,1)S(1)} collective-permute-done((bf16[16,512]{1,0:T(8,128)(2,1)S(1)}, bf16[16,512]{1,0:T(8,128)(2,1)S(1)}, u32[]{:S(2)}, u32[]{:S(2)}) %collective-permute-start.9) | collective-permute-done | bytes 16416 | tf_op jit(solution)/shard_map/ppermute | solution.py:45
  25.3 0.0 collective-permute-done.10.refs_2_
  25.3 0.8 %place.1 = (bf16[16,5120]{1,0:T(8,128)(2,1)}, bf16[16,1024]{1,0:T(8,128)(2,1)}, bf16[16,1024]{1,0:T(8,128)(2,1)}) custom-call(bf16[16,1792]{1,0:T(8,128)(2,1)S(1)} %collective-permute-done.8.refs_0_, bf16[16,512]{1,0:T(8,128)(2,1)S(1)} %collective-permute-done.9.refs_1_, bf16[16,512]{1,0:T(8,128)(2,1)S(1)} %collective-permute-done.10.refs_2_, ...), custom_call_target="tpu_custom_call" | custom-call | tf_op jit(solution)/shard_map/place/pallas_call | solution.py:330
  (16 shorter events, 0.1 us)
Async XLA Ops:
  1.6 7.4 %collective-permute-start = (bf16[128,256]{1,0:T(8,128)(2,1)S(1)}, bf16[128,256]{1,0:T(8,128)(2,1)S(1)}, u32[]{:S(2)}, u32[]{:S(2)}) collective-permute-start(bf16[128,256]{1,0:T(8,128)(2,1)S(1)} %get-tuple-element.28.own.kv), channel_id=1, source_target_pairs={{0,8},{4,12},{8,16},{12,20},{16,24},{20,28},{24,0},{28,4},{1,9},{5... | collective-permute-start | bytes 196616 | tf_op jit(solution)/shard_map/ppermute | solution.py:26
  4.6 6.2 %collective-permute-start.3 = (bf16[16,1280]{1,0:T(8,128)(2,1)S(1)}, bf16[16,1280]{1,0:T(8,128)(2,1)S(1)}, u32[]{:S(2)}, u32[]{:S(2)}) collective-permute-start(bf16[16,1280]{1,0:T(8,128)(2,1)S(1)} %get-tuple-element.37), channel_id=1, source_target_pairs={{0,3},{1,2},{2,1},{3,0},{4,7},{5,6},{6,5},{7,4},{8,11},{9,10},{10,... | collective-permute-start | bytes 122888 | tf_op jit(solution)/shard_map/ppermute | solution.py:45
  8.2 4.9 %collective-permute-start.4 = (bf16[16,1280]{1,0:T(8,128)(2,1)S(1)}, bf16[16,1280]{1,0:T(8,128)(2,1)S(1)}, u32[]{:S(2)}, u32[]{:S(2)}) collective-permute-start(bf16[16,1280]{1,0:T(8,128)(2,1)S(1)} %get-tuple-element.38), channel_id=1, source_target_pairs={{0,2},{1,3},{2,0},{3,1},{4,6},{5,7},{6,4},{7,5},{8,10},{9,11},{10,... | collective-permute-start | bytes 122888 | tf_op jit(solution)/shard_map/ppermute | solution.py:45
  8.2 2.1 %copy-start = (bf16[64,1280]{1,0:T(8,128)(2,1)S(1)}, bf16[64,1280]{1,0:T(8,128)(2,1)}, u32[]{:S(2)}) copy-start(bf16[64,1280]{1,0:T(8,128)(2,1)} %query.2) | copy-start | bytes 491524
  8.2 2.1 %copy-start.1 = (bf16[64,1280]{1,0:T(8,128)(2,1)S(1)}, bf16[64,1280]{1,0:T(8,128)(2,1)}, u32[]{:S(2)}) copy-start(bf16[64,1280]{1,0:T(8,128)(2,1)} %output.1) | copy-start | bytes 491524
  8.2 4.9 %collective-permute-start.5 = (bf16[16,1280]{1,0:T(8,128)(2,1)S(1)}, bf16[16,1280]{1,0:T(8,128)(2,1)S(1)}, u32[]{:S(2)}, u32[]{:S(2)}) collective-permute-start(bf16[16,1280]{1,0:T(8,128)(2,1)S(1)} %get-tuple-element.39), channel_id=1, source_target_pairs={{0,1},{1,0},{2,3},{3,2},{4,5},{5,4},{6,7},{7,6},{8,9},{9,8},{10,11... | collective-permute-start | bytes 122888 | tf_op jit(solution)/shard_map/ppermute | solution.py:45
  9.0 1.3 %copy-start.2 = (f32[10,64]{1,0:T(8,128)S(1)}, f32[10,64]{1,0:T(8,128)}, u32[]{:S(2)}) copy-start(f32[10,64]{1,0:T(8,128)} %lse.1) | copy-start | bytes 7684
  9.0 1.3 %collective-permute-start.1 = (bf16[64,256]{1,0:T(8,128)(2,1)S(1)}, bf16[64,256]{1,0:T(8,128)(2,1)S(1)}, u32[]{:S(2)}, u32[]{:S(2)}) collective-permute-start(bf16[64,256]{1,0:T(8,128)(2,1)S(1)} %get-tuple-element.29), channel_id=1, source_target_pairs={{0,4},{4,0},{8,12},{12,8},{16,20},{20,16},{24,28},{28,24},{1,5},{5... | collective-permute-start | bytes 98312 | tf_op jit(solution)/shard_map/ppermute | solution.py:274
  9.0 4.0 %collective-permute-start.2 = (bf16[64,256]{1,0:T(8,128)(2,1)S(1)}, bf16[64,256]{1,0:T(8,128)(2,1)S(1)}, u32[]{:S(2)}, u32[]{:S(2)}) collective-permute-start(bf16[64,256]{1,0:T(8,128)(2,1)S(1)} %get-tuple-element.36), channel_id=1, source_target_pairs={{0,4},{4,0},{8,12},{12,8},{16,20},{20,16},{24,28},{28,24},{1,5},{5... | collective-permute-start | bytes 98312 | tf_op jit(solution)/shard_map/ppermute | solution.py:274
  13.7 4.6 %collective-permute-start.6 = (bf16[128,256]{1,0:T(8,128)(2,1)S(1)}, bf16[128,256]{1,0:T(8,128)(2,1)S(1)}, u32[]{:S(2)}, u32[]{:S(2)}) collective-permute-start(bf16[128,256]{1,0:T(8,128)(2,1)S(1)} %get-tuple-element.43), channel_id=1, source_target_pairs={{0,24},{4,28},{8,0},{12,4},{16,8},{20,12},{24,16},{28,20},{1,25},{... | collective-permute-start | bytes 196616 | tf_op jit(solution)/shard_map/ppermute | solution.py:26
  15.2 3.1 %collective-permute-start.7 = (bf16[128,256]{1,0:T(8,128)(2,1)S(1)}, bf16[128,256]{1,0:T(8,128)(2,1)S(1)}, u32[]{:S(2)}, u32[]{:S(2)}) collective-permute-start(bf16[128,256]{1,0:T(8,128)(2,1)S(1)} %get-tuple-element.44), channel_id=1, source_target_pairs={{0,28},{4,0},{8,4},{12,8},{16,12},{20,16},{24,20},{28,24},{1,29},{... | collective-permute-start | bytes 196616 | tf_op jit(solution)/shard_map/ppermute | solution.py:26
  15.5 7.3 %collective-permute-start.11 = (bf16[16,1280]{1,0:T(8,128)(2,1)S(1)}, bf16[16,1280]{1,0:T(8,128)(2,1)S(1)}, u32[]{:S(2)}, u32[]{:S(2)}) collective-permute-start(bf16[16,1280]{1,0:T(8,128)(2,1)S(1)} %get-tuple-element.49), channel_id=1, source_target_pairs={{0,1},{1,0},{2,3},{3,2},{4,5},{5,4},{6,7},{7,6},{8,9},{9,8},{10,11... | collective-permute-start | bytes 122888 | tf_op jit(solution)/shard_map/ppermute | solution.py:45
  15.6 7.2 %collective-permute-start.12 = (bf16[16,1280]{1,0:T(8,128)(2,1)S(1)}, bf16[16,1280]{1,0:T(8,128)(2,1)S(1)}, u32[]{:S(2)}, u32[]{:S(2)}) collective-permute-start(bf16[16,1280]{1,0:T(8,128)(2,1)S(1)} %get-tuple-element.50), channel_id=1, source_target_pairs={{0,2},{1,3},{2,0},{3,1},{4,6},{5,7},{6,4},{7,5},{8,10},{9,11},{10,... | collective-permute-start | bytes 122888 | tf_op jit(solution)/shard_map/ppermute | solution.py:45
  18.4 7.0 %collective-permute-start.8 = (bf16[16,1792]{1,0:T(8,128)(2,1)S(1)}, bf16[16,1792]{1,0:T(8,128)(2,1)S(1)}, u32[]{:S(2)}, u32[]{:S(2)}) collective-permute-start(bf16[16,1792]{1,0:T(8,128)(2,1)S(1)} %get-tuple-element.45), channel_id=1, source_target_pairs={{0,3},{1,2},{2,1},{3,0},{4,7},{5,6},{6,5},{7,4},{8,11},{9,10},{10,... | collective-permute-start | bytes 172040 | tf_op jit(solution)/shard_map/ppermute | solution.py:45
  20.1 5.2 %collective-permute-start.9 = (bf16[16,512]{1,0:T(8,128)(2,1)S(1)}, bf16[16,512]{1,0:T(8,128)(2,1)S(1)}, u32[]{:S(2)}, u32[]{:S(2)}) collective-permute-start(bf16[16,512]{1,0:T(8,128)(2,1)S(1)} %get-tuple-element.46), channel_id=1, source_target_pairs={{0,2},{1,3},{2,0},{3,1},{4,6},{5,7},{6,4},{7,5},{8,10},{9,11},{10,... | collective-permute-start | bytes 49160 | tf_op jit(solution)/shard_map/ppermute | solution.py:45
  21.2 4.1 %collective-permute-start.10 = (bf16[16,512]{1,0:T(8,128)(2,1)S(1)}, bf16[16,512]{1,0:T(8,128)(2,1)S(1)}, u32[]{:S(2)}, u32[]{:S(2)}) collective-permute-start(bf16[16,512]{1,0:T(8,128)(2,1)S(1)} %get-tuple-element.47), channel_id=1, source_target_pairs={{0,1},{1,0},{2,3},{3,2},{4,5},{5,4},{6,7},{7,6},{8,9},{9,8},{10,11... | collective-permute-start | bytes 49160 | tf_op jit(solution)/shard_map/ppermute | solution.py:45

commit v6 on v5

--- a/solution.py
+++ b/solution.py
@@ -13,7 +13,7 @@
 STEPS = 3
 GROUP = QHEADS // KVHEADS
 SCALE = HEAD_DIM ** (-0.5)
-AHEAD = (1, 2)
+AHEAD = (2, 1)
 
 VMEM = pl.BlockSpec(memory_space=pltpu.VMEM)
 ANY = pl.BlockSpec(memory_space=pl.ANY)
@@ -76,10 +76,21 @@
         copy.wait()
 
 
-def early_kernel(query, output, lse, kv, near_key, *refs):
+def turns(n):
+    first = [0, n // 2] if n > 2 else [0]
+    return first, [step for step in range(n - 1, 0, -1) if step not in first]
+
+
+def closing(n):
+    return [n - 1] + list(range(1, n - 1))
+
+
+def early_kernel(n, query, output, lse, kv, near_key, *refs):
     moved, refs = refs[: STEPS - 2], refs[STEPS - 2 :]
-    prob, queries, outputs, keys, values = refs
+    keys, values, sides = refs[0], refs[1], refs[2:]
+    me = lax.axis_index("uly")
     tokens = query.shape[0]
+    rows = tokens // n
     kv_local = kv.shape[1] // HEAD_DIM
     for g in range(kv_local):
         cols = pl.ds(g * HEAD_DIM, HEAD_DIM)
@@ -90,16 +101,33 @@
             part = pl.ds(i * tokens, tokens)
             keys[g, part] = moved[i - 2][pl.ds(0, tokens), cols]
             values[g, part] = moved[i - 2][pl.ds(tokens, tokens), cols]
-    for g in range(kv_local):
-        for h in range(GROUP):
-            head = pl.ds((g * GROUP + h) * HEAD_DIM, HEAD_DIM)
-            part = pl.ds(h * tokens, tokens)
-            queries[g, part] = query[:, head]
-            outputs[g, part] = output[:, head]
-        lse_row = jnp.concatenate(
-            [lse[pl.ds(g * GROUP + h, 1), :] for h in range(GROUP)], axis=1
+    heads = kv_local * GROUP
+    lanes = -(-tokens // 128) * 128
+    lse_rows = jnp.concatenate([lse[...], jnp.zeros((-heads % 8, tokens), jnp.float32)], axis=0)
+    if lanes > tokens:
+        lse_rows = jnp.concatenate(
+            [lse_rows, jnp.zeros((lse_rows.shape[0], lanes - tokens), jnp.float32)], axis=1
         )
-        prob[g] = jnp.exp(nt(keys[g], queries[g]) * SCALE - lse_row)
+    for half, steps in enumerate(turns(n)):
+        prob, low, queries, outputs = sides[4 * half : 4 * half + 4]
+        pieces = []
+        for index, step in enumerate(steps):
+            source = partner(me, step, n, back=True) if step else me
+            start = pl.multiple_of(source * rows, rows)
+            pieces.append(pltpu.roll(lse_rows, lax.rem(lanes - start, lanes), 1)[:, :rows])
+            for g in range(kv_local):
+                for h in range(GROUP):
+                    head = pl.ds((g * GROUP + h) * HEAD_DIM, HEAD_DIM)
+                    part = pl.ds((index * GROUP + h) * rows, rows)
+                    queries[g, part] = query[pl.ds(start, rows), head]
+                    outputs[g, part] = output[pl.ds(start, rows), head]
+        for g in range(kv_local):
+            lse_row = jnp.concatenate(
+                [p[g * GROUP + h : g * GROUP + h + 1] for p in pieces for h in range(GROUP)], axis=1
+            )
+            wide = jnp.exp(nt(keys[g], queries[g]) * SCALE - lse_row)
+            prob[g] = wide
+            low[g] = wide.astype(jnp.bfloat16)
 
 
 def halves_kernel(own, pair, first, second):
@@ -117,46 +145,48 @@
         second[...] = own[pl.ds(rows, rows), :]
 
 
-def main_kernel(n, prob, queries, outputs, keys, values, mine, near_value, *refs):
-    received = refs[: n - 1][::-1]
-    rest = refs[n - 1 :]
-    far = rest[: STEPS - 1]
-    own, dscore, stacked = rest[STEPS - 1 :]
-    me = lax.axis_index("uly")
-    rows = mine.shape[0]
-    tokens = rows * n
-    kv_local = prob.shape[0]
-    for step in range(n):
-        source = partner(me, step, n, back=True) if step else me
-        piece = received[step - 1] if step else mine
-        start = pl.multiple_of(source * rows, rows)
-        for g in range(kv_local):
-            for h in range(GROUP):
-                stacked[g, pl.ds(start + h * tokens, rows)] = piece[
-                    :, pl.ds((g * GROUP + h) * HEAD_DIM, HEAD_DIM)
-                ]
-    ones = jnp.ones((8, HEAD_DIM), jnp.bfloat16)
-    for g in range(kv_local):
+def tile_grads(prob, low, queries, outputs, values, near_value, pieces, g):
+    tokens = near_value.shape[0]
+    v = jnp.concatenate(
+        [
+            values[g, pl.ds(0, tokens)],
+            near_value[:, pl.ds(g * HEAD_DIM, HEAD_DIM)],
+            values[g, pl.ds(2 * tokens, (STEPS - 2) * tokens)],
+        ],
+        axis=0,
+    )
+    go = jnp.concatenate(
+        [
+            piece[:, pl.ds((g * GROUP + h) * HEAD_DIM, HEAD_DIM)]
+            for piece in pieces
+            for h in range(GROUP)
+        ],
+        axis=0,
+    )
+    product = go.astype(jnp.float32) * outputs[g].astype(jnp.float32)
+    delta = jnp.sum(product, axis=1)[None, :]
+    ds = (prob[g] * (nt(v, go) - delta)).astype(jnp.bfloat16)
+    return ds, nn(ds, queries[g]), nn(low[g], go)
+
+
+def first_kernel(prob, low, queries, outputs, values, near_value, *refs):
+    pieces, (dscore, dk, dv) = refs[:-3], refs[-3:]
+    for g in range(prob.shape[0]):
+        dscore[g], dk[g], dv[g] = tile_grads(
+            prob, low, queries, outputs, values, near_value, pieces, g
+        )
+
+
+def main_kernel(prob, low, queries, outputs, values, near_value, dk_first, dv_first, *refs):
+    pieces, (*far, own, dscore) = refs[: -STEPS - 1], refs[-STEPS - 1 :]
+    tokens = near_value.shape[0]
+    for g in range(prob.shape[0]):
         cols = pl.ds(g * HEAD_DIM, HEAD_DIM)
-
-        v = jnp.concatenate(
-            [
-                values[g, pl.ds(0, tokens)],
-                near_value[:, cols],
-                values[g, pl.ds(2 * tokens, (STEPS - 2) * tokens)],
-            ],
-            axis=0,
+        dscore[g], dk, dv = tile_grads(
+            prob, low, queries, outputs, values, near_value, pieces, g
         )
-        go = stacked[g]
-        product = go.astype(jnp.float32) * outputs[g].astype(jnp.float32)
-        high = product.astype(jnp.bfloat16)
-        low = (product - high.astype(jnp.float32)).astype(jnp.bfloat16)
-        delta = (nt(ones, high) + nt(ones, low))[0:1, :]
-        p = prob[g]
-        ds = (p * (nt(v, go) - delta)).astype(jnp.bfloat16)
-        dv = nn(p.astype(jnp.bfloat16), go)
-        dk = nn(ds, queries[g]) * SCALE
-        dscore[g] = ds
+        dk = (dk + dk_first[g]) * SCALE
+        dv = dv + dv_first[g]
         own[pl.ds(0, tokens), cols] = dk[:tokens]
         own[pl.ds(tokens, tokens), cols] = dv[:tokens]
         for i in range(1, STEPS):
@@ -165,14 +195,21 @@
             far[i - 1][pl.ds(tokens, tokens), cols] = dv[part].astype(jnp.bfloat16)
 
 
-def query_kernel(n, dscore, keys, out, *sends):
-    tokens = out.shape[0]
-    rows = tokens // n
-    for g in range(dscore.shape[0]):
-        dq = (tn(dscore[g], keys[g]) * SCALE).astype(jnp.bfloat16)
-        for h in range(GROUP):
-            out[:, pl.ds((g * GROUP + h) * HEAD_DIM, HEAD_DIM)] = dq[h * tokens : (h + 1) * tokens]
+def query_kernel(n, keys, *refs):
+    dscores, out, sends = refs[:2], refs[2], refs[3:]
+    rows = out.shape[0] // n
     me = lax.axis_index("uly")
+    for dscore, steps in zip(dscores, turns(n)):
+        for g in range(keys.shape[0]):
+            dq = (tn(dscore[g], keys[g]) * SCALE).astype(jnp.bfloat16)
+            for index, step in enumerate(steps):
+                source = partner(me, step, n, back=True) if step else me
+                start = pl.multiple_of(source * rows, rows)
+                for h in range(GROUP):
+                    first = (index * GROUP + h) * rows
+                    out[pl.ds(start, rows), pl.ds((g * GROUP + h) * HEAD_DIM, HEAD_DIM)] = dq[
+                        first : first + rows
+                    ]
     for step, send in zip(AHEAD, sends):
         start = pl.multiple_of(partner(me, step, n) * rows, rows)
         send[...] = out[pl.ds(start, rows), :]
@@ -209,7 +246,7 @@
 
 
 def place_kernel(n, *refs):
-    parts, refs = refs[:n][::-1], refs[n:]
+    parts, refs = dict(zip(closing(n) + [0], refs[:n])), refs[n:]
     ahead, (dq, dk, dv, sems) = refs[: len(AHEAD)], refs[len(AHEAD) :]
     me = lax.axis_index("uly")
     width = dq.shape[1] // n
@@ -272,39 +309,57 @@
         name="halves",
     )(kv, moved[0])
     near_key, near_value = [lax.ppermute(a, "blk", swap) for a in passed]
-    early = pl.pallas_call(
-        early_kernel,
-        out_shape=[
-            shape((kv_local, key_rows, query_rows), jnp.float32),
-            shape((kv_local, query_rows, HEAD_DIM)),
-            shape((kv_local, query_rows, HEAD_DIM)),
-            shape((kv_local, key_rows, HEAD_DIM)),
-            shape((kv_local, key_rows, HEAD_DIM)),
+    columns = [len(steps) * GROUP * rows for steps in turns(n)]
+    keys, values, *sides = pl.pallas_call(
+        functools.partial(early_kernel, n),
+        out_shape=[shape((kv_local, key_rows, HEAD_DIM))] * 2
+        + [
+            shape(*dims)
+            for c in columns
+            for dims in (
+                ((kv_local, key_rows, c), jnp.float32),
+                ((kv_local, key_rows, c),),
+                ((kv_local, c, HEAD_DIM),),
+                ((kv_local, c, HEAD_DIM),),
+            )
         ],
         in_specs=[VMEM] * (3 + STEPS),
-        out_specs=[VMEM] * 5,
+        out_specs=[VMEM] * 10,
         compiler_params=PARAMS,
         name="early",
     )(query, output, lse, kv, near_key, *moved)
+    received = [slices[0]] + received
+    first, last = ([received[step] for step in steps] for steps in turns(n))
+    part = shape((kv_local, key_rows, HEAD_DIM), jnp.float32)
+    dscore_first, *parts_first = pl.pallas_call(
+        first_kernel,
+        out_shape=[shape((kv_local, key_rows, columns[0])), part, part],
+        in_specs=[VMEM] * (6 + len(first)),
+        out_specs=[VMEM] * 3,
+        compiler_params=PARAMS,
+        name="first",
+    )(*sides[:4], values, near_value, *first)
     *far, own, dscore = pl.pallas_call(
-        functools.partial(main_kernel, n),
+        main_kernel,
         out_shape=[shape((2 * tokens, kv_width))] * (STEPS - 1)
-        + [shape((2 * tokens, kv_width), jnp.float32), shape((kv_local, key_rows, query_rows))],
-        in_specs=[VMEM] * (7 + n - 1),
+        + [
+            shape((2 * tokens, kv_width), jnp.float32),
+            shape((kv_local, key_rows, columns[1])),
+        ],
+        in_specs=[VMEM] * (8 + len(last)),
         out_specs=[VMEM] * (STEPS + 1),
-        scratch_shapes=[pltpu.VMEM((kv_local, query_rows, HEAD_DIM), jnp.bfloat16)],
         compiler_params=PARAMS,
         name="main",
-    )(*early, slices[0], near_value, *received[::-1])
+    )(*sides[4:], values, near_value, *parts_first, *last)
     back = [shifted(far[i - 1], "blk", -i) for i in range(STEPS - 1, 0, -1)]
     dq, *ahead = pl.pallas_call(
         functools.partial(query_kernel, n),
         out_shape=[shape((tokens, width))] + [shape((rows, width))] * len(AHEAD),
-        in_specs=[VMEM] * 2,
+        in_specs=[VMEM] * 3,
         out_specs=[VMEM] * (1 + len(AHEAD)),
         compiler_params=PARAMS,
         name="query",
-    )(dscore, early[3])
+    )(keys, dscore_first, dscore)
     ahead = [exchange(a, "uly", step) for a, step in zip(ahead, AHEAD)]
     *parts, = pl.pallas_call(
         functools.partial(sum_kernel, n),
@@ -339,7 +394,7 @@
         scratch_shapes=[pltpu.SemaphoreType.DMA((n, 3))],
         compiler_params=PARAMS,
         name="place",
-    )(*final[::-1], *ahead)
+    )(*(final[step] for step in closing(n)), final[0], *ahead)
 
 
 def solution(mesh):

time: 26.3 us -> 25.6 us (0.973)
  waiting for transfers between devices: 5.71 us -> 5 us
  Pallas kernels: 3.02 us -> 3.33 us
  starting transfers between devices: 16.7 us -> 16.4 us
    ppermute x8, waiting for transfers between devices: 5 us -> 4.29 us  [exchange(): return lax.ppermute(array, axis, pairs)]
    pallas_call x2 -> x3, Pallas kernels: 0.94 us -> 1.24 us  [the longest x1 0.44 us: body(): pl.pallas_call(main_kernel, out_shape=[shape((2 * tokens, kv_width))] * (...]
    ppermute x8, starting transfers between devices: 11.6 us -> 11.3 us  [exchange(): return lax.ppermute(array, axis, pairs)]
  transfers between devices with their start and end apart: 13 -> 13, of which waited for: 4 -> 3; matrix products, arithmetic and copies ran while one was open for 0% -> 0% of each run, Pallas kernels for 2% -> 5%
where the time goes in v6:
time: 25.6 us; the launch traced here: 25.4 us
  starting transfers between devices  16.4 us (64%)
  waiting for transfers between devices  5 us (20%)
  Pallas kernels  3.33 us (13%)
  between operations  0.72 us (3%)
    ppermute x8, starting transfers between devices, exchange(): return lax.ppermute(array, axis, pairs)  11.3 us
    ppermute x3, starting transfers between devices, shifted(): lax.ppermute(array, axis, [(i, (i + by) % size) for i in range(size)])  4.48 us
    ppermute x8, waiting for transfers between devices, exchange(): return lax.ppermute(array, axis, pairs)  4.29 us
    pallas_call x1, Pallas kernels, body(): pl.pallas_call(functools.partial(prep_kernel, n), out_shape=[shape((rows,...  0.93 us
    pallas_call x1, Pallas kernels, body(): pl.pallas_call(functools.partial(place_kernel, n), out_shape=[shape((rows...  0.79 us
    ppermute x2, waiting for transfers between devices, body(): near_key, near_value = [lax.ppermute(a, 'blk', swap) for a in passed]  0.7 us
    ppermute x2, starting transfers between devices, body(): near_key, near_value = [lax.ppermute(a, 'blk', swap) for a in passed]  0.57 us
  transfers between devices with their start and end apart: 13, of which 3 were waited for; matrix products, arithmetic and copies ran while one was open for 0% of the time, Pallas kernels for 5%

profile of v6, /device:TPU:0, one launch (start us, length us, event | category | flops | bytes accessed | tf_op | source)
XLA Modules:
  0.0 25.4 jit_solution(17739419630038955705)
XLA Ops:
  0.6 0.9 %prep.1 = (bf16[16,1280]{1,0:T(8,128)(2,1)S(1)}, bf16[16,1280]{1,0:T(8,128)(2,1)S(1)}, bf16[16,1280]{1,0:T(8,128)(2,1)S(1)}, bf16[16,1280]{1,0:T(8,128)(2,1)S(1)}, bf16[128,256]{1,0:T(8,128)(2,1)S(1)}) custom-call(bf16[16,5120]{1,0:T(8,128)(2,1)} %grad.1, bf16[64,256]{1,0:T(8,128)(2,1)} %key.1, bf16[64,256]{1,0:T(8,128)(2,1)} %value.1), custom_call_target="tpu_custom_call" | custom-call | tf_op jit(solution)/shard_map/prep/pallas_call | solution.py:290
  1.6 3.0 %collective-permute-start = (bf16[128,256]{1,0:T(8,128)(2,1)S(1)}, bf16[128,256]{1,0:T(8,128)(2,1)S(1)}, u32[]{:S(2)}, u32[]{:S(2)}) collective-permute-start(bf16[128,256]{1,0:T(8,128)(2,1)S(1)} %get-tuple-element.36.own.kv), channel_id=1, source_target_pairs={{0,8},{4,12},{8,16},{12,20},{16,24},{20,28},{24,0},{28,4},{1,9},{5... | collective-permute-start | bytes 196616 | tf_op jit(solution)/shard_map/ppermute | solution.py:26
  4.6 2.6 %collective-permute-start.3 = (bf16[16,1280]{1,0:T(8,128)(2,1)S(1)}, bf16[16,1280]{1,0:T(8,128)(2,1)S(1)}, u32[]{:S(2)}, u32[]{:S(2)}) collective-permute-start(bf16[16,1280]{1,0:T(8,128)(2,1)S(1)} %get-tuple-element.46), channel_id=1, source_target_pairs={{0,2},{1,3},{2,0},{3,1},{4,6},{5,7},{6,4},{7,5},{8,10},{9,11},{10,... | collective-permute-start | bytes 122888 | tf_op jit(solution)/shard_map/ppermute | solution.py:45
  7.2 1.3 %collective-permute-start.4 = (bf16[16,1280]{1,0:T(8,128)(2,1)S(1)}, bf16[16,1280]{1,0:T(8,128)(2,1)S(1)}, u32[]{:S(2)}, u32[]{:S(2)}) collective-permute-start(bf16[16,1280]{1,0:T(8,128)(2,1)S(1)} %get-tuple-element.54), channel_id=1, source_target_pairs={{0,3},{1,2},{2,1},{3,0},{4,7},{5,6},{6,5},{7,4},{8,11},{9,10},{10,... | collective-permute-start | bytes 122888 | tf_op jit(solution)/shard_map/ppermute | solution.py:45
  8.5 0.2 collective-permute-start.5
  8.7 0.0 collective-permute-done.pair.refs_0_
  8.8 0.1 collective-permute-start.1
  8.8 0.5 %collective-permute-start.2 = (bf16[64,256]{1,0:T(8,128)(2,1)S(1)}, bf16[64,256]{1,0:T(8,128)(2,1)S(1)}, u32[]{:S(2)}, u32[]{:S(2)}) collective-permute-start(bf16[64,256]{1,0:T(8,128)(2,1)S(1)} %get-tuple-element.44), channel_id=1, source_target_pairs={{0,4},{4,0},{8,12},{12,8},{16,20},{20,16},{24,28},{28,24},{1,5},{5... | collective-permute-start | bytes 98312 | tf_op jit(solution)/shard_map/ppermute | solution.py:311
  9.3 0.7 %collective-permute-done.1.near_key = bf16[64,256]{1,0:T(8,128)(2,1)S(1)} collective-permute-done((bf16[64,256]{1,0:T(8,128)(2,1)S(1)}, bf16[64,256]{1,0:T(8,128)(2,1)S(1)}, u32[]{:S(2)}, u32[]{:S(2)}) %collective-permute-start.1) | collective-permute-done | bytes 32800 | tf_op jit(solution)/shard_map/ppermute | solution.py:311
  10.0 0.4 %early.1 = (bf16[2,192,128]{2,1,0:T(8,128)(2,1)S(1)}, bf16[2,192,128]{2,1,0:T(8,128)(2,1)S(1)}, f32[2,192,160]{2,1,0:T(8,128)S(1)}, bf16[2,192,160]{2,1,0:T(8,12...) custom-call(bf16[64,1280]{1,0:T(8,128)(2,1)S(1)} %copy-done, ...), custom_call_target="tpu_custom_call" | custom-call | tf_op jit(solution)/shard_map/early/pallas_call | solution.py:313
  10.4 0.0 collective-permute-done.3.refs_1_
  10.4 0.4 %first.1 = (bf16[2,192,160]{2,1,0:T(8,128)(2,1)S(1)}, f32[2,192,128]{2,1,0:T(8,128)S(1)}, f32[2,192,128]{2,1,0:T(8,128)S(1)}) custom-call(f32[2,192,160]{2,1,0:T(8,128)S(1)} %get-tuple-element.39.prob, bf16[2,192,160]{2,1,0:T(8,128)(2,1)S(1)} %get-tuple-element.40.low, bf16[2,160,128]{2,1,0:T(8,128)(2,1)S(1)} %get-tuple-element.41.queries, ...), custom_call_target="tpu_custom_call" | custom-call | tf_op jit(solution)/shard_map/first/pallas_call | solution.py:334
  10.9 2.1 %collective-permute-done.4.refs_0_ = bf16[16,1280]{1,0:T(8,128)(2,1)S(1)} collective-permute-done((bf16[16,1280]{1,0:T(8,128)(2,1)S(1)}, bf16[16,1280]{1,0:T(8,128)(2,1)S(1)}, u32[]{:S(2)}, u32[]{:S(2)}) %collective-permute-start.4) | collective-permute-done | bytes 40992 | tf_op jit(solution)/shard_map/ppermute | solution.py:45
  13.0 0.0 collective-permute-done.5.refs_1_
  13.0 0.4 %main.1 = (bf16[128,256]{1,0:T(8,128)(2,1)S(1)}, bf16[128,256]{1,0:T(8,128)(2,1)S(1)}, f32[128,256]{1,0:T(8,128)S(1)}, bf16[2,192,160]{2,1,0:T(8,128)(2,1)S(1)}) custom-call(f32[2,192,160]{2,1,0:T(8,128)S(1)} %get-tuple-element.48.prob, bf16[2,192,160]{2,1,0:T(8,128)(2,1)S(1)} %get-tuple-element.49.low, bf16[2,160,128]{2,1,0:T(8,128)(2,1)S(1)} %get-tuple-element.50.queries, ...), custom_call_target="tpu_custom_call" | custom-call | tf_op jit(solution)/shard_map/main/pallas_call | solution.py:342
  13.4 1.5 %collective-permute-start.6 = (bf16[128,256]{1,0:T(8,128)(2,1)S(1)}, bf16[128,256]{1,0:T(8,128)(2,1)S(1)}, u32[]{:S(2)}, u32[]{:S(2)}) collective-permute-start(bf16[128,256]{1,0:T(8,128)(2,1)S(1)} %get-tuple-element.59), channel_id=1, source_target_pairs={{0,24},{4,28},{8,0},{12,4},{16,8},{20,12},{24,16},{28,20},{1,25},{... | collective-permute-start | bytes 196616 | tf_op jit(solution)/shard_map/ppermute | solution.py:26
  14.9 0.0 collective-permute-start.7
  14.9 0.3 %query.3 = (bf16[64,1280]{1,0:T(8,128)(2,1)S(1)}, bf16[16,1280]{1,0:T(8,128)(2,1)S(1)}, bf16[16,1280]{1,0:T(8,128)(2,1)S(1)}) custom-call(bf16[2,192,128]{2,1,0:T(8,128)(2,1)S(1)} %get-tuple-element.38.keys, bf16[2,192,160]{2,1,0:T(8,128)(2,1)S(1)} %get-tuple-element.47.refs_0_, bf16[2,192,160]{2,1,0:T(8,128)(2,1)S(1)} %get-tuple-element.56.refs_1_), custom_call_target="tpu_custom_call" | custom-call | tf_op jit(solution)/shard_map/query/pallas_call | solution.py:355
  15.2 1.8 %collective-permute-start.11 = (bf16[16,1280]{1,0:T(8,128)(2,1)S(1)}, bf16[16,1280]{1,0:T(8,128)(2,1)S(1)}, u32[]{:S(2)}, u32[]{:S(2)}) collective-permute-start(bf16[16,1280]{1,0:T(8,128)(2,1)S(1)} %get-tuple-element.65), channel_id=1, source_target_pairs={{0,2},{1,3},{2,0},{3,1},{4,6},{5,7},{6,4},{7,5},{8,10},{9,11},{10,... | collective-permute-start | bytes 122888 | tf_op jit(solution)/shard_map/ppermute | solution.py:45
  17.0 0.9 %collective-permute-start.12 = (bf16[16,1280]{1,0:T(8,128)(2,1)S(1)}, bf16[16,1280]{1,0:T(8,128)(2,1)S(1)}, u32[]{:S(2)}, u32[]{:S(2)}) collective-permute-start(bf16[16,1280]{1,0:T(8,128)(2,1)S(1)} %get-tuple-element.66), channel_id=1, source_target_pairs={{0,1},{1,0},{2,3},{3,2},{4,5},{5,4},{6,7},{7,6},{8,9},{9,8},{10,11... | collective-permute-start | bytes 122888 | tf_op jit(solution)/shard_map/ppermute | solution.py:45
  18.0 1.9 %collective-permute-start.8 = (bf16[16,1792]{1,0:T(8,128)(2,1)S(1)}, bf16[16,1792]{1,0:T(8,128)(2,1)S(1)}, u32[]{:S(2)}, u32[]{:S(2)}) collective-permute-start(bf16[16,1792]{1,0:T(8,128)(2,1)S(1)} %get-tuple-element.61), channel_id=1, source_target_pairs={{0,3},{1,2},{2,1},{3,0},{4,7},{5,6},{6,5},{7,4},{8,11},{9,10},{10,... | collective-permute-start | bytes 172040 | tf_op jit(solution)/shard_map/ppermute | solution.py:45
  19.9 2.5 %collective-permute-start.10 = (bf16[16,512]{1,0:T(8,128)(2,1)S(1)}, bf16[16,512]{1,0:T(8,128)(2,1)S(1)}, u32[]{:S(2)}, u32[]{:S(2)}) collective-permute-start(bf16[16,512]{1,0:T(8,128)(2,1)S(1)} %get-tuple-element.63), channel_id=1, source_target_pairs={{0,2},{1,3},{2,0},{3,1},{4,6},{5,7},{6,4},{7,5},{8,10},{9,11},{10,... | collective-permute-start | bytes 49160 | tf_op jit(solution)/shard_map/ppermute | solution.py:45
  22.4 2.2 %collective-permute-done.9.refs_1_ = bf16[16,512]{1,0:T(8,128)(2,1)S(1)} collective-permute-done((bf16[16,512]{1,0:T(8,128)(2,1)S(1)}, bf16[16,512]{1,0:T(8,128)(2,1)S(1)}, u32[]{:S(2)}, u32[]{:S(2)}) %collective-permute-start.9) | collective-permute-done | bytes 16416 | tf_op jit(solution)/shard_map/ppermute | solution.py:45
  24.6 0.8 %place.1 = (bf16[16,5120]{1,0:T(8,128)(2,1)}, bf16[16,1024]{1,0:T(8,128)(2,1)}, bf16[16,1024]{1,0:T(8,128)(2,1)}) custom-call(bf16[16,1792]{1,0:T(8,128)(2,1)S(1)} %collective-permute-done.8.refs_0_, bf16[16,512]{1,0:T(8,128)(2,1)S(1)} %collective-permute-done.9.refs_1_, bf16[16,512]{1,0:T(8,128)(2,1)S(1)} %collective-permute-done.10.refs_2_, ...), custom_call_target="tpu_custom_call" | custom-call | tf_op jit(solution)/shard_map/place/pallas_call | solution.py:385
  (17 shorter events, 0.1 us)
Async XLA Ops:
  1.6 7.2 %collective-permute-start = (bf16[128,256]{1,0:T(8,128)(2,1)S(1)}, bf16[128,256]{1,0:T(8,128)(2,1)S(1)}, u32[]{:S(2)}, u32[]{:S(2)}) collective-permute-start(bf16[128,256]{1,0:T(8,128)(2,1)S(1)} %get-tuple-element.36.own.kv), channel_id=1, source_target_pairs={{0,8},{4,12},{8,16},{12,20},{16,24},{20,28},{24,0},{28,4},{1,9},{5... | collective-permute-start | bytes 196616 | tf_op jit(solution)/shard_map/ppermute | solution.py:26
  4.6 5.9 %collective-permute-start.3 = (bf16[16,1280]{1,0:T(8,128)(2,1)S(1)}, bf16[16,1280]{1,0:T(8,128)(2,1)S(1)}, u32[]{:S(2)}, u32[]{:S(2)}) collective-permute-start(bf16[16,1280]{1,0:T(8,128)(2,1)S(1)} %get-tuple-element.46), channel_id=1, source_target_pairs={{0,2},{1,3},{2,0},{3,1},{4,6},{5,7},{6,4},{7,5},{8,10},{9,11},{10,... | collective-permute-start | bytes 122888 | tf_op jit(solution)/shard_map/ppermute | solution.py:45
  7.2 5.8 %collective-permute-start.4 = (bf16[16,1280]{1,0:T(8,128)(2,1)S(1)}, bf16[16,1280]{1,0:T(8,128)(2,1)S(1)}, u32[]{:S(2)}, u32[]{:S(2)}) collective-permute-start(bf16[16,1280]{1,0:T(8,128)(2,1)S(1)} %get-tuple-element.54), channel_id=1, source_target_pairs={{0,3},{1,2},{2,1},{3,0},{4,7},{5,6},{6,5},{7,4},{8,11},{9,10},{10,... | collective-permute-start | bytes 122888 | tf_op jit(solution)/shard_map/ppermute | solution.py:45
  8.5 1.5 %copy-start = (bf16[64,1280]{1,0:T(8,128)(2,1)S(1)}, bf16[64,1280]{1,0:T(8,128)(2,1)}, u32[]{:S(2)}) copy-start(bf16[64,1280]{1,0:T(8,128)(2,1)} %query.2) | copy-start | bytes 491524
  8.5 1.5 %copy-start.1 = (bf16[64,1280]{1,0:T(8,128)(2,1)S(1)}, bf16[64,1280]{1,0:T(8,128)(2,1)}, u32[]{:S(2)}) copy-start(bf16[64,1280]{1,0:T(8,128)(2,1)} %output.1) | copy-start | bytes 491524
  8.5 4.5 %collective-permute-start.5 = (bf16[16,1280]{1,0:T(8,128)(2,1)S(1)}, bf16[16,1280]{1,0:T(8,128)(2,1)S(1)}, u32[]{:S(2)}, u32[]{:S(2)}) collective-permute-start(bf16[16,1280]{1,0:T(8,128)(2,1)S(1)} %get-tuple-element.55), channel_id=1, source_target_pairs={{0,1},{1,0},{2,3},{3,2},{4,5},{5,4},{6,7},{7,6},{8,9},{9,8},{10,11... | collective-permute-start | bytes 122888 | tf_op jit(solution)/shard_map/ppermute | solution.py:45
  8.7 1.3 %copy-start.2 = (f32[10,64]{1,0:T(8,128)S(1)}, f32[10,64]{1,0:T(8,128)}, u32[]{:S(2)}) copy-start(f32[10,64]{1,0:T(8,128)} %lse.1) | copy-start | bytes 7684
  8.8 1.3 %collective-permute-start.1 = (bf16[64,256]{1,0:T(8,128)(2,1)S(1)}, bf16[64,256]{1,0:T(8,128)(2,1)S(1)}, u32[]{:S(2)}, u32[]{:S(2)}) collective-permute-start(bf16[64,256]{1,0:T(8,128)(2,1)S(1)} %get-tuple-element.37), channel_id=1, source_target_pairs={{0,4},{4,0},{8,12},{12,8},{16,20},{20,16},{24,28},{28,24},{1,5},{5... | collective-permute-start | bytes 98312 | tf_op jit(solution)/shard_map/ppermute | solution.py:311
  8.8 1.6 %collective-permute-start.2 = (bf16[64,256]{1,0:T(8,128)(2,1)S(1)}, bf16[64,256]{1,0:T(8,128)(2,1)S(1)}, u32[]{:S(2)}, u32[]{:S(2)}) collective-permute-start(bf16[64,256]{1,0:T(8,128)(2,1)S(1)} %get-tuple-element.44), channel_id=1, source_target_pairs={{0,4},{4,0},{8,12},{12,8},{16,20},{20,16},{24,28},{28,24},{1,5},{5... | collective-permute-start | bytes 98312 | tf_op jit(solution)/shard_map/ppermute | solution.py:311
  13.4 4.5 %collective-permute-start.6 = (bf16[128,256]{1,0:T(8,128)(2,1)S(1)}, bf16[128,256]{1,0:T(8,128)(2,1)S(1)}, u32[]{:S(2)}, u32[]{:S(2)}) collective-permute-start(bf16[128,256]{1,0:T(8,128)(2,1)S(1)} %get-tuple-element.59), channel_id=1, source_target_pairs={{0,24},{4,28},{8,0},{12,4},{16,8},{20,12},{24,16},{28,20},{1,25},{... | collective-permute-start | bytes 196616 | tf_op jit(solution)/shard_map/ppermute | solution.py:26
  14.9 3.0 %collective-permute-start.7 = (bf16[128,256]{1,0:T(8,128)(2,1)S(1)}, bf16[128,256]{1,0:T(8,128)(2,1)S(1)}, u32[]{:S(2)}, u32[]{:S(2)}) collective-permute-start(bf16[128,256]{1,0:T(8,128)(2,1)S(1)} %get-tuple-element.60), channel_id=1, source_target_pairs={{0,28},{4,0},{8,4},{12,8},{16,12},{20,16},{24,20},{28,24},{1,29},{... | collective-permute-start | bytes 196616 | tf_op jit(solution)/shard_map/ppermute | solution.py:26
  15.2 7.2 %collective-permute-start.11 = (bf16[16,1280]{1,0:T(8,128)(2,1)S(1)}, bf16[16,1280]{1,0:T(8,128)(2,1)S(1)}, u32[]{:S(2)}, u32[]{:S(2)}) collective-permute-start(bf16[16,1280]{1,0:T(8,128)(2,1)S(1)} %get-tuple-element.65), channel_id=1, source_target_pairs={{0,2},{1,3},{2,0},{3,1},{4,6},{5,7},{6,4},{7,5},{8,10},{9,11},{10,... | collective-permute-start | bytes 122888 | tf_op jit(solution)/shard_map/ppermute | solution.py:45
  17.0 5.4 %collective-permute-start.12 = (bf16[16,1280]{1,0:T(8,128)(2,1)S(1)}, bf16[16,1280]{1,0:T(8,128)(2,1)S(1)}, u32[]{:S(2)}, u32[]{:S(2)}) collective-permute-start(bf16[16,1280]{1,0:T(8,128)(2,1)S(1)} %get-tuple-element.66), channel_id=1, source_target_pairs={{0,1},{1,0},{2,3},{3,2},{4,5},{5,4},{6,7},{7,6},{8,9},{9,8},{10,11... | collective-permute-start | bytes 122888 | tf_op jit(solution)/shard_map/ppermute | solution.py:45
  18.0 6.7 %collective-permute-start.8 = (bf16[16,1792]{1,0:T(8,128)(2,1)S(1)}, bf16[16,1792]{1,0:T(8,128)(2,1)S(1)}, u32[]{:S(2)}, u32[]{:S(2)}) collective-permute-start(bf16[16,1792]{1,0:T(8,128)(2,1)S(1)} %get-tuple-element.61), channel_id=1, source_target_pairs={{0,3},{1,2},{2,1},{3,0},{4,7},{5,6},{6,5},{7,4},{8,11},{9,10},{10,... | collective-permute-start | bytes 172040 | tf_op jit(solution)/shard_map/ppermute | solution.py:45
  19.9 4.8 %collective-permute-start.9 = (bf16[16,512]{1,0:T(8,128)(2,1)S(1)}, bf16[16,512]{1,0:T(8,128)(2,1)S(1)}, u32[]{:S(2)}, u32[]{:S(2)}) collective-permute-start(bf16[16,512]{1,0:T(8,128)(2,1)S(1)} %get-tuple-element.62), channel_id=1, source_target_pairs={{0,1},{1,0},{2,3},{3,2},{4,5},{5,4},{6,7},{7,6},{8,9},{9,8},{10,11... | collective-permute-start | bytes 49160 | tf_op jit(solution)/shard_map/ppermute | solution.py:45
  19.9 4.8 %collective-permute-start.10 = (bf16[16,512]{1,0:T(8,128)(2,1)S(1)}, bf16[16,512]{1,0:T(8,128)(2,1)S(1)}, u32[]{:S(2)}, u32[]{:S(2)}) collective-permute-start(bf16[16,512]{1,0:T(8,128)(2,1)S(1)} %get-tuple-element.63), channel_id=1, source_target_pairs={{0,2},{1,3},{2,0},{3,1},{4,6},{5,7},{6,4},{7,5},{8,10},{9,11},{10,... | collective-permute-start | bytes 49160 | tf_op jit(solution)/shard_map/ppermute | solution.py:45

commit v7 on v6

--- a/solution.py
+++ b/solution.py
@@ -145,48 +145,57 @@
         second[...] = own[pl.ds(rows, rows), :]
 
 
-def tile_grads(prob, low, queries, outputs, values, near_value, pieces, g):
+def score_grads(prob, outputs, values, near_value, pieces):
     tokens = near_value.shape[0]
-    v = jnp.concatenate(
-        [
-            values[g, pl.ds(0, tokens)],
-            near_value[:, pl.ds(g * HEAD_DIM, HEAD_DIM)],
-            values[g, pl.ds(2 * tokens, (STEPS - 2) * tokens)],
-        ],
-        axis=0,
-    )
-    go = jnp.concatenate(
-        [
-            piece[:, pl.ds((g * GROUP + h) * HEAD_DIM, HEAD_DIM)]
-            for piece in pieces
-            for h in range(GROUP)
-        ],
-        axis=0,
-    )
-    product = go.astype(jnp.float32) * outputs[g].astype(jnp.float32)
-    delta = jnp.sum(product, axis=1)[None, :]
-    ds = (prob[g] * (nt(v, go) - delta)).astype(jnp.bfloat16)
-    return ds, nn(ds, queries[g]), nn(low[g], go)
+    heads = range(prob.shape[0])
+    stacked, products = [], []
+    for g in heads:
+        v = jnp.concatenate(
+            [
+                values[g, pl.ds(0, tokens)],
+                near_value[:, pl.ds(g * HEAD_DIM, HEAD_DIM)],
+                values[g, pl.ds(2 * tokens, (STEPS - 2) * tokens)],
+            ],
+            axis=0,
+        )
+        go = jnp.concatenate(
+            [
+                piece[:, pl.ds((g * GROUP + h) * HEAD_DIM, HEAD_DIM)]
+                for piece in pieces
+                for h in range(GROUP)
+            ],
+            axis=0,
+        )
+        stacked.append(go)
+        products.append(nt(v, go))
+    deltas = [
+        jnp.sum(stacked[g].astype(jnp.float32) * outputs[g].astype(jnp.float32), axis=1)[None, :]
+        for g in heads
+    ]
+    scores = [
+        (prob[g] * (products[g] - deltas[g])).astype(jnp.bfloat16) for g in heads
+    ]
+    return stacked, scores
 
 
 def first_kernel(prob, low, queries, outputs, values, near_value, *refs):
     pieces, (dscore, dk, dv) = refs[:-3], refs[-3:]
+    stacked, scores = score_grads(prob, outputs, values, near_value, pieces)
     for g in range(prob.shape[0]):
-        dscore[g], dk[g], dv[g] = tile_grads(
-            prob, low, queries, outputs, values, near_value, pieces, g
-        )
+        dscore[g] = scores[g]
+        dk[g] = nn(scores[g], queries[g])
+        dv[g] = nn(low[g], stacked[g])
 
 
 def main_kernel(prob, low, queries, outputs, values, near_value, dk_first, dv_first, *refs):
     pieces, (*far, own, dscore) = refs[: -STEPS - 1], refs[-STEPS - 1 :]
     tokens = near_value.shape[0]
+    stacked, scores = score_grads(prob, outputs, values, near_value, pieces)
     for g in range(prob.shape[0]):
         cols = pl.ds(g * HEAD_DIM, HEAD_DIM)
-        dscore[g], dk, dv = tile_grads(
-            prob, low, queries, outputs, values, near_value, pieces, g
-        )
-        dk = (dk + dk_first[g]) * SCALE
-        dv = dv + dv_first[g]
+        dscore[g] = scores[g]
+        dk = (nn(scores[g], queries[g]) + dk_first[g]) * SCALE
+        dv = nn(low[g], stacked[g]) + dv_first[g]
         own[pl.ds(0, tokens), cols] = dk[:tokens]
         own[pl.ds(tokens, tokens), cols] = dv[:tokens]
         for i in range(1, STEPS):

time: 25.6 us -> 25.6 us (level)
  transfers between devices with their start and end apart: 13 -> 13, of which waited for: 3 -> 3; matrix products, arithmetic and copies ran while one was open for 0% -> 0% of each run, Pallas kernels for 5% -> 4%
where the time goes in v7:
time: 25.6 us; the launch traced here: 25.4 us
  starting transfers between devices  16.3 us (64%)
  waiting for transfers between devices  5.08 us (20%)
  Pallas kernels  3.23 us (13%)
  between operations  0.72 us (3%)
    ppermute x8, starting transfers between devices, exchange(): return lax.ppermute(array, axis, pairs)  11.3 us
    ppermute x3, starting transfers between devices, shifted(): lax.ppermute(array, axis, [(i, (i + by) % size) for i in range(size)])  4.48 us
    ppermute x8, waiting for transfers between devices, exchange(): return lax.ppermute(array, axis, pairs)  4.37 us
    pallas_call x1, Pallas kernels, body(): pl.pallas_call(functools.partial(prep_kernel, n), out_shape=[shape((rows,...  0.93 us
    pallas_call x1, Pallas kernels, body(): pl.pallas_call(functools.partial(place_kernel, n), out_shape=[shape((rows...  0.79 us
    ppermute x2, waiting for transfers between devices, body(): near_key, near_value = [lax.ppermute(a, 'blk', swap) for a in passed]  0.7 us
    ppermute x2, starting transfers between devices, body(): near_key, near_value = [lax.ppermute(a, 'blk', swap) for a in passed]  0.57 us
  transfers between devices with their start and end apart: 13, of which 3 were waited for; matrix products, arithmetic and copies ran while one was open for 0% of the time, Pallas kernels for 4%

profile of v7, /device:TPU:0, one launch (start us, length us, event | category | flops | bytes accessed | tf_op | source)
XLA Modules:
  0.0 25.4 jit_solution(13805853588814887822)
XLA Ops:
  0.6 0.9 %prep.1 = (bf16[16,1280]{1,0:T(8,128)(2,1)S(1)}, bf16[16,1280]{1,0:T(8,128)(2,1)S(1)}, bf16[16,1280]{1,0:T(8,128)(2,1)S(1)}, bf16[16,1280]{1,0:T(8,128)(2,1)S(1)}, bf16[128,256]{1,0:T(8,128)(2,1)S(1)}) custom-call(bf16[16,5120]{1,0:T(8,128)(2,1)} %grad.1, bf16[64,256]{1,0:T(8,128)(2,1)} %key.1, bf16[64,256]{1,0:T(8,128)(2,1)} %value.1), custom_call_target="tpu_custom_call" | custom-call | tf_op jit(solution)/shard_map/prep/pallas_call | solution.py:299
  1.6 3.0 %collective-permute-start = (bf16[128,256]{1,0:T(8,128)(2,1)S(1)}, bf16[128,256]{1,0:T(8,128)(2,1)S(1)}, u32[]{:S(2)}, u32[]{:S(2)}) collective-permute-start(bf16[128,256]{1,0:T(8,128)(2,1)S(1)} %get-tuple-element.36.own.kv), channel_id=1, source_target_pairs={{0,8},{4,12},{8,16},{12,20},{16,24},{20,28},{24,0},{28,4},{1,9},{5... | collective-permute-start | bytes 196616 | tf_op jit(solution)/shard_map/ppermute | solution.py:26
  4.6 2.6 %collective-permute-start.3 = (bf16[16,1280]{1,0:T(8,128)(2,1)S(1)}, bf16[16,1280]{1,0:T(8,128)(2,1)S(1)}, u32[]{:S(2)}, u32[]{:S(2)}) collective-permute-start(bf16[16,1280]{1,0:T(8,128)(2,1)S(1)} %get-tuple-element.46), channel_id=1, source_target_pairs={{0,2},{1,3},{2,0},{3,1},{4,6},{5,7},{6,4},{7,5},{8,10},{9,11},{10,... | collective-permute-start | bytes 122888 | tf_op jit(solution)/shard_map/ppermute | solution.py:45
  7.2 1.3 %collective-permute-start.4 = (bf16[16,1280]{1,0:T(8,128)(2,1)S(1)}, bf16[16,1280]{1,0:T(8,128)(2,1)S(1)}, u32[]{:S(2)}, u32[]{:S(2)}) collective-permute-start(bf16[16,1280]{1,0:T(8,128)(2,1)S(1)} %get-tuple-element.54), channel_id=1, source_target_pairs={{0,3},{1,2},{2,1},{3,0},{4,7},{5,6},{6,5},{7,4},{8,11},{9,10},{10,... | collective-permute-start | bytes 122888 | tf_op jit(solution)/shard_map/ppermute | solution.py:45
  8.5 0.2 collective-permute-start.5
  8.7 0.0 collective-permute-done.pair.refs_0_
  8.8 0.1 collective-permute-start.1
  8.8 0.5 %collective-permute-start.2 = (bf16[64,256]{1,0:T(8,128)(2,1)S(1)}, bf16[64,256]{1,0:T(8,128)(2,1)S(1)}, u32[]{:S(2)}, u32[]{:S(2)}) collective-permute-start(bf16[64,256]{1,0:T(8,128)(2,1)S(1)} %get-tuple-element.44), channel_id=1, source_target_pairs={{0,4},{4,0},{8,12},{12,8},{16,20},{20,16},{24,28},{28,24},{1,5},{5... | collective-permute-start | bytes 98312 | tf_op jit(solution)/shard_map/ppermute | solution.py:320
  9.3 0.7 %collective-permute-done.1.near_key = bf16[64,256]{1,0:T(8,128)(2,1)S(1)} collective-permute-done((bf16[64,256]{1,0:T(8,128)(2,1)S(1)}, bf16[64,256]{1,0:T(8,128)(2,1)S(1)}, u32[]{:S(2)}, u32[]{:S(2)}) %collective-permute-start.1) | collective-permute-done | bytes 32800 | tf_op jit(solution)/shard_map/ppermute | solution.py:320
  10.0 0.4 %early.1 = (bf16[2,192,128]{2,1,0:T(8,128)(2,1)S(1)}, bf16[2,192,128]{2,1,0:T(8,128)(2,1)S(1)}, f32[2,192,160]{2,1,0:T(8,128)S(1)}, bf16[2,192,160]{2,1,0:T(8,12...) custom-call(bf16[64,1280]{1,0:T(8,128)(2,1)S(1)} %copy-done, ...), custom_call_target="tpu_custom_call" | custom-call | tf_op jit(solution)/shard_map/early/pallas_call | solution.py:322
  10.4 0.0 collective-permute-done.3.refs_1_
  10.4 0.4 %first.1 = (bf16[2,192,160]{2,1,0:T(8,128)(2,1)S(1)}, f32[2,192,128]{2,1,0:T(8,128)S(1)}, f32[2,192,128]{2,1,0:T(8,128)S(1)}) custom-call(f32[2,192,160]{2,1,0:T(8,128)S(1)} %get-tuple-element.39.prob, bf16[2,192,160]{2,1,0:T(8,128)(2,1)S(1)} %get-tuple-element.40.low, bf16[2,160,128]{2,1,0:T(8,128)(2,1)S(1)} %get-tuple-element.41.queries, ...), custom_call_target="tpu_custom_call" | custom-call | tf_op jit(solution)/shard_map/first/pallas_call | solution.py:343
  10.8 2.1 %collective-permute-done.4.refs_0_ = bf16[16,1280]{1,0:T(8,128)(2,1)S(1)} collective-permute-done((bf16[16,1280]{1,0:T(8,128)(2,1)S(1)}, bf16[16,1280]{1,0:T(8,128)(2,1)S(1)}, u32[]{:S(2)}, u32[]{:S(2)}) %collective-permute-start.4) | collective-permute-done | bytes 40992 | tf_op jit(solution)/shard_map/ppermute | solution.py:45
  13.0 0.4 %main.1 = (bf16[128,256]{1,0:T(8,128)(2,1)S(1)}, bf16[128,256]{1,0:T(8,128)(2,1)S(1)}, f32[128,256]{1,0:T(8,128)S(1)}, bf16[2,192,160]{2,1,0:T(8,128)(2,1)S(1)}) custom-call(f32[2,192,160]{2,1,0:T(8,128)S(1)} %get-tuple-element.48.prob, bf16[2,192,160]{2,1,0:T(8,128)(2,1)S(1)} %get-tuple-element.49.low, bf16[2,160,128]{2,1,0:T(8,128)(2,1)S(1)} %get-tuple-element.50.queries, ...), custom_call_target="tpu_custom_call" | custom-call | tf_op jit(solution)/shard_map/main/pallas_call | solution.py:351
  13.4 1.5 %collective-permute-start.6 = (bf16[128,256]{1,0:T(8,128)(2,1)S(1)}, bf16[128,256]{1,0:T(8,128)(2,1)S(1)}, u32[]{:S(2)}, u32[]{:S(2)}) collective-permute-start(bf16[128,256]{1,0:T(8,128)(2,1)S(1)} %get-tuple-element.59), channel_id=1, source_target_pairs={{0,24},{4,28},{8,0},{12,4},{16,8},{20,12},{24,16},{28,20},{1,25},{... | collective-permute-start | bytes 196616 | tf_op jit(solution)/shard_map/ppermute | solution.py:26
  14.8 0.3 %query.3 = (bf16[64,1280]{1,0:T(8,128)(2,1)S(1)}, bf16[16,1280]{1,0:T(8,128)(2,1)S(1)}, bf16[16,1280]{1,0:T(8,128)(2,1)S(1)}) custom-call(bf16[2,192,128]{2,1,0:T(8,128)(2,1)S(1)} %get-tuple-element.38.keys, bf16[2,192,160]{2,1,0:T(8,128)(2,1)S(1)} %get-tuple-element.47.refs_0_, bf16[2,192,160]{2,1,0:T(8,128)(2,1)S(1)} %get-tuple-element.56.refs_1_), custom_call_target="tpu_custom_call" | custom-call | tf_op jit(solution)/shard_map/query/pallas_call | solution.py:364
  15.2 1.8 %collective-permute-start.11 = (bf16[16,1280]{1,0:T(8,128)(2,1)S(1)}, bf16[16,1280]{1,0:T(8,128)(2,1)S(1)}, u32[]{:S(2)}, u32[]{:S(2)}) collective-permute-start(bf16[16,1280]{1,0:T(8,128)(2,1)S(1)} %get-tuple-element.65), channel_id=1, source_target_pairs={{0,2},{1,3},{2,0},{3,1},{4,6},{5,7},{6,4},{7,5},{8,10},{9,11},{10,... | collective-permute-start | bytes 122888 | tf_op jit(solution)/shard_map/ppermute | solution.py:45
  17.0 0.9 %collective-permute-start.12 = (bf16[16,1280]{1,0:T(8,128)(2,1)S(1)}, bf16[16,1280]{1,0:T(8,128)(2,1)S(1)}, u32[]{:S(2)}, u32[]{:S(2)}) collective-permute-start(bf16[16,1280]{1,0:T(8,128)(2,1)S(1)} %get-tuple-element.66), channel_id=1, source_target_pairs={{0,1},{1,0},{2,3},{3,2},{4,5},{5,4},{6,7},{7,6},{8,9},{9,8},{10,11... | collective-permute-start | bytes 122888 | tf_op jit(solution)/shard_map/ppermute | solution.py:45
  17.8 0.0 collective-permute-done.7.refs_1_
  17.9 1.9 %collective-permute-start.8 = (bf16[16,1792]{1,0:T(8,128)(2,1)S(1)}, bf16[16,1792]{1,0:T(8,128)(2,1)S(1)}, u32[]{:S(2)}, u32[]{:S(2)}) collective-permute-start(bf16[16,1792]{1,0:T(8,128)(2,1)S(1)} %get-tuple-element.61), channel_id=1, source_target_pairs={{0,3},{1,2},{2,1},{3,0},{4,7},{5,6},{6,5},{7,4},{8,11},{9,10},{10,... | collective-permute-start | bytes 172040 | tf_op jit(solution)/shard_map/ppermute | solution.py:45
  19.8 2.5 %collective-permute-start.10 = (bf16[16,512]{1,0:T(8,128)(2,1)S(1)}, bf16[16,512]{1,0:T(8,128)(2,1)S(1)}, u32[]{:S(2)}, u32[]{:S(2)}) collective-permute-start(bf16[16,512]{1,0:T(8,128)(2,1)S(1)} %get-tuple-element.63), channel_id=1, source_target_pairs={{0,2},{1,3},{2,0},{3,1},{4,6},{5,7},{6,4},{7,5},{8,10},{9,11},{10,... | collective-permute-start | bytes 49160 | tf_op jit(solution)/shard_map/ppermute | solution.py:45
  22.3 0.0 collective-permute-done.11.refs_0_
  22.4 2.2 %collective-permute-done.9.refs_1_ = bf16[16,512]{1,0:T(8,128)(2,1)S(1)} collective-permute-done((bf16[16,512]{1,0:T(8,128)(2,1)S(1)}, bf16[16,512]{1,0:T(8,128)(2,1)S(1)}, u32[]{:S(2)}, u32[]{:S(2)}) %collective-permute-start.9) | collective-permute-done | bytes 16416 | tf_op jit(solution)/shard_map/ppermute | solution.py:45
  24.6 0.8 %place.1 = (bf16[16,5120]{1,0:T(8,128)(2,1)}, bf16[16,1024]{1,0:T(8,128)(2,1)}, bf16[16,1024]{1,0:T(8,128)(2,1)}) custom-call(bf16[16,1792]{1,0:T(8,128)(2,1)S(1)} %collective-permute-done.8.refs_0_, bf16[16,512]{1,0:T(8,128)(2,1)S(1)} %collective-permute-done.9.refs_1_, bf16[16,512]{1,0:T(8,128)(2,1)S(1)} %collective-permute-done.10.refs_2_, ...), custom_call_target="tpu_custom_call" | custom-call | tf_op jit(solution)/shard_map/place/pallas_call | solution.py:394
  (17 shorter events, 0.1 us)
Async XLA Ops:
  1.6 7.2 %collective-permute-start = (bf16[128,256]{1,0:T(8,128)(2,1)S(1)}, bf16[128,256]{1,0:T(8,128)(2,1)S(1)}, u32[]{:S(2)}, u32[]{:S(2)}) collective-permute-start(bf16[128,256]{1,0:T(8,128)(2,1)S(1)} %get-tuple-element.36.own.kv), channel_id=1, source_target_pairs={{0,8},{4,12},{8,16},{12,20},{16,24},{20,28},{24,0},{28,4},{1,9},{5... | collective-permute-start | bytes 196616 | tf_op jit(solution)/shard_map/ppermute | solution.py:26
  4.6 5.9 %collective-permute-start.3 = (bf16[16,1280]{1,0:T(8,128)(2,1)S(1)}, bf16[16,1280]{1,0:T(8,128)(2,1)S(1)}, u32[]{:S(2)}, u32[]{:S(2)}) collective-permute-start(bf16[16,1280]{1,0:T(8,128)(2,1)S(1)} %get-tuple-element.46), channel_id=1, source_target_pairs={{0,2},{1,3},{2,0},{3,1},{4,6},{5,7},{6,4},{7,5},{8,10},{9,11},{10,... | collective-permute-start | bytes 122888 | tf_op jit(solution)/shard_map/ppermute | solution.py:45
  7.2 5.8 %collective-permute-start.4 = (bf16[16,1280]{1,0:T(8,128)(2,1)S(1)}, bf16[16,1280]{1,0:T(8,128)(2,1)S(1)}, u32[]{:S(2)}, u32[]{:S(2)}) collective-permute-start(bf16[16,1280]{1,0:T(8,128)(2,1)S(1)} %get-tuple-element.54), channel_id=1, source_target_pairs={{0,3},{1,2},{2,1},{3,0},{4,7},{5,6},{6,5},{7,4},{8,11},{9,10},{10,... | collective-permute-start | bytes 122888 | tf_op jit(solution)/shard_map/ppermute | solution.py:45
  8.5 1.5 %copy-start = (bf16[64,1280]{1,0:T(8,128)(2,1)S(1)}, bf16[64,1280]{1,0:T(8,128)(2,1)}, u32[]{:S(2)}) copy-start(bf16[64,1280]{1,0:T(8,128)(2,1)} %query.2) | copy-start | bytes 491524
  8.5 1.5 %copy-start.1 = (bf16[64,1280]{1,0:T(8,128)(2,1)S(1)}, bf16[64,1280]{1,0:T(8,128)(2,1)}, u32[]{:S(2)}) copy-start(bf16[64,1280]{1,0:T(8,128)(2,1)} %output.1) | copy-start | bytes 491524
  8.5 4.5 %collective-permute-start.5 = (bf16[16,1280]{1,0:T(8,128)(2,1)S(1)}, bf16[16,1280]{1,0:T(8,128)(2,1)S(1)}, u32[]{:S(2)}, u32[]{:S(2)}) collective-permute-start(bf16[16,1280]{1,0:T(8,128)(2,1)S(1)} %get-tuple-element.55), channel_id=1, source_target_pairs={{0,1},{1,0},{2,3},{3,2},{4,5},{5,4},{6,7},{7,6},{8,9},{9,8},{10,11... | collective-permute-start | bytes 122888 | tf_op jit(solution)/shard_map/ppermute | solution.py:45
  8.7 1.3 %copy-start.2 = (f32[10,64]{1,0:T(8,128)S(1)}, f32[10,64]{1,0:T(8,128)}, u32[]{:S(2)}) copy-start(f32[10,64]{1,0:T(8,128)} %lse.1) | copy-start | bytes 7684
  8.8 1.3 %collective-permute-start.1 = (bf16[64,256]{1,0:T(8,128)(2,1)S(1)}, bf16[64,256]{1,0:T(8,128)(2,1)S(1)}, u32[]{:S(2)}, u32[]{:S(2)}) collective-permute-start(bf16[64,256]{1,0:T(8,128)(2,1)S(1)} %get-tuple-element.37), channel_id=1, source_target_pairs={{0,4},{4,0},{8,12},{12,8},{16,20},{20,16},{24,28},{28,24},{1,5},{5... | collective-permute-start | bytes 98312 | tf_op jit(solution)/shard_map/ppermute | solution.py:320
  8.8 1.6 %collective-permute-start.2 = (bf16[64,256]{1,0:T(8,128)(2,1)S(1)}, bf16[64,256]{1,0:T(8,128)(2,1)S(1)}, u32[]{:S(2)}, u32[]{:S(2)}) collective-permute-start(bf16[64,256]{1,0:T(8,128)(2,1)S(1)} %get-tuple-element.44), channel_id=1, source_target_pairs={{0,4},{4,0},{8,12},{12,8},{16,20},{20,16},{24,28},{28,24},{1,5},{5... | collective-permute-start | bytes 98312 | tf_op jit(solution)/shard_map/ppermute | solution.py:320
  13.4 4.5 %collective-permute-start.6 = (bf16[128,256]{1,0:T(8,128)(2,1)S(1)}, bf16[128,256]{1,0:T(8,128)(2,1)S(1)}, u32[]{:S(2)}, u32[]{:S(2)}) collective-permute-start(bf16[128,256]{1,0:T(8,128)(2,1)S(1)} %get-tuple-element.59), channel_id=1, source_target_pairs={{0,24},{4,28},{8,0},{12,4},{16,8},{20,12},{24,16},{28,20},{1,25},{... | collective-permute-start | bytes 196616 | tf_op jit(solution)/shard_map/ppermute | solution.py:26
  14.8 3.0 %collective-permute-start.7 = (bf16[128,256]{1,0:T(8,128)(2,1)S(1)}, bf16[128,256]{1,0:T(8,128)(2,1)S(1)}, u32[]{:S(2)}, u32[]{:S(2)}) collective-permute-start(bf16[128,256]{1,0:T(8,128)(2,1)S(1)} %get-tuple-element.60), channel_id=1, source_target_pairs={{0,28},{4,0},{8,4},{12,8},{16,12},{20,16},{24,20},{28,24},{1,29},{... | collective-permute-start | bytes 196616 | tf_op jit(solution)/shard_map/ppermute | solution.py:26
  15.2 7.2 %collective-permute-start.11 = (bf16[16,1280]{1,0:T(8,128)(2,1)S(1)}, bf16[16,1280]{1,0:T(8,128)(2,1)S(1)}, u32[]{:S(2)}, u32[]{:S(2)}) collective-permute-start(bf16[16,1280]{1,0:T(8,128)(2,1)S(1)} %get-tuple-element.65), channel_id=1, source_target_pairs={{0,2},{1,3},{2,0},{3,1},{4,6},{5,7},{6,4},{7,5},{8,10},{9,11},{10,... | collective-permute-start | bytes 122888 | tf_op jit(solution)/shard_map/ppermute | solution.py:45
  17.0 5.4 %collective-permute-start.12 = (bf16[16,1280]{1,0:T(8,128)(2,1)S(1)}, bf16[16,1280]{1,0:T(8,128)(2,1)S(1)}, u32[]{:S(2)}, u32[]{:S(2)}) collective-permute-start(bf16[16,1280]{1,0:T(8,128)(2,1)S(1)} %get-tuple-element.66), channel_id=1, source_target_pairs={{0,1},{1,0},{2,3},{3,2},{4,5},{5,4},{6,7},{7,6},{8,9},{9,8},{10,11... | collective-permute-start | bytes 122888 | tf_op jit(solution)/shard_map/ppermute | solution.py:45
  17.9 6.7 %collective-permute-start.8 = (bf16[16,1792]{1,0:T(8,128)(2,1)S(1)}, bf16[16,1792]{1,0:T(8,128)(2,1)S(1)}, u32[]{:S(2)}, u32[]{:S(2)}) collective-permute-start(bf16[16,1792]{1,0:T(8,128)(2,1)S(1)} %get-tuple-element.61), channel_id=1, source_target_pairs={{0,3},{1,2},{2,1},{3,0},{4,7},{5,6},{6,5},{7,4},{8,11},{9,10},{10,... | collective-permute-start | bytes 172040 | tf_op jit(solution)/shard_map/ppermute | solution.py:45
  19.8 4.8 %collective-permute-start.9 = (bf16[16,512]{1,0:T(8,128)(2,1)S(1)}, bf16[16,512]{1,0:T(8,128)(2,1)S(1)}, u32[]{:S(2)}, u32[]{:S(2)}) collective-permute-start(bf16[16,512]{1,0:T(8,128)(2,1)S(1)} %get-tuple-element.62), channel_id=1, source_target_pairs={{0,1},{1,0},{2,3},{3,2},{4,5},{5,4},{6,7},{7,6},{8,9},{9,8},{10,11... | collective-permute-start | bytes 49160 | tf_op jit(solution)/shard_map/ppermute | solution.py:45
  19.8 4.8 %collective-permute-start.10 = (bf16[16,512]{1,0:T(8,128)(2,1)S(1)}, bf16[16,512]{1,0:T(8,128)(2,1)S(1)}, u32[]{:S(2)}, u32[]{:S(2)}) collective-permute-start(bf16[16,512]{1,0:T(8,128)(2,1)S(1)} %get-tuple-element.63), channel_id=1, source_target_pairs={{0,2},{1,3},{2,0},{3,1},{4,6},{5,7},{6,4},{7,5},{8,10},{9,11},{10,... | collective-permute-start | bytes 49160 | tf_op jit(solution)/shard_map/ppermute | solution.py:45

commit v8 on v7

--- a/solution.py
+++ b/solution.py
@@ -178,13 +178,20 @@
     return stacked, scores
 
 
-def first_kernel(prob, low, queries, outputs, values, near_value, *refs):
-    pieces, (dscore, dk, dv) = refs[:-3], refs[-3:]
+def first_kernel(prob, low, queries, outputs, values, near_value, keys, *refs):
+    pieces, (dq, dk, dv) = refs[:-3], refs[-3:]
     stacked, scores = score_grads(prob, outputs, values, near_value, pieces)
+    rows = pieces[0].shape[0]
     for g in range(prob.shape[0]):
-        dscore[g] = scores[g]
         dk[g] = nn(scores[g], queries[g])
         dv[g] = nn(low[g], stacked[g])
+        query_rows = (tn(scores[g], keys[g]) * SCALE).astype(jnp.bfloat16)
+        for index in range(len(pieces)):
+            for h in range(GROUP):
+                start = (index * GROUP + h) * rows
+                dq[pl.ds(index * rows, rows), pl.ds((g * GROUP + h) * HEAD_DIM, HEAD_DIM)] = (
+                    query_rows[start : start + rows]
+                )
 
 
 def main_kernel(prob, low, queries, outputs, values, near_value, dk_first, dv_first, *refs):
@@ -204,21 +211,24 @@
             far[i - 1][pl.ds(tokens, tokens), cols] = dv[part].astype(jnp.bfloat16)
 
 
-def query_kernel(n, keys, *refs):
-    dscores, out, sends = refs[:2], refs[2], refs[3:]
+def query_kernel(n, keys, dq_first, dscore, out, *sends):
     rows = out.shape[0] // n
     me = lax.axis_index("uly")
-    for dscore, steps in zip(dscores, turns(n)):
-        for g in range(keys.shape[0]):
-            dq = (tn(dscore[g], keys[g]) * SCALE).astype(jnp.bfloat16)
-            for index, step in enumerate(steps):
-                source = partner(me, step, n, back=True) if step else me
-                start = pl.multiple_of(source * rows, rows)
-                for h in range(GROUP):
-                    first = (index * GROUP + h) * rows
-                    out[pl.ds(start, rows), pl.ds((g * GROUP + h) * HEAD_DIM, HEAD_DIM)] = dq[
-                        first : first + rows
-                    ]
+    first, last = turns(n)
+    for index, step in enumerate(first):
+        source = partner(me, step, n, back=True) if step else me
+        out[pl.ds(pl.multiple_of(source * rows, rows), rows), :] = dq_first[
+            pl.ds(index * rows, rows), :
+        ]
+    for g in range(keys.shape[0]):
+        dq = (tn(dscore[g], keys[g]) * SCALE).astype(jnp.bfloat16)
+        for index, step in enumerate(last):
+            start = pl.multiple_of(partner(me, step, n, back=True) * rows, rows)
+            for h in range(GROUP):
+                at = (index * GROUP + h) * rows
+                out[pl.ds(start, rows), pl.ds((g * GROUP + h) * HEAD_DIM, HEAD_DIM)] = dq[
+                    at : at + rows
+                ]
     for step, send in zip(AHEAD, sends):
         start = pl.multiple_of(partner(me, step, n) * rows, rows)
         send[...] = out[pl.ds(start, rows), :]
@@ -340,14 +350,14 @@
     received = [slices[0]] + received
     first, last = ([received[step] for step in steps] for steps in turns(n))
     part = shape((kv_local, key_rows, HEAD_DIM), jnp.float32)
-    dscore_first, *parts_first = pl.pallas_call(
+    dq_first, *parts_first = pl.pallas_call(
         first_kernel,
-        out_shape=[shape((kv_local, key_rows, columns[0])), part, part],
-        in_specs=[VMEM] * (6 + len(first)),
+        out_shape=[shape((len(first) * rows, width)), part, part],
+        in_specs=[VMEM] * (7 + len(first)),
         out_specs=[VMEM] * 3,
         compiler_params=PARAMS,
         name="first",
-    )(*sides[:4], values, near_value, *first)
+    )(*sides[:4], values, near_value, keys, *first)
     *far, own, dscore = pl.pallas_call(
         main_kernel,
         out_shape=[shape((2 * tokens, kv_width))] * (STEPS - 1)
@@ -368,7 +378,7 @@
         out_specs=[VMEM] * (1 + len(AHEAD)),
         compiler_params=PARAMS,
         name="query",
-    )(keys, dscore_first, dscore)
+    )(keys, dq_first, dscore)
     ahead = [exchange(a, "uly", step) for a, step in zip(ahead, AHEAD)]
     *parts, = pl.pallas_call(
         functools.partial(sum_kernel, n),

time: 25.6 us -> 25.6 us (level)
  transfers between devices with their start and end apart: 13 -> 13, of which waited for: 3 -> 3; matrix products, arithmetic and copies ran while one was open for 0% -> 0% of each run, Pallas kernels for 4% -> 5%
where the time goes in v8:
time: 25.6 us; the launch traced here: 25.4 us
  starting transfers between devices  16.4 us (64%)
  waiting for transfers between devices  4.96 us (19%)
  Pallas kernels  3.27 us (13%)
  between operations  0.72 us (3%)
    ppermute x8, starting transfers between devices, exchange(): return lax.ppermute(array, axis, pairs)  11.4 us
    ppermute x3, starting transfers between devices, shifted(): lax.ppermute(array, axis, [(i, (i + by) % size) for i in range(size)])  4.48 us
    ppermute x8, waiting for transfers between devices, exchange(): return lax.ppermute(array, axis, pairs)  4.25 us
    pallas_call x1, Pallas kernels, body(): pl.pallas_call(functools.partial(prep_kernel, n), out_shape=[shape((rows,...  0.93 us
    pallas_call x1, Pallas kernels, body(): pl.pallas_call(functools.partial(place_kernel, n), out_shape=[shape((rows...  0.79 us
    ppermute x2, waiting for transfers between devices, body(): near_key, near_value = [lax.ppermute(a, 'blk', swap) for a in passed]  0.7 us
    ppermute x2, starting transfers between devices, body(): near_key, near_value = [lax.ppermute(a, 'blk', swap) for a in passed]  0.57 us
  transfers between devices with their start and end apart: 13, of which 3 were waited for; matrix products, arithmetic and copies ran while one was open for 0% of the time, Pallas kernels for 5%

profile of v8, /device:TPU:0, one launch (start us, length us, event | category | flops | bytes accessed | tf_op | source)
XLA Modules:
  0.0 25.4 jit_solution(1632138159868769789)
XLA Ops:
  0.6 0.9 %prep.1 = (bf16[16,1280]{1,0:T(8,128)(2,1)S(1)}, bf16[16,1280]{1,0:T(8,128)(2,1)S(1)}, bf16[16,1280]{1,0:T(8,128)(2,1)S(1)}, bf16[16,1280]{1,0:T(8,128)(2,1)S(1)}, bf16[128,256]{1,0:T(8,128)(2,1)S(1)}) custom-call(bf16[16,5120]{1,0:T(8,128)(2,1)} %grad.1, bf16[64,256]{1,0:T(8,128)(2,1)} %key.1, bf16[64,256]{1,0:T(8,128)(2,1)} %value.1), custom_call_target="tpu_custom_call" | custom-call | tf_op jit(solution)/shard_map/prep/pallas_call | solution.py:309
  1.6 3.0 %collective-permute-start = (bf16[128,256]{1,0:T(8,128)(2,1)S(1)}, bf16[128,256]{1,0:T(8,128)(2,1)S(1)}, u32[]{:S(2)}, u32[]{:S(2)}) collective-permute-start(bf16[128,256]{1,0:T(8,128)(2,1)S(1)} %get-tuple-element.36.own.kv), channel_id=1, source_target_pairs={{0,8},{4,12},{8,16},{12,20},{16,24},{20,28},{24,0},{28,4},{1,9},{5... | collective-permute-start | bytes 196616 | tf_op jit(solution)/shard_map/ppermute | solution.py:26
  4.6 2.6 %collective-permute-start.3 = (bf16[16,1280]{1,0:T(8,128)(2,1)S(1)}, bf16[16,1280]{1,0:T(8,128)(2,1)S(1)}, u32[]{:S(2)}, u32[]{:S(2)}) collective-permute-start(bf16[16,1280]{1,0:T(8,128)(2,1)S(1)} %get-tuple-element.46), channel_id=1, source_target_pairs={{0,2},{1,3},{2,0},{3,1},{4,6},{5,7},{6,4},{7,5},{8,10},{9,11},{10,... | collective-permute-start | bytes 122888 | tf_op jit(solution)/shard_map/ppermute | solution.py:45
  7.2 1.3 %collective-permute-start.4 = (bf16[16,1280]{1,0:T(8,128)(2,1)S(1)}, bf16[16,1280]{1,0:T(8,128)(2,1)S(1)}, u32[]{:S(2)}, u32[]{:S(2)}) collective-permute-start(bf16[16,1280]{1,0:T(8,128)(2,1)S(1)} %get-tuple-element.54), channel_id=1, source_target_pairs={{0,3},{1,2},{2,1},{3,0},{4,7},{5,6},{6,5},{7,4},{8,11},{9,10},{10,... | collective-permute-start | bytes 122888 | tf_op jit(solution)/shard_map/ppermute | solution.py:45
  8.5 0.2 collective-permute-start.5
  8.7 0.0 collective-permute-done.pair.refs_0_
  8.8 0.1 collective-permute-start.1
  8.8 0.5 %collective-permute-start.2 = (bf16[64,256]{1,0:T(8,128)(2,1)S(1)}, bf16[64,256]{1,0:T(8,128)(2,1)S(1)}, u32[]{:S(2)}, u32[]{:S(2)}) collective-permute-start(bf16[64,256]{1,0:T(8,128)(2,1)S(1)} %get-tuple-element.44), channel_id=1, source_target_pairs={{0,4},{4,0},{8,12},{12,8},{16,20},{20,16},{24,28},{28,24},{1,5},{5... | collective-permute-start | bytes 98312 | tf_op jit(solution)/shard_map/ppermute | solution.py:330
  9.3 0.7 %collective-permute-done.1.near_key = bf16[64,256]{1,0:T(8,128)(2,1)S(1)} collective-permute-done((bf16[64,256]{1,0:T(8,128)(2,1)S(1)}, bf16[64,256]{1,0:T(8,128)(2,1)S(1)}, u32[]{:S(2)}, u32[]{:S(2)}) %collective-permute-start.1) | collective-permute-done | bytes 32800 | tf_op jit(solution)/shard_map/ppermute | solution.py:330
  10.0 0.4 %early.1 = (bf16[2,192,128]{2,1,0:T(8,128)(2,1)S(1)}, bf16[2,192,128]{2,1,0:T(8,128)(2,1)S(1)}, f32[2,192,160]{2,1,0:T(8,128)S(1)}, bf16[2,192,160]{2,1,0:T(8,12...) custom-call(bf16[64,1280]{1,0:T(8,128)(2,1)S(1)} %copy-done, ...), custom_call_target="tpu_custom_call" | custom-call | tf_op jit(solution)/shard_map/early/pallas_call | solution.py:332
  10.4 0.0 collective-permute-done.3.refs_1_
  10.4 0.0 collective-permute-done.2.near_value
  10.4 0.5 %first.1 = (bf16[32,1280]{1,0:T(8,128)(2,1)S(1)}, f32[2,192,128]{2,1,0:T(8,128)S(1)}, f32[2,192,128]{2,1,0:T(8,128)S(1)}) custom-call(f32[2,192,160]{2,1,0:T(8,128)S(1)} %get-tuple-element.39.prob, bf16[2,192,160]{2,1,0:T(8,128)(2,1)S(1)} %get-tuple-element.40.low, bf16[2,160,128]{2,1,0:T(8,128)(2,1)S(1)} %get-tuple-element.41.queries, ...), custom_call_target="tpu_custom_call" | custom-call | tf_op jit(solution)/shard_map/first/pallas_call | solution.py:353
  10.9 2.0 %collective-permute-done.4.refs_0_ = bf16[16,1280]{1,0:T(8,128)(2,1)S(1)} collective-permute-done((bf16[16,1280]{1,0:T(8,128)(2,1)S(1)}, bf16[16,1280]{1,0:T(8,128)(2,1)S(1)}, u32[]{:S(2)}, u32[]{:S(2)}) %collective-permute-start.4) | collective-permute-done | bytes 40992 | tf_op jit(solution)/shard_map/ppermute | solution.py:45
  13.0 0.4 %main.1 = (bf16[128,256]{1,0:T(8,128)(2,1)S(1)}, bf16[128,256]{1,0:T(8,128)(2,1)S(1)}, f32[128,256]{1,0:T(8,128)S(1)}, bf16[2,192,160]{2,1,0:T(8,128)(2,1)S(1)}) custom-call(f32[2,192,160]{2,1,0:T(8,128)S(1)} %get-tuple-element.48.prob, bf16[2,192,160]{2,1,0:T(8,128)(2,1)S(1)} %get-tuple-element.49.low, bf16[2,160,128]{2,1,0:T(8,128)(2,1)S(1)} %get-tuple-element.50.queries, ...), custom_call_target="tpu_custom_call" | custom-call | tf_op jit(solution)/shard_map/main/pallas_call | solution.py:361
  13.4 1.5 %collective-permute-start.6 = (bf16[128,256]{1,0:T(8,128)(2,1)S(1)}, bf16[128,256]{1,0:T(8,128)(2,1)S(1)}, u32[]{:S(2)}, u32[]{:S(2)}) collective-permute-start(bf16[128,256]{1,0:T(8,128)(2,1)S(1)} %get-tuple-element.59), channel_id=1, source_target_pairs={{0,24},{4,28},{8,0},{12,4},{16,8},{20,12},{24,16},{28,20},{1,25},{... | collective-permute-start | bytes 196616 | tf_op jit(solution)/shard_map/ppermute | solution.py:26
  14.8 0.2 query.3
  15.1 1.9 %collective-permute-start.11 = (bf16[16,1280]{1,0:T(8,128)(2,1)S(1)}, bf16[16,1280]{1,0:T(8,128)(2,1)S(1)}, u32[]{:S(2)}, u32[]{:S(2)}) collective-permute-start(bf16[16,1280]{1,0:T(8,128)(2,1)S(1)} %get-tuple-element.65), channel_id=1, source_target_pairs={{0,2},{1,3},{2,0},{3,1},{4,6},{5,7},{6,4},{7,5},{8,10},{9,11},{10,... | collective-permute-start | bytes 122888 | tf_op jit(solution)/shard_map/ppermute | solution.py:45
  17.0 0.8 %collective-permute-start.12 = (bf16[16,1280]{1,0:T(8,128)(2,1)S(1)}, bf16[16,1280]{1,0:T(8,128)(2,1)S(1)}, u32[]{:S(2)}, u32[]{:S(2)}) collective-permute-start(bf16[16,1280]{1,0:T(8,128)(2,1)S(1)} %get-tuple-element.66), channel_id=1, source_target_pairs={{0,1},{1,0},{2,3},{3,2},{4,5},{5,4},{6,7},{7,6},{8,9},{9,8},{10,11... | collective-permute-start | bytes 122888 | tf_op jit(solution)/shard_map/ppermute | solution.py:45
  17.9 1.9 %collective-permute-start.8 = (bf16[16,1792]{1,0:T(8,128)(2,1)S(1)}, bf16[16,1792]{1,0:T(8,128)(2,1)S(1)}, u32[]{:S(2)}, u32[]{:S(2)}) collective-permute-start(bf16[16,1792]{1,0:T(8,128)(2,1)S(1)} %get-tuple-element.61), channel_id=1, source_target_pairs={{0,3},{1,2},{2,1},{3,0},{4,7},{5,6},{6,5},{7,4},{8,11},{9,10},{10,... | collective-permute-start | bytes 172040 | tf_op jit(solution)/shard_map/ppermute | solution.py:45
  19.8 0.0 collective-permute-start.9
  19.8 2.5 %collective-permute-start.10 = (bf16[16,512]{1,0:T(8,128)(2,1)S(1)}, bf16[16,512]{1,0:T(8,128)(2,1)S(1)}, u32[]{:S(2)}, u32[]{:S(2)}) collective-permute-start(bf16[16,512]{1,0:T(8,128)(2,1)S(1)} %get-tuple-element.63), channel_id=1, source_target_pairs={{0,2},{1,3},{2,0},{3,1},{4,6},{5,7},{6,4},{7,5},{8,10},{9,11},{10,... | collective-permute-start | bytes 49160 | tf_op jit(solution)/shard_map/ppermute | solution.py:45
  22.4 2.2 %collective-permute-done.9.refs_1_ = bf16[16,512]{1,0:T(8,128)(2,1)S(1)} collective-permute-done((bf16[16,512]{1,0:T(8,128)(2,1)S(1)}, bf16[16,512]{1,0:T(8,128)(2,1)S(1)}, u32[]{:S(2)}, u32[]{:S(2)}) %collective-permute-start.9) | collective-permute-done | bytes 16416 | tf_op jit(solution)/shard_map/ppermute | solution.py:45
  24.6 0.8 %place.1 = (bf16[16,5120]{1,0:T(8,128)(2,1)}, bf16[16,1024]{1,0:T(8,128)(2,1)}, bf16[16,1024]{1,0:T(8,128)(2,1)}) custom-call(bf16[16,1792]{1,0:T(8,128)(2,1)S(1)} %collective-permute-done.8.refs_0_, bf16[16,512]{1,0:T(8,128)(2,1)S(1)} %collective-permute-done.9.refs_1_, bf16[16,512]{1,0:T(8,128)(2,1)S(1)} %collective-permute-done.10.refs_2_, ...), custom_call_target="tpu_custom_call" | custom-call | tf_op jit(solution)/shard_map/place/pallas_call | solution.py:404
  (17 shorter events, 0.1 us)
Async XLA Ops:
  1.6 7.2 %collective-permute-start = (bf16[128,256]{1,0:T(8,128)(2,1)S(1)}, bf16[128,256]{1,0:T(8,128)(2,1)S(1)}, u32[]{:S(2)}, u32[]{:S(2)}) collective-permute-start(bf16[128,256]{1,0:T(8,128)(2,1)S(1)} %get-tuple-element.36.own.kv), channel_id=1, source_target_pairs={{0,8},{4,12},{8,16},{12,20},{16,24},{20,28},{24,0},{28,4},{1,9},{5... | collective-permute-start | bytes 196616 | tf_op jit(solution)/shard_map/ppermute | solution.py:26
  4.6 5.9 %collective-permute-start.3 = (bf16[16,1280]{1,0:T(8,128)(2,1)S(1)}, bf16[16,1280]{1,0:T(8,128)(2,1)S(1)}, u32[]{:S(2)}, u32[]{:S(2)}) collective-permute-start(bf16[16,1280]{1,0:T(8,128)(2,1)S(1)} %get-tuple-element.46), channel_id=1, source_target_pairs={{0,2},{1,3},{2,0},{3,1},{4,6},{5,7},{6,4},{7,5},{8,10},{9,11},{10,... | collective-permute-start | bytes 122888 | tf_op jit(solution)/shard_map/ppermute | solution.py:45
  7.2 5.8 %collective-permute-start.4 = (bf16[16,1280]{1,0:T(8,128)(2,1)S(1)}, bf16[16,1280]{1,0:T(8,128)(2,1)S(1)}, u32[]{:S(2)}, u32[]{:S(2)}) collective-permute-start(bf16[16,1280]{1,0:T(8,128)(2,1)S(1)} %get-tuple-element.54), channel_id=1, source_target_pairs={{0,3},{1,2},{2,1},{3,0},{4,7},{5,6},{6,5},{7,4},{8,11},{9,10},{10,... | collective-permute-start | bytes 122888 | tf_op jit(solution)/shard_map/ppermute | solution.py:45
  8.5 1.5 %copy-start = (bf16[64,1280]{1,0:T(8,128)(2,1)S(1)}, bf16[64,1280]{1,0:T(8,128)(2,1)}, u32[]{:S(2)}) copy-start(bf16[64,1280]{1,0:T(8,128)(2,1)} %query.2) | copy-start | bytes 491524
  8.5 1.5 %copy-start.1 = (bf16[64,1280]{1,0:T(8,128)(2,1)S(1)}, bf16[64,1280]{1,0:T(8,128)(2,1)}, u32[]{:S(2)}) copy-start(bf16[64,1280]{1,0:T(8,128)(2,1)} %output.1) | copy-start | bytes 491524
  8.5 4.5 %collective-permute-start.5 = (bf16[16,1280]{1,0:T(8,128)(2,1)S(1)}, bf16[16,1280]{1,0:T(8,128)(2,1)S(1)}, u32[]{:S(2)}, u32[]{:S(2)}) collective-permute-start(bf16[16,1280]{1,0:T(8,128)(2,1)S(1)} %get-tuple-element.55), channel_id=1, source_target_pairs={{0,1},{1,0},{2,3},{3,2},{4,5},{5,4},{6,7},{7,6},{8,9},{9,8},{10,11... | collective-permute-start | bytes 122888 | tf_op jit(solution)/shard_map/ppermute | solution.py:45
  8.7 1.3 %copy-start.2 = (f32[10,64]{1,0:T(8,128)S(1)}, f32[10,64]{1,0:T(8,128)}, u32[]{:S(2)}) copy-start(f32[10,64]{1,0:T(8,128)} %lse.1) | copy-start | bytes 7684
  8.8 1.3 %collective-permute-start.1 = (bf16[64,256]{1,0:T(8,128)(2,1)S(1)}, bf16[64,256]{1,0:T(8,128)(2,1)S(1)}, u32[]{:S(2)}, u32[]{:S(2)}) collective-permute-start(bf16[64,256]{1,0:T(8,128)(2,1)S(1)} %get-tuple-element.37), channel_id=1, source_target_pairs={{0,4},{4,0},{8,12},{12,8},{16,20},{20,16},{24,28},{28,24},{1,5},{5... | collective-permute-start | bytes 98312 | tf_op jit(solution)/shard_map/ppermute | solution.py:330
  8.8 1.6 %collective-permute-start.2 = (bf16[64,256]{1,0:T(8,128)(2,1)S(1)}, bf16[64,256]{1,0:T(8,128)(2,1)S(1)}, u32[]{:S(2)}, u32[]{:S(2)}) collective-permute-start(bf16[64,256]{1,0:T(8,128)(2,1)S(1)} %get-tuple-element.44), channel_id=1, source_target_pairs={{0,4},{4,0},{8,12},{12,8},{16,20},{20,16},{24,28},{28,24},{1,5},{5... | collective-permute-start | bytes 98312 | tf_op jit(solution)/shard_map/ppermute | solution.py:330
  13.4 4.5 %collective-permute-start.6 = (bf16[128,256]{1,0:T(8,128)(2,1)S(1)}, bf16[128,256]{1,0:T(8,128)(2,1)S(1)}, u32[]{:S(2)}, u32[]{:S(2)}) collective-permute-start(bf16[128,256]{1,0:T(8,128)(2,1)S(1)} %get-tuple-element.59), channel_id=1, source_target_pairs={{0,24},{4,28},{8,0},{12,4},{16,8},{20,12},{24,16},{28,20},{1,25},{... | collective-permute-start | bytes 196616 | tf_op jit(solution)/shard_map/ppermute | solution.py:26
  14.8 3.0 %collective-permute-start.7 = (bf16[128,256]{1,0:T(8,128)(2,1)S(1)}, bf16[128,256]{1,0:T(8,128)(2,1)S(1)}, u32[]{:S(2)}, u32[]{:S(2)}) collective-permute-start(bf16[128,256]{1,0:T(8,128)(2,1)S(1)} %get-tuple-element.60), channel_id=1, source_target_pairs={{0,28},{4,0},{8,4},{12,8},{16,12},{20,16},{24,20},{28,24},{1,29},{... | collective-permute-start | bytes 196616 | tf_op jit(solution)/shard_map/ppermute | solution.py:26
  15.1 7.2 %collective-permute-start.11 = (bf16[16,1280]{1,0:T(8,128)(2,1)S(1)}, bf16[16,1280]{1,0:T(8,128)(2,1)S(1)}, u32[]{:S(2)}, u32[]{:S(2)}) collective-permute-start(bf16[16,1280]{1,0:T(8,128)(2,1)S(1)} %get-tuple-element.65), channel_id=1, source_target_pairs={{0,2},{1,3},{2,0},{3,1},{4,6},{5,7},{6,4},{7,5},{8,10},{9,11},{10,... | collective-permute-start | bytes 122888 | tf_op jit(solution)/shard_map/ppermute | solution.py:45
  17.0 5.4 %collective-permute-start.12 = (bf16[16,1280]{1,0:T(8,128)(2,1)S(1)}, bf16[16,1280]{1,0:T(8,128)(2,1)S(1)}, u32[]{:S(2)}, u32[]{:S(2)}) collective-permute-start(bf16[16,1280]{1,0:T(8,128)(2,1)S(1)} %get-tuple-element.66), channel_id=1, source_target_pairs={{0,1},{1,0},{2,3},{3,2},{4,5},{5,4},{6,7},{7,6},{8,9},{9,8},{10,11... | collective-permute-start | bytes 122888 | tf_op jit(solution)/shard_map/ppermute | solution.py:45
  17.9 6.7 %collective-permute-start.8 = (bf16[16,1792]{1,0:T(8,128)(2,1)S(1)}, bf16[16,1792]{1,0:T(8,128)(2,1)S(1)}, u32[]{:S(2)}, u32[]{:S(2)}) collective-permute-start(bf16[16,1792]{1,0:T(8,128)(2,1)S(1)} %get-tuple-element.61), channel_id=1, source_target_pairs={{0,3},{1,2},{2,1},{3,0},{4,7},{5,6},{6,5},{7,4},{8,11},{9,10},{10,... | collective-permute-start | bytes 172040 | tf_op jit(solution)/shard_map/ppermute | solution.py:45
  19.8 4.8 %collective-permute-start.9 = (bf16[16,512]{1,0:T(8,128)(2,1)S(1)}, bf16[16,512]{1,0:T(8,128)(2,1)S(1)}, u32[]{:S(2)}, u32[]{:S(2)}) collective-permute-start(bf16[16,512]{1,0:T(8,128)(2,1)S(1)} %get-tuple-element.62), channel_id=1, source_target_pairs={{0,1},{1,0},{2,3},{3,2},{4,5},{5,4},{6,7},{7,6},{8,9},{9,8},{10,11... | collective-permute-start | bytes 49160 | tf_op jit(solution)/shard_map/ppermute | solution.py:45
  19.8 4.8 %collective-permute-start.10 = (bf16[16,512]{1,0:T(8,128)(2,1)S(1)}, bf16[16,512]{1,0:T(8,128)(2,1)S(1)}, u32[]{:S(2)}, u32[]{:S(2)}) collective-permute-start(bf16[16,512]{1,0:T(8,128)(2,1)S(1)} %get-tuple-element.63), channel_id=1, source_target_pairs={{0,2},{1,3},{2,0},{3,1},{4,6},{5,7},{6,4},{7,5},{8,10},{9,11},{10,... | collective-permute-start | bytes 49160 | tf_op jit(solution)/shard_map/ppermute | solution.py:45

commit v9 on v8

--- a/solution.py
+++ b/solution.py
@@ -79,6 +79,10 @@
 def turns(n):
     first = [0, n // 2] if n > 2 else [0]
     return first, [step for step in range(n - 1, 0, -1) if step not in first]
+
+
+def ready(n):
+    return [step for step in AHEAD if is_power(n) and step in turns(n)[0]]
 
 
 def closing(n):
@@ -178,8 +182,9 @@
     return stacked, scores
 
 
-def first_kernel(prob, low, queries, outputs, values, near_value, keys, *refs):
-    pieces, (dq, dk, dv) = refs[:-3], refs[-3:]
+def first_kernel(n, prob, low, queries, outputs, values, near_value, keys, *refs):
+    steps = turns(n)[0]
+    pieces, (dq, dk, dv, *sends) = refs[: len(steps)], refs[len(steps) :]
     stacked, scores = score_grads(prob, outputs, values, near_value, pieces)
     rows = pieces[0].shape[0]
     for g in range(prob.shape[0]):
@@ -192,6 +197,8 @@
                 dq[pl.ds(index * rows, rows), pl.ds((g * GROUP + h) * HEAD_DIM, HEAD_DIM)] = (
                     query_rows[start : start + rows]
                 )
+    for step, send in zip(ready(n), sends):
+        send[...] = dq[pl.ds(steps.index(step) * rows, rows), :]
 
 
 def main_kernel(prob, low, queries, outputs, values, near_value, dk_first, dv_first, *refs):
@@ -229,7 +236,7 @@
                 out[pl.ds(start, rows), pl.ds((g * GROUP + h) * HEAD_DIM, HEAD_DIM)] = dq[
                     at : at + rows
                 ]
-    for step, send in zip(AHEAD, sends):
+    for step, send in zip([step for step in AHEAD if step not in ready(n)], sends):
         start = pl.multiple_of(partner(me, step, n) * rows, rows)
         send[...] = out[pl.ds(start, rows), :]
 
@@ -351,10 +358,11 @@
     first, last = ([received[step] for step in steps] for steps in turns(n))
     part = shape((kv_local, key_rows, HEAD_DIM), jnp.float32)
     dq_first, *parts_first = pl.pallas_call(
-        first_kernel,
-        out_shape=[shape((len(first) * rows, width)), part, part],
+        functools.partial(first_kernel, n),
+        out_shape=[shape((len(first) * rows, width)), part, part]
+        + [shape((rows, width))] * len(ready(n)),
         in_specs=[VMEM] * (7 + len(first)),
-        out_specs=[VMEM] * 3,
+        out_specs=[VMEM] * (3 + len(ready(n))),
         compiler_params=PARAMS,
         name="first",
     )(*sides[:4], values, near_value, keys, *first)
@@ -369,17 +377,21 @@
         out_specs=[VMEM] * (STEPS + 1),
         compiler_params=PARAMS,
         name="main",
-    )(*sides[4:], values, near_value, *parts_first, *last)
+    )(*sides[4:], values, near_value, *parts_first[:2], *last)
     back = [shifted(far[i - 1], "blk", -i) for i in range(STEPS - 1, 0, -1)]
     dq, *ahead = pl.pallas_call(
         functools.partial(query_kernel, n),
-        out_shape=[shape((tokens, width))] + [shape((rows, width))] * len(AHEAD),
+        out_shape=[shape((tokens, width))] + [shape((rows, width))] * (len(AHEAD) - len(ready(n))),
         in_specs=[VMEM] * 3,
-        out_specs=[VMEM] * (1 + len(AHEAD)),
+        out_specs=[VMEM] * (1 + len(AHEAD) - len(ready(n))),
         compiler_params=PARAMS,
         name="query",
     )(keys, dq_first, dscore)
-    ahead = [exchange(a, "uly", step) for a, step in zip(ahead, AHEAD)]
+    early_sends, later_sends = iter(parts_first[2:]), iter(ahead)
+    ahead = [
+        exchange(next(early_sends if step in ready(n) else later_sends), "uly", step)
+        for step in AHEAD
+    ]
     *parts, = pl.pallas_call(
         functools.partial(sum_kernel, n),
         out_shape=[

time: 25.6 us -> 25.6 us (level)
  transfers between devices with their start and end apart: 13 -> 13, of which waited for: 3 -> 3; matrix products, arithmetic and copies ran while one was open for 0% -> 0% of each run, Pallas kernels for 5% -> 4%
where the time goes in v9:
time: 25.6 us; the launch traced here: 25.4 us
  starting transfers between devices  16.4 us (64%)
  waiting for transfers between devices  4.96 us (19%)
  Pallas kernels  3.26 us (13%)
  between operations  0.71 us (3%)
    ppermute x8, starting transfers between devices, exchange(): return lax.ppermute(array, axis, pairs)  11.4 us
    ppermute x3, starting transfers between devices, shifted(): lax.ppermute(array, axis, [(i, (i + by) % size) for i in range(size)])  4.48 us
    ppermute x8, waiting for transfers between devices, exchange(): return lax.ppermute(array, axis, pairs)  4.25 us
    pallas_call x1, Pallas kernels, body(): pl.pallas_call(functools.partial(prep_kernel, n), out_shape=[shape((rows,...  0.93 us
    pallas_call x1, Pallas kernels, body(): pl.pallas_call(functools.partial(place_kernel, n), out_shape=[shape((rows...  0.79 us
    ppermute x2, waiting for transfers between devices, body(): near_key, near_value = [lax.ppermute(a, 'blk', swap) for a in passed]  0.7 us
    ppermute x2, starting transfers between devices, body(): near_key, near_value = [lax.ppermute(a, 'blk', swap) for a in passed]  0.57 us
  transfers between devices with their start and end apart: 13, of which 3 were waited for; matrix products, arithmetic and copies ran while one was open for 0% of the time, Pallas kernels for 4%

profile of v9, /device:TPU:0, one launch (start us, length us, event | category | flops | bytes accessed | tf_op | source)
XLA Modules:
  0.0 25.4 jit_solution(15185033633802515721)
XLA Ops:
  0.6 0.9 %prep.1 = (bf16[16,1280]{1,0:T(8,128)(2,1)S(1)}, bf16[16,1280]{1,0:T(8,128)(2,1)S(1)}, bf16[16,1280]{1,0:T(8,128)(2,1)S(1)}, bf16[16,1280]{1,0:T(8,128)(2,1)S(1)}, bf16[128,256]{1,0:T(8,128)(2,1)S(1)}) custom-call(bf16[16,5120]{1,0:T(8,128)(2,1)} %grad.1, bf16[64,256]{1,0:T(8,128)(2,1)} %key.1, bf16[64,256]{1,0:T(8,128)(2,1)} %value.1), custom_call_target="tpu_custom_call" | custom-call | tf_op jit(solution)/shard_map/prep/pallas_call | solution.py:316
  1.6 3.0 %collective-permute-start = (bf16[128,256]{1,0:T(8,128)(2,1)S(1)}, bf16[128,256]{1,0:T(8,128)(2,1)S(1)}, u32[]{:S(2)}, u32[]{:S(2)}) collective-permute-start(bf16[128,256]{1,0:T(8,128)(2,1)S(1)} %get-tuple-element.36.own.kv), channel_id=1, source_target_pairs={{0,8},{4,12},{8,16},{12,20},{16,24},{20,28},{24,0},{28,4},{1,9},{5... | collective-permute-start | bytes 196616 | tf_op jit(solution)/shard_map/ppermute | solution.py:26
  4.6 2.6 %collective-permute-start.3 = (bf16[16,1280]{1,0:T(8,128)(2,1)S(1)}, bf16[16,1280]{1,0:T(8,128)(2,1)S(1)}, u32[]{:S(2)}, u32[]{:S(2)}) collective-permute-start(bf16[16,1280]{1,0:T(8,128)(2,1)S(1)} %get-tuple-element.46), channel_id=1, source_target_pairs={{0,2},{1,3},{2,0},{3,1},{4,6},{5,7},{6,4},{7,5},{8,10},{9,11},{10,... | collective-permute-start | bytes 122888 | tf_op jit(solution)/shard_map/ppermute | solution.py:45
  7.2 1.3 %collective-permute-start.4 = (bf16[16,1280]{1,0:T(8,128)(2,1)S(1)}, bf16[16,1280]{1,0:T(8,128)(2,1)S(1)}, u32[]{:S(2)}, u32[]{:S(2)}) collective-permute-start(bf16[16,1280]{1,0:T(8,128)(2,1)S(1)} %get-tuple-element.54), channel_id=1, source_target_pairs={{0,3},{1,2},{2,1},{3,0},{4,7},{5,6},{6,5},{7,4},{8,11},{9,10},{10,... | collective-permute-start | bytes 122888 | tf_op jit(solution)/shard_map/ppermute | solution.py:45
  8.5 0.2 collective-permute-start.5
  8.7 0.0 collective-permute-done.pair.refs_0_
  8.8 0.1 collective-permute-start.1
  8.8 0.5 %collective-permute-start.2 = (bf16[64,256]{1,0:T(8,128)(2,1)S(1)}, bf16[64,256]{1,0:T(8,128)(2,1)S(1)}, u32[]{:S(2)}, u32[]{:S(2)}) collective-permute-start(bf16[64,256]{1,0:T(8,128)(2,1)S(1)} %get-tuple-element.44), channel_id=1, source_target_pairs={{0,4},{4,0},{8,12},{12,8},{16,20},{20,16},{24,28},{28,24},{1,5},{5... | collective-permute-start | bytes 98312 | tf_op jit(solution)/shard_map/ppermute | solution.py:337
  9.3 0.7 %collective-permute-done.1.near_key = bf16[64,256]{1,0:T(8,128)(2,1)S(1)} collective-permute-done((bf16[64,256]{1,0:T(8,128)(2,1)S(1)}, bf16[64,256]{1,0:T(8,128)(2,1)S(1)}, u32[]{:S(2)}, u32[]{:S(2)}) %collective-permute-start.1) | collective-permute-done | bytes 32800 | tf_op jit(solution)/shard_map/ppermute | solution.py:337
  10.0 0.4 %early.1 = (bf16[2,192,128]{2,1,0:T(8,128)(2,1)S(1)}, bf16[2,192,128]{2,1,0:T(8,128)(2,1)S(1)}, f32[2,192,160]{2,1,0:T(8,128)S(1)}, bf16[2,192,160]{2,1,0:T(8,12...) custom-call(bf16[64,1280]{1,0:T(8,128)(2,1)S(1)} %copy-done, ...), custom_call_target="tpu_custom_call" | custom-call | tf_op jit(solution)/shard_map/early/pallas_call | solution.py:339
  10.4 0.0 collective-permute-done.3.refs_1_
  10.4 0.0 collective-permute-done.2.near_value
  10.4 0.5 %first.1 = (bf16[32,1280]{1,0:T(8,128)(2,1)S(1)}, f32[2,192,128]{2,1,0:T(8,128)S(1)}, f32[2,192,128]{2,1,0:T(8,128)S(1)}, bf16[16,1280]{1,0:T(8,128)(2,1)S(1)}) custom-call(f32[2,192,160]{2,1,0:T(8,128)S(1)} %get-tuple-element.39.prob, bf16[2,192,160]{2,1,0:T(8,128)(2,1)S(1)} %get-tuple-element.40.low, bf16[2,160,128]{2,1,0:T(8,128)(2,1)S(1)} %get-tuple-element.41.queries, ...), custom_call_target="tpu_custom_call" | custom-call | tf_op jit(solution)/shard_map/first/pallas_call | solution.py:360
  10.9 2.0 %collective-permute-done.4.refs_0_ = bf16[16,1280]{1,0:T(8,128)(2,1)S(1)} collective-permute-done((bf16[16,1280]{1,0:T(8,128)(2,1)S(1)}, bf16[16,1280]{1,0:T(8,128)(2,1)S(1)}, u32[]{:S(2)}, u32[]{:S(2)}) %collective-permute-start.4) | collective-permute-done | bytes 40992 | tf_op jit(solution)/shard_map/ppermute | solution.py:45
  13.0 0.4 %main.1 = (bf16[128,256]{1,0:T(8,128)(2,1)S(1)}, bf16[128,256]{1,0:T(8,128)(2,1)S(1)}, f32[128,256]{1,0:T(8,128)S(1)}, bf16[2,192,160]{2,1,0:T(8,128)(2,1)S(1)}) custom-call(f32[2,192,160]{2,1,0:T(8,128)S(1)} %get-tuple-element.48.prob, bf16[2,192,160]{2,1,0:T(8,128)(2,1)S(1)} %get-tuple-element.49.low, bf16[2,160,128]{2,1,0:T(8,128)(2,1)S(1)} %get-tuple-element.50.queries, ...), custom_call_target="tpu_custom_call" | custom-call | tf_op jit(solution)/shard_map/main/pallas_call | solution.py:369
  13.4 1.5 %collective-permute-start.6 = (bf16[128,256]{1,0:T(8,128)(2,1)S(1)}, bf16[128,256]{1,0:T(8,128)(2,1)S(1)}, u32[]{:S(2)}, u32[]{:S(2)}) collective-permute-start(bf16[128,256]{1,0:T(8,128)(2,1)S(1)} %get-tuple-element.59), channel_id=1, source_target_pairs={{0,24},{4,28},{8,0},{12,4},{16,8},{20,12},{24,16},{28,20},{1,25},{... | collective-permute-start | bytes 196616 | tf_op jit(solution)/shard_map/ppermute | solution.py:26
  14.8 0.0 collective-permute-start.7
  14.8 0.2 query.3
  15.1 0.9 %collective-permute-start.12 = (bf16[16,1280]{1,0:T(8,128)(2,1)S(1)}, bf16[16,1280]{1,0:T(8,128)(2,1)S(1)}, u32[]{:S(2)}, u32[]{:S(2)}) collective-permute-start(bf16[16,1280]{1,0:T(8,128)(2,1)S(1)} %get-tuple-element.66), channel_id=1, source_target_pairs={{0,1},{1,0},{2,3},{3,2},{4,5},{5,4},{6,7},{7,6},{8,9},{9,8},{10,11... | collective-permute-start | bytes 122888 | tf_op jit(solution)/shard_map/ppermute | solution.py:45
  16.0 1.9 %collective-permute-start.11 = (bf16[16,1280]{1,0:T(8,128)(2,1)S(1)}, bf16[16,1280]{1,0:T(8,128)(2,1)S(1)}, u32[]{:S(2)}, u32[]{:S(2)}) collective-permute-start(bf16[16,1280]{1,0:T(8,128)(2,1)S(1)} %get-tuple-element.65), channel_id=1, source_target_pairs={{0,2},{1,3},{2,0},{3,1},{4,6},{5,7},{6,4},{7,5},{8,10},{9,11},{10,... | collective-permute-start | bytes 122888 | tf_op jit(solution)/shard_map/ppermute | solution.py:45
  17.9 1.9 %collective-permute-start.8 = (bf16[16,1792]{1,0:T(8,128)(2,1)S(1)}, bf16[16,1792]{1,0:T(8,128)(2,1)S(1)}, u32[]{:S(2)}, u32[]{:S(2)}) collective-permute-start(bf16[16,1792]{1,0:T(8,128)(2,1)S(1)} %get-tuple-element.61), channel_id=1, source_target_pairs={{0,3},{1,2},{2,1},{3,0},{4,7},{5,6},{6,5},{7,4},{8,11},{9,10},{10,... | collective-permute-start | bytes 172040 | tf_op jit(solution)/shard_map/ppermute | solution.py:45
  19.8 2.5 %collective-permute-start.10 = (bf16[16,512]{1,0:T(8,128)(2,1)S(1)}, bf16[16,512]{1,0:T(8,128)(2,1)S(1)}, u32[]{:S(2)}, u32[]{:S(2)}) collective-permute-start(bf16[16,512]{1,0:T(8,128)(2,1)S(1)} %get-tuple-element.63), channel_id=1, source_target_pairs={{0,2},{1,3},{2,0},{3,1},{4,6},{5,7},{6,4},{7,5},{8,10},{9,11},{10,... | collective-permute-start | bytes 49160 | tf_op jit(solution)/shard_map/ppermute | solution.py:45
  22.4 2.2 %collective-permute-done.9.refs_1_ = bf16[16,512]{1,0:T(8,128)(2,1)S(1)} collective-permute-done((bf16[16,512]{1,0:T(8,128)(2,1)S(1)}, bf16[16,512]{1,0:T(8,128)(2,1)S(1)}, u32[]{:S(2)}, u32[]{:S(2)}) %collective-permute-start.9) | collective-permute-done | bytes 16416 | tf_op jit(solution)/shard_map/ppermute | solution.py:45
  24.6 0.8 %place.1 = (bf16[16,5120]{1,0:T(8,128)(2,1)}, bf16[16,1024]{1,0:T(8,128)(2,1)}, bf16[16,1024]{1,0:T(8,128)(2,1)}) custom-call(bf16[16,1792]{1,0:T(8,128)(2,1)S(1)} %collective-permute-done.8.refs_0_, bf16[16,512]{1,0:T(8,128)(2,1)S(1)} %collective-permute-done.9.refs_1_, bf16[16,512]{1,0:T(8,128)(2,1)S(1)} %collective-permute-done.10.refs_2_, ...), custom_call_target="tpu_custom_call" | custom-call | tf_op jit(solution)/shard_map/place/pallas_call | solution.py:416
  (17 shorter events, 0.1 us)
Async XLA Ops:
  1.6 7.2 %collective-permute-start = (bf16[128,256]{1,0:T(8,128)(2,1)S(1)}, bf16[128,256]{1,0:T(8,128)(2,1)S(1)}, u32[]{:S(2)}, u32[]{:S(2)}) collective-permute-start(bf16[128,256]{1,0:T(8,128)(2,1)S(1)} %get-tuple-element.36.own.kv), channel_id=1, source_target_pairs={{0,8},{4,12},{8,16},{12,20},{16,24},{20,28},{24,0},{28,4},{1,9},{5... | collective-permute-start | bytes 196616 | tf_op jit(solution)/shard_map/ppermute | solution.py:26
  4.6 5.9 %collective-permute-start.3 = (bf16[16,1280]{1,0:T(8,128)(2,1)S(1)}, bf16[16,1280]{1,0:T(8,128)(2,1)S(1)}, u32[]{:S(2)}, u32[]{:S(2)}) collective-permute-start(bf16[16,1280]{1,0:T(8,128)(2,1)S(1)} %get-tuple-element.46), channel_id=1, source_target_pairs={{0,2},{1,3},{2,0},{3,1},{4,6},{5,7},{6,4},{7,5},{8,10},{9,11},{10,... | collective-permute-start | bytes 122888 | tf_op jit(solution)/shard_map/ppermute | solution.py:45
  7.2 5.8 %collective-permute-start.4 = (bf16[16,1280]{1,0:T(8,128)(2,1)S(1)}, bf16[16,1280]{1,0:T(8,128)(2,1)S(1)}, u32[]{:S(2)}, u32[]{:S(2)}) collective-permute-start(bf16[16,1280]{1,0:T(8,128)(2,1)S(1)} %get-tuple-element.54), channel_id=1, source_target_pairs={{0,3},{1,2},{2,1},{3,0},{4,7},{5,6},{6,5},{7,4},{8,11},{9,10},{10,... | collective-permute-start | bytes 122888 | tf_op jit(solution)/shard_map/ppermute | solution.py:45
  8.5 1.5 %copy-start = (bf16[64,1280]{1,0:T(8,128)(2,1)S(1)}, bf16[64,1280]{1,0:T(8,128)(2,1)}, u32[]{:S(2)}) copy-start(bf16[64,1280]{1,0:T(8,128)(2,1)} %query.2) | copy-start | bytes 491524
  8.5 1.5 %copy-start.1 = (bf16[64,1280]{1,0:T(8,128)(2,1)S(1)}, bf16[64,1280]{1,0:T(8,128)(2,1)}, u32[]{:S(2)}) copy-start(bf16[64,1280]{1,0:T(8,128)(2,1)} %output.1) | copy-start | bytes 491524
  8.5 4.5 %collective-permute-start.5 = (bf16[16,1280]{1,0:T(8,128)(2,1)S(1)}, bf16[16,1280]{1,0:T(8,128)(2,1)S(1)}, u32[]{:S(2)}, u32[]{:S(2)}) collective-permute-start(bf16[16,1280]{1,0:T(8,128)(2,1)S(1)} %get-tuple-element.55), channel_id=1, source_target_pairs={{0,1},{1,0},{2,3},{3,2},{4,5},{5,4},{6,7},{7,6},{8,9},{9,8},{10,11... | collective-permute-start | bytes 122888 | tf_op jit(solution)/shard_map/ppermute | solution.py:45
  8.7 1.3 %copy-start.2 = (f32[10,64]{1,0:T(8,128)S(1)}, f32[10,64]{1,0:T(8,128)}, u32[]{:S(2)}) copy-start(f32[10,64]{1,0:T(8,128)} %lse.1) | copy-start | bytes 7684
  8.8 1.3 %collective-permute-start.1 = (bf16[64,256]{1,0:T(8,128)(2,1)S(1)}, bf16[64,256]{1,0:T(8,128)(2,1)S(1)}, u32[]{:S(2)}, u32[]{:S(2)}) collective-permute-start(bf16[64,256]{1,0:T(8,128)(2,1)S(1)} %get-tuple-element.37), channel_id=1, source_target_pairs={{0,4},{4,0},{8,12},{12,8},{16,20},{20,16},{24,28},{28,24},{1,5},{5... | collective-permute-start | bytes 98312 | tf_op jit(solution)/shard_map/ppermute | solution.py:337
  8.8 1.6 %collective-permute-start.2 = (bf16[64,256]{1,0:T(8,128)(2,1)S(1)}, bf16[64,256]{1,0:T(8,128)(2,1)S(1)}, u32[]{:S(2)}, u32[]{:S(2)}) collective-permute-start(bf16[64,256]{1,0:T(8,128)(2,1)S(1)} %get-tuple-element.44), channel_id=1, source_target_pairs={{0,4},{4,0},{8,12},{12,8},{16,20},{20,16},{24,28},{28,24},{1,5},{5... | collective-permute-start | bytes 98312 | tf_op jit(solution)/shard_map/ppermute | solution.py:337
  13.4 4.5 %collective-permute-start.6 = (bf16[128,256]{1,0:T(8,128)(2,1)S(1)}, bf16[128,256]{1,0:T(8,128)(2,1)S(1)}, u32[]{:S(2)}, u32[]{:S(2)}) collective-permute-start(bf16[128,256]{1,0:T(8,128)(2,1)S(1)} %get-tuple-element.59), channel_id=1, source_target_pairs={{0,24},{4,28},{8,0},{12,4},{16,8},{20,12},{24,16},{28,20},{1,25},{... | collective-permute-start | bytes 196616 | tf_op jit(solution)/shard_map/ppermute | solution.py:26
  14.8 3.0 %collective-permute-start.7 = (bf16[128,256]{1,0:T(8,128)(2,1)S(1)}, bf16[128,256]{1,0:T(8,128)(2,1)S(1)}, u32[]{:S(2)}, u32[]{:S(2)}) collective-permute-start(bf16[128,256]{1,0:T(8,128)(2,1)S(1)} %get-tuple-element.60), channel_id=1, source_target_pairs={{0,28},{4,0},{8,4},{12,8},{16,12},{20,16},{24,20},{28,24},{1,29},{... | collective-permute-start | bytes 196616 | tf_op jit(solution)/shard_map/ppermute | solution.py:26
  15.1 7.3 %collective-permute-start.12 = (bf16[16,1280]{1,0:T(8,128)(2,1)S(1)}, bf16[16,1280]{1,0:T(8,128)(2,1)S(1)}, u32[]{:S(2)}, u32[]{:S(2)}) collective-permute-start(bf16[16,1280]{1,0:T(8,128)(2,1)S(1)} %get-tuple-element.66), channel_id=1, source_target_pairs={{0,1},{1,0},{2,3},{3,2},{4,5},{5,4},{6,7},{7,6},{8,9},{9,8},{10,11... | collective-permute-start | bytes 122888 | tf_op jit(solution)/shard_map/ppermute | solution.py:45
  16.0 6.4 %collective-permute-start.11 = (bf16[16,1280]{1,0:T(8,128)(2,1)S(1)}, bf16[16,1280]{1,0:T(8,128)(2,1)S(1)}, u32[]{:S(2)}, u32[]{:S(2)}) collective-permute-start(bf16[16,1280]{1,0:T(8,128)(2,1)S(1)} %get-tuple-element.65), channel_id=1, source_target_pairs={{0,2},{1,3},{2,0},{3,1},{4,6},{5,7},{6,4},{7,5},{8,10},{9,11},{10,... | collective-permute-start | bytes 122888 | tf_op jit(solution)/shard_map/ppermute | solution.py:45
  17.9 6.7 %collective-permute-start.8 = (bf16[16,1792]{1,0:T(8,128)(2,1)S(1)}, bf16[16,1792]{1,0:T(8,128)(2,1)S(1)}, u32[]{:S(2)}, u32[]{:S(2)}) collective-permute-start(bf16[16,1792]{1,0:T(8,128)(2,1)S(1)} %get-tuple-element.61), channel_id=1, source_target_pairs={{0,3},{1,2},{2,1},{3,0},{4,7},{5,6},{6,5},{7,4},{8,11},{9,10},{10,... | collective-permute-start | bytes 172040 | tf_op jit(solution)/shard_map/ppermute | solution.py:45
  19.8 4.8 %collective-permute-start.9 = (bf16[16,512]{1,0:T(8,128)(2,1)S(1)}, bf16[16,512]{1,0:T(8,128)(2,1)S(1)}, u32[]{:S(2)}, u32[]{:S(2)}) collective-permute-start(bf16[16,512]{1,0:T(8,128)(2,1)S(1)} %get-tuple-element.62), channel_id=1, source_target_pairs={{0,1},{1,0},{2,3},{3,2},{4,5},{5,4},{6,7},{7,6},{8,9},{9,8},{10,11... | collective-permute-start | bytes 49160 | tf_op jit(solution)/shard_map/ppermute | solution.py:45
  19.8 4.8 %collective-permute-start.10 = (bf16[16,512]{1,0:T(8,128)(2,1)S(1)}, bf16[16,512]{1,0:T(8,128)(2,1)S(1)}, u32[]{:S(2)}, u32[]{:S(2)}) collective-permute-start(bf16[16,512]{1,0:T(8,128)(2,1)S(1)} %get-tuple-element.63), channel_id=1, source_target_pairs={{0,2},{1,3},{2,0},{3,1},{4,6},{5,7},{6,4},{7,5},{8,10},{9,11},{10,... | collective-permute-start | bytes 49160 | tf_op jit(solution)/shard_map/ppermute | solution.py:45

commit v10 on v9

--- a/solution.py
+++ b/solution.py
@@ -149,19 +149,10 @@
         second[...] = own[pl.ds(rows, rows), :]
 
 
-def score_grads(prob, outputs, values, near_value, pieces):
-    tokens = near_value.shape[0]
+def score_grads(prob, outputs, values, pieces):
     heads = range(prob.shape[0])
     stacked, products = [], []
     for g in heads:
-        v = jnp.concatenate(
-            [
-                values[g, pl.ds(0, tokens)],
-                near_value[:, pl.ds(g * HEAD_DIM, HEAD_DIM)],
-                values[g, pl.ds(2 * tokens, (STEPS - 2) * tokens)],
-            ],
-            axis=0,
-        )
         go = jnp.concatenate(
             [
                 piece[:, pl.ds((g * GROUP + h) * HEAD_DIM, HEAD_DIM)]
@@ -171,7 +162,7 @@
             axis=0,
         )
         stacked.append(go)
-        products.append(nt(v, go))
+        products.append(nt(values[g], go))
     deltas = [
         jnp.sum(stacked[g].astype(jnp.float32) * outputs[g].astype(jnp.float32), axis=1)[None, :]
         for g in heads
@@ -184,8 +175,13 @@
 
 def first_kernel(n, prob, low, queries, outputs, values, near_value, keys, *refs):
     steps = turns(n)[0]
-    pieces, (dq, dk, dv, *sends) = refs[: len(steps)], refs[len(steps) :]
-    stacked, scores = score_grads(prob, outputs, values, near_value, pieces)
+    pieces, (joined, dq, dk, dv, *sends) = refs[: len(steps)], refs[len(steps) :]
+    tokens = near_value.shape[0]
+    near = pl.ds(tokens, tokens)
+    for g in range(prob.shape[0]):
+        joined[g] = values[g]
+        joined[g, near] = near_value[:, pl.ds(g * HEAD_DIM, HEAD_DIM)]
+    stacked, scores = score_grads(prob, outputs, joined, pieces)
     rows = pieces[0].shape[0]
     for g in range(prob.shape[0]):
         dk[g] = nn(scores[g], queries[g])
@@ -201,10 +197,10 @@
         send[...] = dq[pl.ds(steps.index(step) * rows, rows), :]
 
 
-def main_kernel(prob, low, queries, outputs, values, near_value, dk_first, dv_first, *refs):
+def main_kernel(prob, low, queries, outputs, values, dk_first, dv_first, *refs):
     pieces, (*far, own, dscore) = refs[: -STEPS - 1], refs[-STEPS - 1 :]
-    tokens = near_value.shape[0]
-    stacked, scores = score_grads(prob, outputs, values, near_value, pieces)
+    tokens = values.shape[1] // STEPS
+    stacked, scores = score_grads(prob, outputs, values, pieces)
     for g in range(prob.shape[0]):
         cols = pl.ds(g * HEAD_DIM, HEAD_DIM)
         dscore[g] = scores[g]
@@ -357,12 +353,12 @@
     received = [slices[0]] + received
     first, last = ([received[step] for step in steps] for steps in turns(n))
     part = shape((kv_local, key_rows, HEAD_DIM), jnp.float32)
-    dq_first, *parts_first = pl.pallas_call(
+    joined, dq_first, *parts_first = pl.pallas_call(
         functools.partial(first_kernel, n),
-        out_shape=[shape((len(first) * rows, width)), part, part]
+        out_shape=[shape(values.shape), shape((len(first) * rows, width)), part, part]
         + [shape((rows, width))] * len(ready(n)),
         in_specs=[VMEM] * (7 + len(first)),
-        out_specs=[VMEM] * (3 + len(ready(n))),
+        out_specs=[VMEM] * (4 + len(ready(n))),
         compiler_params=PARAMS,
         name="first",
     )(*sides[:4], values, near_value, keys, *first)
@@ -373,11 +369,11 @@
             shape((2 * tokens, kv_width), jnp.float32),
             shape((kv_local, key_rows, columns[1])),
         ],
-        in_specs=[VMEM] * (8 + len(last)),
+        in_specs=[VMEM] * (7 + len(last)),
         out_specs=[VMEM] * (STEPS + 1),
         compiler_params=PARAMS,
         name="main",
-    )(*sides[4:], values, near_value, *parts_first[:2], *last)
+    )(*sides[4:], joined, *parts_first[:2], *last)
     back = [shifted(far[i - 1], "blk", -i) for i in range(STEPS - 1, 0, -1)]
     dq, *ahead = pl.pallas_call(
         functools.partial(query_kernel, n),

time: 25.6 us -> 25.6 us (level)
  no operation moved by 1% of the time
where the time goes in v10:
time: 25.6 us; the launch traced here: 25.4 us
  starting transfers between devices  16.4 us (64%)
  waiting for transfers between devices  4.96 us (19%)
  Pallas kernels  3.26 us (13%)
  between operations  0.72 us (3%)
    ppermute x8, starting transfers between devices, exchange(): return lax.ppermute(array, axis, pairs)  11.4 us
    ppermute x3, starting transfers between devices, shifted(): lax.ppermute(array, axis, [(i, (i + by) % size) for i in range(size)])  4.48 us
    ppermute x8, waiting for transfers between devices, exchange(): return lax.ppermute(array, axis, pairs)  4.25 us
    pallas_call x1, Pallas kernels, body(): pl.pallas_call(functools.partial(prep_kernel, n), out_shape=[shape((rows,...  0.93 us
    pallas_call x1, Pallas kernels, body(): pl.pallas_call(functools.partial(place_kernel, n), out_shape=[shape((rows...  0.79 us
    ppermute x2, waiting for transfers between devices, body(): near_key, near_value = [lax.ppermute(a, 'blk', swap) for a in passed]  0.7 us
    ppermute x2, starting transfers between devices, body(): near_key, near_value = [lax.ppermute(a, 'blk', swap) for a in passed]  0.57 us
  transfers between devices with their start and end apart: 13, of which 3 were waited for; matrix products, arithmetic and copies ran while one was open for 0% of the time, Pallas kernels for 4%

profile of v10, /device:TPU:0, one launch (start us, length us, event | category | flops | bytes accessed | tf_op | source)
XLA Modules:
  0.0 25.4 jit_solution(16591697882929098559)
XLA Ops:
  0.6 0.9 %prep.1 = (bf16[16,1280]{1,0:T(8,128)(2,1)S(1)}, bf16[16,1280]{1,0:T(8,128)(2,1)S(1)}, bf16[16,1280]{1,0:T(8,128)(2,1)S(1)}, bf16[16,1280]{1,0:T(8,128)(2,1)S(1)}, bf16[128,256]{1,0:T(8,128)(2,1)S(1)}) custom-call(bf16[16,5120]{1,0:T(8,128)(2,1)} %grad.1, bf16[64,256]{1,0:T(8,128)(2,1)} %key.1, bf16[64,256]{1,0:T(8,128)(2,1)} %value.1), custom_call_target="tpu_custom_call" | custom-call | tf_op jit(solution)/shard_map/prep/pallas_call | solution.py:312
  1.6 3.0 %collective-permute-start = (bf16[128,256]{1,0:T(8,128)(2,1)S(1)}, bf16[128,256]{1,0:T(8,128)(2,1)S(1)}, u32[]{:S(2)}, u32[]{:S(2)}) collective-permute-start(bf16[128,256]{1,0:T(8,128)(2,1)S(1)} %get-tuple-element.37.own.kv), channel_id=1, source_target_pairs={{0,8},{4,12},{8,16},{12,20},{16,24},{20,28},{24,0},{28,4},{1,9},{5... | collective-permute-start | bytes 196616 | tf_op jit(solution)/shard_map/ppermute | solution.py:26
  4.6 2.6 %collective-permute-start.3 = (bf16[16,1280]{1,0:T(8,128)(2,1)S(1)}, bf16[16,1280]{1,0:T(8,128)(2,1)S(1)}, u32[]{:S(2)}, u32[]{:S(2)}) collective-permute-start(bf16[16,1280]{1,0:T(8,128)(2,1)S(1)} %get-tuple-element.47), channel_id=1, source_target_pairs={{0,2},{1,3},{2,0},{3,1},{4,6},{5,7},{6,4},{7,5},{8,10},{9,11},{10,... | collective-permute-start | bytes 122888 | tf_op jit(solution)/shard_map/ppermute | solution.py:45
  7.2 1.3 %collective-permute-start.4 = (bf16[16,1280]{1,0:T(8,128)(2,1)S(1)}, bf16[16,1280]{1,0:T(8,128)(2,1)S(1)}, u32[]{:S(2)}, u32[]{:S(2)}) collective-permute-start(bf16[16,1280]{1,0:T(8,128)(2,1)S(1)} %get-tuple-element.56), channel_id=1, source_target_pairs={{0,3},{1,2},{2,1},{3,0},{4,7},{5,6},{6,5},{7,4},{8,11},{9,10},{10,... | collective-permute-start | bytes 122888 | tf_op jit(solution)/shard_map/ppermute | solution.py:45
  8.5 0.2 collective-permute-start.5
  8.8 0.1 collective-permute-start.1
  8.8 0.5 %collective-permute-start.2 = (bf16[64,256]{1,0:T(8,128)(2,1)S(1)}, bf16[64,256]{1,0:T(8,128)(2,1)S(1)}, u32[]{:S(2)}, u32[]{:S(2)}) collective-permute-start(bf16[64,256]{1,0:T(8,128)(2,1)S(1)} %get-tuple-element.45), channel_id=1, source_target_pairs={{0,4},{4,0},{8,12},{12,8},{16,20},{20,16},{24,28},{28,24},{1,5},{5... | collective-permute-start | bytes 98312 | tf_op jit(solution)/shard_map/ppermute | solution.py:333
  9.3 0.7 %collective-permute-done.1.near_key = bf16[64,256]{1,0:T(8,128)(2,1)S(1)} collective-permute-done((bf16[64,256]{1,0:T(8,128)(2,1)S(1)}, bf16[64,256]{1,0:T(8,128)(2,1)S(1)}, u32[]{:S(2)}, u32[]{:S(2)}) %collective-permute-start.1) | collective-permute-done | bytes 32800 | tf_op jit(solution)/shard_map/ppermute | solution.py:333
  10.0 0.4 %early.1 = (bf16[2,192,128]{2,1,0:T(8,128)(2,1)S(1)}, bf16[2,192,128]{2,1,0:T(8,128)(2,1)S(1)}, f32[2,192,160]{2,1,0:T(8,128)S(1)}, bf16[2,192,160]{2,1,0:T(8,12...) custom-call(bf16[64,1280]{1,0:T(8,128)(2,1)S(1)} %copy-done, ...), custom_call_target="tpu_custom_call" | custom-call | tf_op jit(solution)/shard_map/early/pallas_call | solution.py:335
  10.4 0.0 collective-permute-done.2.near_value
  10.4 0.5 %first.1 = (bf16[2,192,128]{2,1,0:T(8,128)(2,1)S(1)}, bf16[32,1280]{1,0:T(8,128)(2,1)S(1)}, f32[2,192,128]{2,1,0:T(8,128)S(1)}, f32[2,192,128]{2,1,0:T(8,128)S(1)}, bf16[16,1280]{1,0:T(8,128)(2,1)S(1)}) custom-call(f32[2,192,160]{2,1,0:T(8,128)S(1)} %get-tuple-element.40.prob, bf16[2,192,160]{2,1,0:T(8,128)(2,1)S(1)} %get-tuple-element.41.low, ...), custom_call_target="tpu_custom_call" | custom-call | tf_op jit(solution)/shard_map/first/pallas_call | solution.py:356
  10.9 2.0 %collective-permute-done.4.refs_0_ = bf16[16,1280]{1,0:T(8,128)(2,1)S(1)} collective-permute-done((bf16[16,1280]{1,0:T(8,128)(2,1)S(1)}, bf16[16,1280]{1,0:T(8,128)(2,1)S(1)}, u32[]{:S(2)}, u32[]{:S(2)}) %collective-permute-start.4) | collective-permute-done | bytes 40992 | tf_op jit(solution)/shard_map/ppermute | solution.py:45
  13.0 0.4 %main.1 = (bf16[128,256]{1,0:T(8,128)(2,1)S(1)}, bf16[128,256]{1,0:T(8,128)(2,1)S(1)}, f32[128,256]{1,0:T(8,128)S(1)}, bf16[2,192,160]{2,1,0:T(8,128)(2,1)S(1)}) custom-call(f32[2,192,160]{2,1,0:T(8,128)S(1)} %get-tuple-element.49.prob, bf16[2,192,160]{2,1,0:T(8,128)(2,1)S(1)} %get-tuple-element.50.low, bf16[2,160,128]{2,1,0:T(8,128)(2,1)S(1)} %get-tuple-element.51.queries, ...), custom_call_target="tpu_custom_call" | custom-call | tf_op jit(solution)/shard_map/main/pallas_call | solution.py:365
  13.4 1.5 %collective-permute-start.6 = (bf16[128,256]{1,0:T(8,128)(2,1)S(1)}, bf16[128,256]{1,0:T(8,128)(2,1)S(1)}, u32[]{:S(2)}, u32[]{:S(2)}) collective-permute-start(bf16[128,256]{1,0:T(8,128)(2,1)S(1)} %get-tuple-element.61), channel_id=1, source_target_pairs={{0,24},{4,28},{8,0},{12,4},{16,8},{20,12},{24,16},{28,20},{1,25},{... | collective-permute-start | bytes 196616 | tf_op jit(solution)/shard_map/ppermute | solution.py:26
  14.8 0.0 collective-permute-start.7
  14.8 0.2 query.3
  15.1 0.9 %collective-permute-start.12 = (bf16[16,1280]{1,0:T(8,128)(2,1)S(1)}, bf16[16,1280]{1,0:T(8,128)(2,1)S(1)}, u32[]{:S(2)}, u32[]{:S(2)}) collective-permute-start(bf16[16,1280]{1,0:T(8,128)(2,1)S(1)} %get-tuple-element.68), channel_id=1, source_target_pairs={{0,1},{1,0},{2,3},{3,2},{4,5},{5,4},{6,7},{7,6},{8,9},{9,8},{10,11... | collective-permute-start | bytes 122888 | tf_op jit(solution)/shard_map/ppermute | solution.py:45
  16.0 1.9 %collective-permute-start.11 = (bf16[16,1280]{1,0:T(8,128)(2,1)S(1)}, bf16[16,1280]{1,0:T(8,128)(2,1)S(1)}, u32[]{:S(2)}, u32[]{:S(2)}) collective-permute-start(bf16[16,1280]{1,0:T(8,128)(2,1)S(1)} %get-tuple-element.67), channel_id=1, source_target_pairs={{0,2},{1,3},{2,0},{3,1},{4,6},{5,7},{6,4},{7,5},{8,10},{9,11},{10,... | collective-permute-start | bytes 122888 | tf_op jit(solution)/shard_map/ppermute | solution.py:45
  17.8 0.0 collective-permute-done.6.refs_0_
  17.9 1.9 %collective-permute-start.8 = (bf16[16,1792]{1,0:T(8,128)(2,1)S(1)}, bf16[16,1792]{1,0:T(8,128)(2,1)S(1)}, u32[]{:S(2)}, u32[]{:S(2)}) collective-permute-start(bf16[16,1792]{1,0:T(8,128)(2,1)S(1)} %get-tuple-element.63), channel_id=1, source_target_pairs={{0,3},{1,2},{2,1},{3,0},{4,7},{5,6},{6,5},{7,4},{8,11},{9,10},{10,... | collective-permute-start | bytes 172040 | tf_op jit(solution)/shard_map/ppermute | solution.py:45
  19.8 0.0 collective-permute-start.9
  19.8 2.5 %collective-permute-start.10 = (bf16[16,512]{1,0:T(8,128)(2,1)S(1)}, bf16[16,512]{1,0:T(8,128)(2,1)S(1)}, u32[]{:S(2)}, u32[]{:S(2)}) collective-permute-start(bf16[16,512]{1,0:T(8,128)(2,1)S(1)} %get-tuple-element.65), channel_id=1, source_target_pairs={{0,2},{1,3},{2,0},{3,1},{4,6},{5,7},{6,4},{7,5},{8,10},{9,11},{10,... | collective-permute-start | bytes 49160 | tf_op jit(solution)/shard_map/ppermute | solution.py:45
  22.4 2.2 %collective-permute-done.9.refs_1_ = bf16[16,512]{1,0:T(8,128)(2,1)S(1)} collective-permute-done((bf16[16,512]{1,0:T(8,128)(2,1)S(1)}, bf16[16,512]{1,0:T(8,128)(2,1)S(1)}, u32[]{:S(2)}, u32[]{:S(2)}) %collective-permute-start.9) | collective-permute-done | bytes 16416 | tf_op jit(solution)/shard_map/ppermute | solution.py:45
  24.6 0.8 %place.1 = (bf16[16,5120]{1,0:T(8,128)(2,1)}, bf16[16,1024]{1,0:T(8,128)(2,1)}, bf16[16,1024]{1,0:T(8,128)(2,1)}) custom-call(bf16[16,1792]{1,0:T(8,128)(2,1)S(1)} %collective-permute-done.8.refs_0_, bf16[16,512]{1,0:T(8,128)(2,1)S(1)} %collective-permute-done.9.refs_1_, bf16[16,512]{1,0:T(8,128)(2,1)S(1)} %collective-permute-done.10.refs_2_, ...), custom_call_target="tpu_custom_call" | custom-call | tf_op jit(solution)/shard_map/place/pallas_call | solution.py:412
  (17 shorter events, 0.1 us)
Async XLA Ops:
  1.6 7.2 %collective-permute-start = (bf16[128,256]{1,0:T(8,128)(2,1)S(1)}, bf16[128,256]{1,0:T(8,128)(2,1)S(1)}, u32[]{:S(2)}, u32[]{:S(2)}) collective-permute-start(bf16[128,256]{1,0:T(8,128)(2,1)S(1)} %get-tuple-element.37.own.kv), channel_id=1, source_target_pairs={{0,8},{4,12},{8,16},{12,20},{16,24},{20,28},{24,0},{28,4},{1,9},{5... | collective-permute-start | bytes 196616 | tf_op jit(solution)/shard_map/ppermute | solution.py:26
  4.6 5.9 %collective-permute-start.3 = (bf16[16,1280]{1,0:T(8,128)(2,1)S(1)}, bf16[16,1280]{1,0:T(8,128)(2,1)S(1)}, u32[]{:S(2)}, u32[]{:S(2)}) collective-permute-start(bf16[16,1280]{1,0:T(8,128)(2,1)S(1)} %get-tuple-element.47), channel_id=1, source_target_pairs={{0,2},{1,3},{2,0},{3,1},{4,6},{5,7},{6,4},{7,5},{8,10},{9,11},{10,... | collective-permute-start | bytes 122888 | tf_op jit(solution)/shard_map/ppermute | solution.py:45
  7.2 5.8 %collective-permute-start.4 = (bf16[16,1280]{1,0:T(8,128)(2,1)S(1)}, bf16[16,1280]{1,0:T(8,128)(2,1)S(1)}, u32[]{:S(2)}, u32[]{:S(2)}) collective-permute-start(bf16[16,1280]{1,0:T(8,128)(2,1)S(1)} %get-tuple-element.56), channel_id=1, source_target_pairs={{0,3},{1,2},{2,1},{3,0},{4,7},{5,6},{6,5},{7,4},{8,11},{9,10},{10,... | collective-permute-start | bytes 122888 | tf_op jit(solution)/shard_map/ppermute | solution.py:45
  8.5 1.5 %copy-start = (bf16[64,1280]{1,0:T(8,128)(2,1)S(1)}, bf16[64,1280]{1,0:T(8,128)(2,1)}, u32[]{:S(2)}) copy-start(bf16[64,1280]{1,0:T(8,128)(2,1)} %query.2) | copy-start | bytes 491524
  8.5 1.5 %copy-start.1 = (bf16[64,1280]{1,0:T(8,128)(2,1)S(1)}, bf16[64,1280]{1,0:T(8,128)(2,1)}, u32[]{:S(2)}) copy-start(bf16[64,1280]{1,0:T(8,128)(2,1)} %output.1) | copy-start | bytes 491524
  8.5 4.5 %collective-permute-start.5 = (bf16[16,1280]{1,0:T(8,128)(2,1)S(1)}, bf16[16,1280]{1,0:T(8,128)(2,1)S(1)}, u32[]{:S(2)}, u32[]{:S(2)}) collective-permute-start(bf16[16,1280]{1,0:T(8,128)(2,1)S(1)} %get-tuple-element.57), channel_id=1, source_target_pairs={{0,1},{1,0},{2,3},{3,2},{4,5},{5,4},{6,7},{7,6},{8,9},{9,8},{10,11... | collective-permute-start | bytes 122888 | tf_op jit(solution)/shard_map/ppermute | solution.py:45
  8.7 1.3 %copy-start.2 = (f32[10,64]{1,0:T(8,128)S(1)}, f32[10,64]{1,0:T(8,128)}, u32[]{:S(2)}) copy-start(f32[10,64]{1,0:T(8,128)} %lse.1) | copy-start | bytes 7684
  8.8 1.3 %collective-permute-start.1 = (bf16[64,256]{1,0:T(8,128)(2,1)S(1)}, bf16[64,256]{1,0:T(8,128)(2,1)S(1)}, u32[]{:S(2)}, u32[]{:S(2)}) collective-permute-start(bf16[64,256]{1,0:T(8,128)(2,1)S(1)} %get-tuple-element.38), channel_id=1, source_target_pairs={{0,4},{4,0},{8,12},{12,8},{16,20},{20,16},{24,28},{28,24},{1,5},{5... | collective-permute-start | bytes 98312 | tf_op jit(solution)/shard_map/ppermute | solution.py:333
  8.8 1.6 %collective-permute-start.2 = (bf16[64,256]{1,0:T(8,128)(2,1)S(1)}, bf16[64,256]{1,0:T(8,128)(2,1)S(1)}, u32[]{:S(2)}, u32[]{:S(2)}) collective-permute-start(bf16[64,256]{1,0:T(8,128)(2,1)S(1)} %get-tuple-element.45), channel_id=1, source_target_pairs={{0,4},{4,0},{8,12},{12,8},{16,20},{20,16},{24,28},{28,24},{1,5},{5... | collective-permute-start | bytes 98312 | tf_op jit(solution)/shard_map/ppermute | solution.py:333
  13.4 4.5 %collective-permute-start.6 = (bf16[128,256]{1,0:T(8,128)(2,1)S(1)}, bf16[128,256]{1,0:T(8,128)(2,1)S(1)}, u32[]{:S(2)}, u32[]{:S(2)}) collective-permute-start(bf16[128,256]{1,0:T(8,128)(2,1)S(1)} %get-tuple-element.61), channel_id=1, source_target_pairs={{0,24},{4,28},{8,0},{12,4},{16,8},{20,12},{24,16},{28,20},{1,25},{... | collective-permute-start | bytes 196616 | tf_op jit(solution)/shard_map/ppermute | solution.py:26
  14.8 3.0 %collective-permute-start.7 = (bf16[128,256]{1,0:T(8,128)(2,1)S(1)}, bf16[128,256]{1,0:T(8,128)(2,1)S(1)}, u32[]{:S(2)}, u32[]{:S(2)}) collective-permute-start(bf16[128,256]{1,0:T(8,128)(2,1)S(1)} %get-tuple-element.62), channel_id=1, source_target_pairs={{0,28},{4,0},{8,4},{12,8},{16,12},{20,16},{24,20},{28,24},{1,29},{... | collective-permute-start | bytes 196616 | tf_op jit(solution)/shard_map/ppermute | solution.py:26
  15.1 7.3 %collective-permute-start.12 = (bf16[16,1280]{1,0:T(8,128)(2,1)S(1)}, bf16[16,1280]{1,0:T(8,128)(2,1)S(1)}, u32[]{:S(2)}, u32[]{:S(2)}) collective-permute-start(bf16[16,1280]{1,0:T(8,128)(2,1)S(1)} %get-tuple-element.68), channel_id=1, source_target_pairs={{0,1},{1,0},{2,3},{3,2},{4,5},{5,4},{6,7},{7,6},{8,9},{9,8},{10,11... | collective-permute-start | bytes 122888 | tf_op jit(solution)/shard_map/ppermute | solution.py:45
  16.0 6.4 %collective-permute-start.11 = (bf16[16,1280]{1,0:T(8,128)(2,1)S(1)}, bf16[16,1280]{1,0:T(8,128)(2,1)S(1)}, u32[]{:S(2)}, u32[]{:S(2)}) collective-permute-start(bf16[16,1280]{1,0:T(8,128)(2,1)S(1)} %get-tuple-element.67), channel_id=1, source_target_pairs={{0,2},{1,3},{2,0},{3,1},{4,6},{5,7},{6,4},{7,5},{8,10},{9,11},{10,... | collective-permute-start | bytes 122888 | tf_op jit(solution)/shard_map/ppermute | solution.py:45
  17.9 6.7 %collective-permute-start.8 = (bf16[16,1792]{1,0:T(8,128)(2,1)S(1)}, bf16[16,1792]{1,0:T(8,128)(2,1)S(1)}, u32[]{:S(2)}, u32[]{:S(2)}) collective-permute-start(bf16[16,1792]{1,0:T(8,128)(2,1)S(1)} %get-tuple-element.63), channel_id=1, source_target_pairs={{0,3},{1,2},{2,1},{3,0},{4,7},{5,6},{6,5},{7,4},{8,11},{9,10},{10,... | collective-permute-start | bytes 172040 | tf_op jit(solution)/shard_map/ppermute | solution.py:45
  19.8 4.8 %collective-permute-start.9 = (bf16[16,512]{1,0:T(8,128)(2,1)S(1)}, bf16[16,512]{1,0:T(8,128)(2,1)S(1)}, u32[]{:S(2)}, u32[]{:S(2)}) collective-permute-start(bf16[16,512]{1,0:T(8,128)(2,1)S(1)} %get-tuple-element.64), channel_id=1, source_target_pairs={{0,1},{1,0},{2,3},{3,2},{4,5},{5,4},{6,7},{7,6},{8,9},{9,8},{10,11... | collective-permute-start | bytes 49160 | tf_op jit(solution)/shard_map/ppermute | solution.py:45
  19.8 4.8 %collective-permute-start.10 = (bf16[16,512]{1,0:T(8,128)(2,1)S(1)}, bf16[16,512]{1,0:T(8,128)(2,1)S(1)}, u32[]{:S(2)}, u32[]{:S(2)}) collective-permute-start(bf16[16,512]{1,0:T(8,128)(2,1)S(1)} %get-tuple-element.65), channel_id=1, source_target_pairs={{0,2},{1,3},{2,0},{3,1},{4,6},{5,7},{6,4},{7,5},{8,10},{9,11},{10,... | collective-permute-start | bytes 49160 | tf_op jit(solution)/shard_map/ppermute | solution.py:45

commit v11 on v9

--- a/solution.py
+++ b/solution.py
@@ -13,7 +13,7 @@
 STEPS = 3
 GROUP = QHEADS // KVHEADS
 SCALE = HEAD_DIM ** (-0.5)
-AHEAD = (2, 1)
+AHEAD = (1, 2)
 
 VMEM = pl.BlockSpec(memory_space=pltpu.VMEM)
 ANY = pl.BlockSpec(memory_space=pl.ANY)

time: 25.6 us -> 25.6 us (level)
  no operation moved by 1% of the time
where the time goes in v11:
time: 25.6 us; the launch traced here: 25.4 us
  starting transfers between devices  16.4 us (64%)
  waiting for transfers between devices  4.96 us (19%)
  Pallas kernels  3.26 us (13%)
  between operations  0.71 us (3%)
    ppermute x8, starting transfers between devices, exchange(): return lax.ppermute(array, axis, pairs)  11.4 us
    ppermute x3, starting transfers between devices, shifted(): lax.ppermute(array, axis, [(i, (i + by) % size) for i in range(size)])  4.48 us
    ppermute x8, waiting for transfers between devices, exchange(): return lax.ppermute(array, axis, pairs)  4.25 us
    pallas_call x1, Pallas kernels, body(): pl.pallas_call(functools.partial(prep_kernel, n), out_shape=[shape((rows,...  0.93 us
    pallas_call x1, Pallas kernels, body(): pl.pallas_call(functools.partial(place_kernel, n), out_shape=[shape((rows...  0.79 us
    ppermute x2, waiting for transfers between devices, body(): near_key, near_value = [lax.ppermute(a, 'blk', swap) for a in passed]  0.7 us
    ppermute x2, starting transfers between devices, body(): near_key, near_value = [lax.ppermute(a, 'blk', swap) for a in passed]  0.57 us
  transfers between devices with their start and end apart: 13, of which 3 were waited for; matrix products, arithmetic and copies ran while one was open for 0% of the time, Pallas kernels for 4%

profile of v11, /device:TPU:0, one launch (start us, length us, event | category | flops | bytes accessed | tf_op | source)
XLA Modules:
  0.0 25.4 jit_solution(2115898294179061500)
XLA Ops:
  0.6 0.9 %prep.1 = (bf16[16,1280]{1,0:T(8,128)(2,1)S(1)}, bf16[16,1280]{1,0:T(8,128)(2,1)S(1)}, bf16[16,1280]{1,0:T(8,128)(2,1)S(1)}, bf16[16,1280]{1,0:T(8,128)(2,1)S(1)}, bf16[128,256]{1,0:T(8,128)(2,1)S(1)}) custom-call(bf16[16,5120]{1,0:T(8,128)(2,1)} %grad.1, bf16[64,256]{1,0:T(8,128)(2,1)} %key.1, bf16[64,256]{1,0:T(8,128)(2,1)} %value.1), custom_call_target="tpu_custom_call" | custom-call | tf_op jit(solution)/shard_map/prep/pallas_call | solution.py:316
  1.6 3.0 %collective-permute-start = (bf16[128,256]{1,0:T(8,128)(2,1)S(1)}, bf16[128,256]{1,0:T(8,128)(2,1)S(1)}, u32[]{:S(2)}, u32[]{:S(2)}) collective-permute-start(bf16[128,256]{1,0:T(8,128)(2,1)S(1)} %get-tuple-element.36.own.kv), channel_id=1, source_target_pairs={{0,8},{4,12},{8,16},{12,20},{16,24},{20,28},{24,0},{28,4},{1,9},{5... | collective-permute-start | bytes 196616 | tf_op jit(solution)/shard_map/ppermute | solution.py:26
  4.6 2.6 %collective-permute-start.3 = (bf16[16,1280]{1,0:T(8,128)(2,1)S(1)}, bf16[16,1280]{1,0:T(8,128)(2,1)S(1)}, u32[]{:S(2)}, u32[]{:S(2)}) collective-permute-start(bf16[16,1280]{1,0:T(8,128)(2,1)S(1)} %get-tuple-element.46), channel_id=1, source_target_pairs={{0,2},{1,3},{2,0},{3,1},{4,6},{5,7},{6,4},{7,5},{8,10},{9,11},{10,... | collective-permute-start | bytes 122888 | tf_op jit(solution)/shard_map/ppermute | solution.py:45
  7.2 1.3 %collective-permute-start.4 = (bf16[16,1280]{1,0:T(8,128)(2,1)S(1)}, bf16[16,1280]{1,0:T(8,128)(2,1)S(1)}, u32[]{:S(2)}, u32[]{:S(2)}) collective-permute-start(bf16[16,1280]{1,0:T(8,128)(2,1)S(1)} %get-tuple-element.54), channel_id=1, source_target_pairs={{0,3},{1,2},{2,1},{3,0},{4,7},{5,6},{6,5},{7,4},{8,11},{9,10},{10,... | collective-permute-start | bytes 122888 | tf_op jit(solution)/shard_map/ppermute | solution.py:45
  8.5 0.2 collective-permute-start.5
  8.7 0.0 collective-permute-done.pair.refs_0_
  8.8 0.1 collective-permute-start.1
  8.8 0.5 %collective-permute-start.2 = (bf16[64,256]{1,0:T(8,128)(2,1)S(1)}, bf16[64,256]{1,0:T(8,128)(2,1)S(1)}, u32[]{:S(2)}, u32[]{:S(2)}) collective-permute-start(bf16[64,256]{1,0:T(8,128)(2,1)S(1)} %get-tuple-element.44), channel_id=1, source_target_pairs={{0,4},{4,0},{8,12},{12,8},{16,20},{20,16},{24,28},{28,24},{1,5},{5... | collective-permute-start | bytes 98312 | tf_op jit(solution)/shard_map/ppermute | solution.py:337
  9.3 0.7 %collective-permute-done.1.near_key = bf16[64,256]{1,0:T(8,128)(2,1)S(1)} collective-permute-done((bf16[64,256]{1,0:T(8,128)(2,1)S(1)}, bf16[64,256]{1,0:T(8,128)(2,1)S(1)}, u32[]{:S(2)}, u32[]{:S(2)}) %collective-permute-start.1) | collective-permute-done | bytes 32800 | tf_op jit(solution)/shard_map/ppermute | solution.py:337
  10.0 0.4 %early.1 = (bf16[2,192,128]{2,1,0:T(8,128)(2,1)S(1)}, bf16[2,192,128]{2,1,0:T(8,128)(2,1)S(1)}, f32[2,192,160]{2,1,0:T(8,128)S(1)}, bf16[2,192,160]{2,1,0:T(8,12...) custom-call(bf16[64,1280]{1,0:T(8,128)(2,1)S(1)} %copy-done, ...), custom_call_target="tpu_custom_call" | custom-call | tf_op jit(solution)/shard_map/early/pallas_call | solution.py:339
  10.4 0.0 collective-permute-done.3.refs_1_
  10.4 0.0 collective-permute-done.2.near_value
  10.4 0.5 %first.1 = (bf16[32,1280]{1,0:T(8,128)(2,1)S(1)}, f32[2,192,128]{2,1,0:T(8,128)S(1)}, f32[2,192,128]{2,1,0:T(8,128)S(1)}, bf16[16,1280]{1,0:T(8,128)(2,1)S(1)}) custom-call(f32[2,192,160]{2,1,0:T(8,128)S(1)} %get-tuple-element.39.prob, bf16[2,192,160]{2,1,0:T(8,128)(2,1)S(1)} %get-tuple-element.40.low, bf16[2,160,128]{2,1,0:T(8,128)(2,1)S(1)} %get-tuple-element.41.queries, ...), custom_call_target="tpu_custom_call" | custom-call | tf_op jit(solution)/shard_map/first/pallas_call | solution.py:360
  10.9 2.0 %collective-permute-done.4.refs_0_ = bf16[16,1280]{1,0:T(8,128)(2,1)S(1)} collective-permute-done((bf16[16,1280]{1,0:T(8,128)(2,1)S(1)}, bf16[16,1280]{1,0:T(8,128)(2,1)S(1)}, u32[]{:S(2)}, u32[]{:S(2)}) %collective-permute-start.4) | collective-permute-done | bytes 40992 | tf_op jit(solution)/shard_map/ppermute | solution.py:45
  13.0 0.4 %main.1 = (bf16[128,256]{1,0:T(8,128)(2,1)S(1)}, bf16[128,256]{1,0:T(8,128)(2,1)S(1)}, f32[128,256]{1,0:T(8,128)S(1)}, bf16[2,192,160]{2,1,0:T(8,128)(2,1)S(1)}) custom-call(f32[2,192,160]{2,1,0:T(8,128)S(1)} %get-tuple-element.48.prob, bf16[2,192,160]{2,1,0:T(8,128)(2,1)S(1)} %get-tuple-element.49.low, bf16[2,160,128]{2,1,0:T(8,128)(2,1)S(1)} %get-tuple-element.50.queries, ...), custom_call_target="tpu_custom_call" | custom-call | tf_op jit(solution)/shard_map/main/pallas_call | solution.py:369
  13.4 1.5 %collective-permute-start.6 = (bf16[128,256]{1,0:T(8,128)(2,1)S(1)}, bf16[128,256]{1,0:T(8,128)(2,1)S(1)}, u32[]{:S(2)}, u32[]{:S(2)}) collective-permute-start(bf16[128,256]{1,0:T(8,128)(2,1)S(1)} %get-tuple-element.59), channel_id=1, source_target_pairs={{0,24},{4,28},{8,0},{12,4},{16,8},{20,12},{24,16},{28,20},{1,25},{... | collective-permute-start | bytes 196616 | tf_op jit(solution)/shard_map/ppermute | solution.py:26
  14.8 0.0 collective-permute-start.7
  14.8 0.2 query.3
  15.1 0.9 %collective-permute-start.11 = (bf16[16,1280]{1,0:T(8,128)(2,1)S(1)}, bf16[16,1280]{1,0:T(8,128)(2,1)S(1)}, u32[]{:S(2)}, u32[]{:S(2)}) collective-permute-start(bf16[16,1280]{1,0:T(8,128)(2,1)S(1)} %get-tuple-element.65), channel_id=1, source_target_pairs={{0,1},{1,0},{2,3},{3,2},{4,5},{5,4},{6,7},{7,6},{8,9},{9,8},{10,11... | collective-permute-start | bytes 122888 | tf_op jit(solution)/shard_map/ppermute | solution.py:45
  16.0 1.9 %collective-permute-start.12 = (bf16[16,1280]{1,0:T(8,128)(2,1)S(1)}, bf16[16,1280]{1,0:T(8,128)(2,1)S(1)}, u32[]{:S(2)}, u32[]{:S(2)}) collective-permute-start(bf16[16,1280]{1,0:T(8,128)(2,1)S(1)} %get-tuple-element.66), channel_id=1, source_target_pairs={{0,2},{1,3},{2,0},{3,1},{4,6},{5,7},{6,4},{7,5},{8,10},{9,11},{10,... | collective-permute-start | bytes 122888 | tf_op jit(solution)/shard_map/ppermute | solution.py:45
  17.9 1.9 %collective-permute-start.8 = (bf16[16,1792]{1,0:T(8,128)(2,1)S(1)}, bf16[16,1792]{1,0:T(8,128)(2,1)S(1)}, u32[]{:S(2)}, u32[]{:S(2)}) collective-permute-start(bf16[16,1792]{1,0:T(8,128)(2,1)S(1)} %get-tuple-element.61), channel_id=1, source_target_pairs={{0,3},{1,2},{2,1},{3,0},{4,7},{5,6},{6,5},{7,4},{8,11},{9,10},{10,... | collective-permute-start | bytes 172040 | tf_op jit(solution)/shard_map/ppermute | solution.py:45
  19.8 2.5 %collective-permute-start.10 = (bf16[16,512]{1,0:T(8,128)(2,1)S(1)}, bf16[16,512]{1,0:T(8,128)(2,1)S(1)}, u32[]{:S(2)}, u32[]{:S(2)}) collective-permute-start(bf16[16,512]{1,0:T(8,128)(2,1)S(1)} %get-tuple-element.63), channel_id=1, source_target_pairs={{0,2},{1,3},{2,0},{3,1},{4,6},{5,7},{6,4},{7,5},{8,10},{9,11},{10,... | collective-permute-start | bytes 49160 | tf_op jit(solution)/shard_map/ppermute | solution.py:45
  22.4 2.2 %collective-permute-done.9.refs_1_ = bf16[16,512]{1,0:T(8,128)(2,1)S(1)} collective-permute-done((bf16[16,512]{1,0:T(8,128)(2,1)S(1)}, bf16[16,512]{1,0:T(8,128)(2,1)S(1)}, u32[]{:S(2)}, u32[]{:S(2)}) %collective-permute-start.9) | collective-permute-done | bytes 16416 | tf_op jit(solution)/shard_map/ppermute | solution.py:45
  24.6 0.8 %place.1 = (bf16[16,5120]{1,0:T(8,128)(2,1)}, bf16[16,1024]{1,0:T(8,128)(2,1)}, bf16[16,1024]{1,0:T(8,128)(2,1)}) custom-call(bf16[16,1792]{1,0:T(8,128)(2,1)S(1)} %collective-permute-done.8.refs_0_, bf16[16,512]{1,0:T(8,128)(2,1)S(1)} %collective-permute-done.9.refs_1_, bf16[16,512]{1,0:T(8,128)(2,1)S(1)} %collective-permute-done.10.refs_2_, ...), custom_call_target="tpu_custom_call" | custom-call | tf_op jit(solution)/shard_map/place/pallas_call | solution.py:416
  (17 shorter events, 0.1 us)
Async XLA Ops:
  1.6 7.2 %collective-permute-start = (bf16[128,256]{1,0:T(8,128)(2,1)S(1)}, bf16[128,256]{1,0:T(8,128)(2,1)S(1)}, u32[]{:S(2)}, u32[]{:S(2)}) collective-permute-start(bf16[128,256]{1,0:T(8,128)(2,1)S(1)} %get-tuple-element.36.own.kv), channel_id=1, source_target_pairs={{0,8},{4,12},{8,16},{12,20},{16,24},{20,28},{24,0},{28,4},{1,9},{5... | collective-permute-start | bytes 196616 | tf_op jit(solution)/shard_map/ppermute | solution.py:26
  4.6 5.9 %collective-permute-start.3 = (bf16[16,1280]{1,0:T(8,128)(2,1)S(1)}, bf16[16,1280]{1,0:T(8,128)(2,1)S(1)}, u32[]{:S(2)}, u32[]{:S(2)}) collective-permute-start(bf16[16,1280]{1,0:T(8,128)(2,1)S(1)} %get-tuple-element.46), channel_id=1, source_target_pairs={{0,2},{1,3},{2,0},{3,1},{4,6},{5,7},{6,4},{7,5},{8,10},{9,11},{10,... | collective-permute-start | bytes 122888 | tf_op jit(solution)/shard_map/ppermute | solution.py:45
  7.2 5.8 %collective-permute-start.4 = (bf16[16,1280]{1,0:T(8,128)(2,1)S(1)}, bf16[16,1280]{1,0:T(8,128)(2,1)S(1)}, u32[]{:S(2)}, u32[]{:S(2)}) collective-permute-start(bf16[16,1280]{1,0:T(8,128)(2,1)S(1)} %get-tuple-element.54), channel_id=1, source_target_pairs={{0,3},{1,2},{2,1},{3,0},{4,7},{5,6},{6,5},{7,4},{8,11},{9,10},{10,... | collective-permute-start | bytes 122888 | tf_op jit(solution)/shard_map/ppermute | solution.py:45
  8.5 1.5 %copy-start = (bf16[64,1280]{1,0:T(8,128)(2,1)S(1)}, bf16[64,1280]{1,0:T(8,128)(2,1)}, u32[]{:S(2)}) copy-start(bf16[64,1280]{1,0:T(8,128)(2,1)} %query.2) | copy-start | bytes 491524
  8.5 1.5 %copy-start.1 = (bf16[64,1280]{1,0:T(8,128)(2,1)S(1)}, bf16[64,1280]{1,0:T(8,128)(2,1)}, u32[]{:S(2)}) copy-start(bf16[64,1280]{1,0:T(8,128)(2,1)} %output.1) | copy-start | bytes 491524
  8.5 4.5 %collective-permute-start.5 = (bf16[16,1280]{1,0:T(8,128)(2,1)S(1)}, bf16[16,1280]{1,0:T(8,128)(2,1)S(1)}, u32[]{:S(2)}, u32[]{:S(2)}) collective-permute-start(bf16[16,1280]{1,0:T(8,128)(2,1)S(1)} %get-tuple-element.55), channel_id=1, source_target_pairs={{0,1},{1,0},{2,3},{3,2},{4,5},{5,4},{6,7},{7,6},{8,9},{9,8},{10,11... | collective-permute-start | bytes 122888 | tf_op jit(solution)/shard_map/ppermute | solution.py:45
  8.7 1.3 %copy-start.2 = (f32[10,64]{1,0:T(8,128)S(1)}, f32[10,64]{1,0:T(8,128)}, u32[]{:S(2)}) copy-start(f32[10,64]{1,0:T(8,128)} %lse.1) | copy-start | bytes 7684
  8.8 1.3 %collective-permute-start.1 = (bf16[64,256]{1,0:T(8,128)(2,1)S(1)}, bf16[64,256]{1,0:T(8,128)(2,1)S(1)}, u32[]{:S(2)}, u32[]{:S(2)}) collective-permute-start(bf16[64,256]{1,0:T(8,128)(2,1)S(1)} %get-tuple-element.37), channel_id=1, source_target_pairs={{0,4},{4,0},{8,12},{12,8},{16,20},{20,16},{24,28},{28,24},{1,5},{5... | collective-permute-start | bytes 98312 | tf_op jit(solution)/shard_map/ppermute | solution.py:337
  8.8 1.6 %collective-permute-start.2 = (bf16[64,256]{1,0:T(8,128)(2,1)S(1)}, bf16[64,256]{1,0:T(8,128)(2,1)S(1)}, u32[]{:S(2)}, u32[]{:S(2)}) collective-permute-start(bf16[64,256]{1,0:T(8,128)(2,1)S(1)} %get-tuple-element.44), channel_id=1, source_target_pairs={{0,4},{4,0},{8,12},{12,8},{16,20},{20,16},{24,28},{28,24},{1,5},{5... | collective-permute-start | bytes 98312 | tf_op jit(solution)/shard_map/ppermute | solution.py:337
  13.4 4.5 %collective-permute-start.6 = (bf16[128,256]{1,0:T(8,128)(2,1)S(1)}, bf16[128,256]{1,0:T(8,128)(2,1)S(1)}, u32[]{:S(2)}, u32[]{:S(2)}) collective-permute-start(bf16[128,256]{1,0:T(8,128)(2,1)S(1)} %get-tuple-element.59), channel_id=1, source_target_pairs={{0,24},{4,28},{8,0},{12,4},{16,8},{20,12},{24,16},{28,20},{1,25},{... | collective-permute-start | bytes 196616 | tf_op jit(solution)/shard_map/ppermute | solution.py:26
  14.8 3.0 %collective-permute-start.7 = (bf16[128,256]{1,0:T(8,128)(2,1)S(1)}, bf16[128,256]{1,0:T(8,128)(2,1)S(1)}, u32[]{:S(2)}, u32[]{:S(2)}) collective-permute-start(bf16[128,256]{1,0:T(8,128)(2,1)S(1)} %get-tuple-element.60), channel_id=1, source_target_pairs={{0,28},{4,0},{8,4},{12,8},{16,12},{20,16},{24,20},{28,24},{1,29},{... | collective-permute-start | bytes 196616 | tf_op jit(solution)/shard_map/ppermute | solution.py:26
  15.1 7.3 %collective-permute-start.11 = (bf16[16,1280]{1,0:T(8,128)(2,1)S(1)}, bf16[16,1280]{1,0:T(8,128)(2,1)S(1)}, u32[]{:S(2)}, u32[]{:S(2)}) collective-permute-start(bf16[16,1280]{1,0:T(8,128)(2,1)S(1)} %get-tuple-element.65), channel_id=1, source_target_pairs={{0,1},{1,0},{2,3},{3,2},{4,5},{5,4},{6,7},{7,6},{8,9},{9,8},{10,11... | collective-permute-start | bytes 122888 | tf_op jit(solution)/shard_map/ppermute | solution.py:45
  16.0 6.4 %collective-permute-start.12 = (bf16[16,1280]{1,0:T(8,128)(2,1)S(1)}, bf16[16,1280]{1,0:T(8,128)(2,1)S(1)}, u32[]{:S(2)}, u32[]{:S(2)}) collective-permute-start(bf16[16,1280]{1,0:T(8,128)(2,1)S(1)} %get-tuple-element.66), channel_id=1, source_target_pairs={{0,2},{1,3},{2,0},{3,1},{4,6},{5,7},{6,4},{7,5},{8,10},{9,11},{10,... | collective-permute-start | bytes 122888 | tf_op jit(solution)/shard_map/ppermute | solution.py:45
  17.9 6.7 %collective-permute-start.8 = (bf16[16,1792]{1,0:T(8,128)(2,1)S(1)}, bf16[16,1792]{1,0:T(8,128)(2,1)S(1)}, u32[]{:S(2)}, u32[]{:S(2)}) collective-permute-start(bf16[16,1792]{1,0:T(8,128)(2,1)S(1)} %get-tuple-element.61), channel_id=1, source_target_pairs={{0,3},{1,2},{2,1},{3,0},{4,7},{5,6},{6,5},{7,4},{8,11},{9,10},{10,... | collective-permute-start | bytes 172040 | tf_op jit(solution)/shard_map/ppermute | solution.py:45
  19.8 4.8 %collective-permute-start.9 = (bf16[16,512]{1,0:T(8,128)(2,1)S(1)}, bf16[16,512]{1,0:T(8,128)(2,1)S(1)}, u32[]{:S(2)}, u32[]{:S(2)}) collective-permute-start(bf16[16,512]{1,0:T(8,128)(2,1)S(1)} %get-tuple-element.62), channel_id=1, source_target_pairs={{0,1},{1,0},{2,3},{3,2},{4,5},{5,4},{6,7},{7,6},{8,9},{9,8},{10,11... | collective-permute-start | bytes 49160 | tf_op jit(solution)/shard_map/ppermute | solution.py:45
  19.8 4.8 %collective-permute-start.10 = (bf16[16,512]{1,0:T(8,128)(2,1)S(1)}, bf16[16,512]{1,0:T(8,128)(2,1)S(1)}, u32[]{:S(2)}, u32[]{:S(2)}) collective-permute-start(bf16[16,512]{1,0:T(8,128)(2,1)S(1)} %get-tuple-element.63), channel_id=1, source_target_pairs={{0,2},{1,3},{2,0},{3,1},{4,6},{5,7},{6,4},{7,5},{8,10},{9,11},{10,... | collective-permute-start | bytes 49160 | tf_op jit(solution)/shard_map/ppermute | solution.py:45
